TPU v7x, 32 devices: a whole 2x2x4 slice. The times are simulated.
32 devices in a mesh: rep: 4 (over x, core), shard: 8 (over z, y).
Axes of the slice: x: 2, y: 2, z: 4, core: 2. Of those that a mesh axis runs over, the one named last changes fastest.
Arguments:
- tokens_in: bfloat16 [64, 1024, 768], P(('rep', 'shard')), may hold values from -6 to 6
- cotangent: bfloat16 [64, 1024, 768], P(('rep', 'shard')), may hold values from -6 to 6
- segment_ids: int32 [64, 1024], P(('rep', 'shard')), may hold values from 0 to 1023, as said below
- block_map: int32 [64, 2, 8], P(('rep', 'shard')), may hold values from 0 to 1, as said below
- timesteps: int32 [64], P(('rep', 'shard')), may hold values from 0 to 1023
- step_table: bfloat16 [1024, 768], P('shard'), may hold values from -6 to 6
- ln1_gain: bfloat16 [768], P('shard'), may hold values from 0.5 to 1.5
- ln1_bias: bfloat16 [768], P('shard'), may hold values from -3 to 3
- w_query: bfloat16 [768, 768], P('shard'), may hold values from -0.21875 to 0.21875
- b_query: bfloat16 [768], P('shard'), may hold values from -3 to 3
- w_key: bfloat16 [768, 768], P('shard'), may hold values from -0.21875 to 0.21875
- w_value: bfloat16 [768, 768], P('shard'), may hold values from -0.21875 to 0.21875
- b_value: bfloat16 [768], P('shard'), may hold values from -3 to 3
- w_out: bfloat16 [768, 768], P('shard'), may hold values from -0.875 to 0.875
- b_out: bfloat16 [768], P('shard'), may hold values from -3 to 3
- ln2_gain: bfloat16 [768], P('shard'), may hold values from 0.5 to 1.5
- ln2_bias: bfloat16 [768], P('shard'), may hold values from -3 to 3
- w_up: bfloat16 [768, 3072], P('shard'), may hold values from -0.21875 to 0.21875
- b_up: bfloat16 [3072], P('shard'), may hold values from -3 to 3
- w_down: bfloat16 [3072, 768], P('shard'), may hold values from -0.109375 to 0.109375
- b_down: bfloat16 [768], P('shard'), may hold values from -3 to 3
Outputs:
- output: bfloat16 [64, 1024, 768], P(('rep', 'shard'))
- grad_input: bfloat16 [64, 1024, 768], P(('rep', 'shard'))
- grad_step_table: float32 [1024, 768], P('shard')
- grad_ln1_gain: float32 [768], P('shard')
- grad_ln1_bias: float32 [768], P('shard')
- grad_w_query: float32 [768, 768], P('shard')
- grad_b_query: float32 [768], P('shard')
- grad_w_key: float32 [768, 768], P('shard')
- grad_w_value: float32 [768, 768], P('shard')
- grad_b_value: float32 [768], P('shard')
- grad_w_out: float32 [768, 768], P('shard')
- grad_b_out: float32 [768], P('shard')
- grad_ln2_gain: float32 [768], P('shard')
- grad_ln2_bias: float32 [768], P('shard')
- grad_w_up: float32 [768, 3072], P('shard')
- grad_b_up: float32 [3072], P('shard')
- grad_w_down: float32 [3072, 768], P('shard')
- grad_b_down: float32 [768], P('shard')
Inputs may be any that keep to these rules, and one draw needn't show every extreme that they name: `segment_ids`: in each sequence the ids start at 0 and never fall; a document is a run of positions with one id. block_map[s, i, j] is 1 exactly where query block i (rows i * 512 onward) and key block j (rows j * 128 onward) of sequence s hold tokens of a common document.
All inputs are finite; a program needn't handle non-finite values.
Results may differ from a plain program's by a relative error of at most 0.013.
Values may be sent and summed in bfloat16 or wider, within the bound.
No kernel may reach another device: no remote copies, remote signals or barrier semaphores. Data moves between devices by JAX's collectives and lax.ppermute only.
A program may use at most 320 MiB of HBM per device.

v0:
```python
import jax
import jax.numpy as jnp
from jax import lax
from jax.sharding import PartitionSpec as P

HEADS = 12
QBLK = 512
KBLK = 128


epsilon = 1e-05


def gelu_exact(values):
    return jax.nn.gelu(values, approximate=False)


def normalize(values):
    center = values - jnp.mean(values, axis=-1, keepdims=True)
    inv_dev = lax.rsqrt(jnp.mean(center * center, axis=-1, keepdims=True) + epsilon)
    return (center * inv_dev, inv_dev)


def norm_back(grad_hidden, normed, inv_dev, gain_row):
    grad_normed = grad_hidden * gain_row
    grad_values = inv_dev * (
        grad_normed
        - jnp.mean(grad_normed, axis=-1, keepdims=True)
        - normed * jnp.mean(grad_normed * normed, axis=-1, keepdims=True)
    )
    return (grad_values, jnp.sum(grad_hidden * normed, axis=0), jnp.sum(grad_hidden, axis=0))


def score_block(query_block, key_rows, key_mask, log_total, score_scale):
    raw_scores = (
        jnp.einsum("qhd,khd->hqk", query_block, key_rows, preferred_element_type=jnp.float32)
        * score_scale
    )
    masked = jnp.where(key_mask[None], raw_scores, -1e30)
    if log_total is None:
        row_top = jnp.max(masked, axis=-1, keepdims=True)
        row_total = jnp.sum(
            jnp.where(key_mask[None], jnp.exp(masked - row_top), 0.0), axis=-1, keepdims=True
        )
        log_total = row_top + jnp.log(row_total)
    attn_prob = jnp.where(key_mask[None], jnp.exp(masked - log_total), 0.0)
    return (attn_prob, log_total)


def sequence_pass(params, table_row, tokens_row, cot_row, seg_row, map_row):
    (
        ln1_gain,
        ln1_bias,
        w_query,
        b_query,
        w_key,
        w_value,
        b_value,
        w_out,
        b_out,
        ln2_gain,
        ln2_bias,
        w_up,
        b_up,
        w_down,
        b_down,
    ) = params
    f32 = jnp.float32
    bf16 = jnp.bfloat16
    seq_len, model_width = tokens_row.shape
    head_size = model_width // HEADS
    score_scale = head_size ** (-0.5)
    base_rows = tokens_row.astype(f32) + table_row
    normed1, inv_first = normalize(base_rows)
    hidden1 = (normed1 * ln1_gain + ln1_bias).astype(bf16)
    query_rows = (jnp.dot(hidden1, w_query, preferred_element_type=f32) + b_query).astype(bf16)
    key_rows = jnp.dot(hidden1, w_key, preferred_element_type=f32).astype(bf16)
    value_rows = (jnp.dot(hidden1, w_value, preferred_element_type=f32) + b_value).astype(bf16)
    query_heads = query_rows.reshape(seq_len, HEADS, head_size)
    key_heads = key_rows.reshape(seq_len, HEADS, head_size)
    value_heads = value_rows.reshape(seq_len, HEADS, head_size)
    allowed = jnp.repeat(map_row, KBLK, axis=1)
    masks = []
    logs = []
    mixed_parts = []
    for block_index in range(seq_len // QBLK):
        lower = block_index * QBLK
        key_mask = (seg_row[lower : lower + QBLK, None] == seg_row[None, :]) & (
            allowed[block_index][None, :] == 1
        )
        attn_prob, log_total = score_block(
            query_heads[lower : lower + QBLK], key_heads, key_mask, None, score_scale
        )
        mixed_parts.append(
            jnp.einsum(
                "hqk,khd->qhd", attn_prob.astype(bf16), value_heads, preferred_element_type=f32
            )
        )
        masks.append(key_mask)
        logs.append(log_total)
    mixed_rows = jnp.concatenate(mixed_parts, axis=0).reshape(seq_len, model_width).astype(bf16)
    middle = base_rows + jnp.dot(mixed_rows, w_out, preferred_element_type=f32) + b_out
    normed2, inv_second = normalize(middle)
    hidden2 = (normed2 * ln2_gain + ln2_bias).astype(bf16)
    up_rows = jnp.dot(hidden2, w_up, preferred_element_type=f32) + b_up
    active, gelu_back = jax.vjp(gelu_exact, up_rows)
    active_low = active.astype(bf16)
    result = (middle + jnp.dot(active_low, w_down, preferred_element_type=f32) + b_down).astype(
        bf16
    )
    grad_out = cot_row.astype(f32)
    grad_w_down = jnp.einsum("sf,sd->fd", active_low, cot_row, preferred_element_type=f32)
    grad_b_down = jnp.sum(grad_out, axis=0)
    grad_active = jnp.einsum("sd,fd->sf", cot_row, w_down, preferred_element_type=f32)
    grad_up = gelu_back(grad_active)[0].astype(bf16)
    grad_w_up = jnp.einsum("sd,sf->df", hidden2, grad_up, preferred_element_type=f32)
    grad_b_up = jnp.sum(grad_up.astype(f32), axis=0)
    grad_hidden2 = jnp.einsum("sf,df->sd", grad_up, w_up, preferred_element_type=f32)
    grad_norm2, grad_ln2_gain, grad_ln2_bias = norm_back(
        grad_hidden2, normed2, inv_second, ln2_gain
    )
    grad_middle = grad_out + grad_norm2
    grad_branch = grad_middle.astype(bf16)
    grad_w_out = jnp.einsum("se,sd->ed", mixed_rows, grad_branch, preferred_element_type=f32)
    grad_b_out = jnp.sum(grad_branch.astype(f32), axis=0)
    grad_mixed = jnp.einsum("sd,ed->se", grad_branch, w_out, preferred_element_type=f32).astype(
        bf16
    )
    grad_mixed = grad_mixed.reshape(seq_len, HEADS, head_size)
    grad_key = jnp.zeros((seq_len, HEADS, head_size), f32)
    grad_value = jnp.zeros((seq_len, HEADS, head_size), f32)
    query_parts = []
    for block_index in range(seq_len // QBLK):
        lower = block_index * QBLK
        query_block = query_heads[lower : lower + QBLK]
        attn_prob, unused = score_block(
            query_block, key_heads, masks[block_index], logs[block_index], score_scale
        )
        grad_rows = grad_mixed[lower : lower + QBLK]
        grad_prob = jnp.einsum("qhd,khd->hqk", grad_rows, value_heads, preferred_element_type=f32)
        row_delta = jnp.sum(attn_prob * grad_prob, axis=-1, keepdims=True)
        grad_score = (attn_prob * (grad_prob - row_delta)).astype(bf16)
        query_parts.append(
            jnp.einsum("hqk,khd->qhd", grad_score, key_heads, preferred_element_type=f32)
            * score_scale
        )
        grad_key = (
            grad_key
            + jnp.einsum("hqk,qhd->khd", grad_score, query_block, preferred_element_type=f32)
            * score_scale
        )
        grad_value = grad_value + jnp.einsum(
            "hqk,qhd->khd", attn_prob.astype(bf16), grad_rows, preferred_element_type=f32
        )
    grad_query = jnp.concatenate(query_parts, axis=0).reshape(seq_len, model_width).astype(bf16)
    grad_key = grad_key.reshape(seq_len, model_width).astype(bf16)
    grad_value = grad_value.reshape(seq_len, model_width).astype(bf16)
    grad_w_query = jnp.einsum("sd,se->de", hidden1, grad_query, preferred_element_type=f32)
    grad_b_query = jnp.sum(grad_query.astype(f32), axis=0)
    grad_w_key = jnp.einsum("sd,se->de", hidden1, grad_key, preferred_element_type=f32)
    grad_w_value = jnp.einsum("sd,se->de", hidden1, grad_value, preferred_element_type=f32)
    grad_b_value = jnp.sum(grad_value.astype(f32), axis=0)
    grad_hidden1 = (
        jnp.einsum("se,de->sd", grad_query, w_query, preferred_element_type=f32)
        + jnp.einsum("se,de->sd", grad_key, w_key, preferred_element_type=f32)
        + jnp.einsum("se,de->sd", grad_value, w_value, preferred_element_type=f32)
    )
    grad_norm1, grad_ln1_gain, grad_ln1_bias = norm_back(grad_hidden1, normed1, inv_first, ln1_gain)
    grad_base = grad_middle + grad_norm1
    row_sum = jnp.sum(grad_base, axis=0)
    local_grads = (
        grad_ln1_gain,
        grad_ln1_bias,
        grad_w_query,
        grad_b_query,
        grad_w_key,
        grad_w_value,
        grad_b_value,
        grad_w_out,
        grad_b_out,
        grad_ln2_gain,
        grad_ln2_bias,
        grad_w_up,
        grad_b_up,
        grad_w_down,
        grad_b_down,
    )
    return (result, grad_base.astype(bf16), row_sum, local_grads)


def on_device(
    tokens_in,
    cotangent,
    segment_ids,
    block_map,
    timesteps,
    step_table,
    ln1_gain,
    ln1_bias,
    w_query,
    b_query,
    w_key,
    w_value,
    b_value,
    w_out,
    b_out,
    ln2_gain,
    ln2_bias,
    w_up,
    b_up,
    w_down,
    b_down,
):
    f32 = jnp.float32
    bf16 = jnp.bfloat16
    owned_rest = (
        ln1_gain,
        ln1_bias,
        w_query,
        b_query,
        w_key,
        w_value,
        b_value,
        w_out,
        b_out,
        ln2_gain,
        ln2_bias,
        w_up,
        b_up,
        w_down,
        b_down,
    )
    shard_count = lax.axis_size("shard")
    own_rows = step_table.shape[0]

    def fetch_all():
        full = (
            lax.all_gather(step_table, "shard", axis=0, tiled=True),
            lax.all_gather(ln1_gain, "shard", axis=0, tiled=True),
            lax.all_gather(ln1_bias, "shard", axis=0, tiled=True),
            lax.all_gather(w_query, "shard", axis=0, tiled=True),
            lax.all_gather(b_query, "shard", axis=0, tiled=True),
            lax.all_gather(w_key, "shard", axis=0, tiled=True),
            lax.all_gather(w_value, "shard", axis=0, tiled=True),
            lax.all_gather(b_value, "shard", axis=0, tiled=True),
            lax.all_gather(w_out, "shard", axis=0, tiled=True),
            lax.all_gather(b_out, "shard", axis=0, tiled=True),
            lax.all_gather(ln2_gain, "shard", axis=0, tiled=True),
            lax.all_gather(ln2_bias, "shard", axis=0, tiled=True),
            lax.all_gather(w_up, "shard", axis=0, tiled=True),
            lax.all_gather(b_up, "shard", axis=0, tiled=True),
            lax.all_gather(w_down, "shard", axis=0, tiled=True),
            lax.all_gather(b_down, "shard", axis=0, tiled=True),
        )
        return (full[0], tuple(full[1:]))

    rest_init = tuple(
        (
            jnp.zeros((member.shape[0] * shard_count,) + member.shape[1:], f32)
            for member in owned_rest
        )
    )
    table_init = jnp.zeros((own_rows * shard_count, step_table.shape[1]), f32)

    def visit(carry, slices):
        table_acc, rest_acc = carry
        tokens_row, cot_row, seg_row, map_row, step_input = slices
        full_table, params = fetch_all()
        picker = (
            lax.broadcasted_iota(jnp.int32, (1, full_table.shape[0]), 1) == step_input
        ).astype(bf16)
        table_row = jnp.dot(picker, full_table, preferred_element_type=f32)
        result, grad_row, row_sum, local_grads = sequence_pass(
            params, table_row, tokens_row, cot_row, seg_row, map_row
        )
        table_grad = picker.astype(f32).T * row_sum[None, :]
        table_grad = table_acc + table_grad
        new_rest = jax.tree.map(jnp.add, rest_acc, tuple(local_grads))
        return ((table_grad, new_rest), (result, grad_row))

    (table_acc, rest_acc), (outputs, grad_rows) = lax.scan(
        visit, (table_init, rest_init), (tokens_in, cotangent, segment_ids, block_map, timesteps)
    )
    summed = (
        lax.psum_scatter(table_acc, "shard", scatter_dimension=0, tiled=True),
        lax.psum_scatter(rest_acc[0], "shard", scatter_dimension=0, tiled=True),
        lax.psum_scatter(rest_acc[1], "shard", scatter_dimension=0, tiled=True),
        lax.psum_scatter(rest_acc[2], "shard", scatter_dimension=0, tiled=True),
        lax.psum_scatter(rest_acc[3], "shard", scatter_dimension=0, tiled=True),
        lax.psum_scatter(rest_acc[4], "shard", scatter_dimension=0, tiled=True),
        lax.psum_scatter(rest_acc[5], "shard", scatter_dimension=0, tiled=True),
        lax.psum_scatter(rest_acc[6], "shard", scatter_dimension=0, tiled=True),
        lax.psum_scatter(rest_acc[7], "shard", scatter_dimension=0, tiled=True),
        lax.psum_scatter(rest_acc[8], "shard", scatter_dimension=0, tiled=True),
        lax.psum_scatter(rest_acc[9], "shard", scatter_dimension=0, tiled=True),
        lax.psum_scatter(rest_acc[10], "shard", scatter_dimension=0, tiled=True),
        lax.psum_scatter(rest_acc[11], "shard", scatter_dimension=0, tiled=True),
        lax.psum_scatter(rest_acc[12], "shard", scatter_dimension=0, tiled=True),
        lax.psum_scatter(rest_acc[13], "shard", scatter_dimension=0, tiled=True),
        lax.psum_scatter(rest_acc[14], "shard", scatter_dimension=0, tiled=True),
    )
    table_acc = summed[0]
    rest_acc = summed[1:]
    totals = lax.psum(
        (
            table_acc,
            rest_acc[0],
            rest_acc[1],
            rest_acc[2],
            rest_acc[3],
            rest_acc[4],
            rest_acc[5],
            rest_acc[6],
            rest_acc[7],
            rest_acc[8],
            rest_acc[9],
            rest_acc[10],
            rest_acc[11],
            rest_acc[12],
            rest_acc[13],
            rest_acc[14],
        ),
        "rep",
    )
    return (
        outputs,
        grad_rows,
        totals[0],
        totals[1],
        totals[2],
        totals[3],
        totals[4],
        totals[5],
        totals[6],
        totals[7],
        totals[8],
        totals[9],
        totals[10],
        totals[11],
        totals[12],
        totals[13],
        totals[14],
        totals[15],
    )


def solution(mesh):
    in_specs = (
        P(("rep", "shard"), None, None),
        P(("rep", "shard"), None, None),
        P(("rep", "shard"), None),
        P(("rep", "shard"), None, None),
        P(("rep", "shard")),
        P("shard", None),
        P("shard"),
        P("shard"),
        P("shard", None),
        P("shard"),
        P("shard", None),
        P("shard", None),
        P("shard"),
        P("shard", None),
        P("shard"),
        P("shard"),
        P("shard"),
        P("shard", None),
        P("shard"),
        P("shard", None),
        P("shard"),
    )
    out_specs = (
        P(("rep", "shard"), None, None),
        P(("rep", "shard"), None, None),
        P("shard", None),
        P("shard"),
        P("shard"),
        P("shard", None),
        P("shard"),
        P("shard", None),
        P("shard", None),
        P("shard"),
        P("shard", None),
        P("shard"),
        P("shard"),
        P("shard"),
        P("shard", None),
        P("shard"),
        P("shard", None),
        P("shard"),
    )
    return jax.shard_map(
        on_device, mesh=mesh, in_specs=in_specs, out_specs=out_specs, check_vma=False
    )
```

profile of v0, /device:TPU:0, one launch (start us, length us, event | category | flops | bytes accessed | tf_op | source)
XLA Modules:
  0.0 2028.1 jit_solution(6277995507341451473)
XLA Ops:
  8.2 1223.7 %while.45 = (s32[]{:T(128)}, f32[1024,768]{1,0:T(8,128)}, f32[768]{0:T(1024)}, f32[768]{0:T(1024)}, f32[768,768]{1,0:T(8,128)}, /*index=5*/f32[768]{0:T(1024)}, ...) while((s32[]{:T(128)}, f32[1024,768]{1,0:T(8,128)}, ...), condition=%wide.region_25.26_spmd.clone, body=%wide.region_0.25_spmd.clone.sunk | while | flops 53939544064 | bytes 1227040896 | solution.py:281
  26.5 39.2 %all-reduce.30 = (bf16[768]{0:T(1024)(128)(2,1)S(1)}, bf16[768]{0:T(1024)(128)(2,1)S(1)}, bf16[768]{0:T(1024)(128)(2,1)S(1)}, bf16[768]{0:T(1024)(128)(2,1)S(1)}...) all-reduce(bf16[768]{0:T(1024)(128)(2,1)S(1)} %dynamic-update-slice, ...), channel_id=1, replica_groups=mesh['rep'=4,'shard'=8] {'shard'}, use_global_device_ids=true, to_apply=%add.2 | all-reduce | flops 6144 | bytes 24576 | tf_op jit(solution)/shard_map/while
  67.8 26.0 %all-gather.3 = bf16[8,1,384]{2,1,0:T(2,128)(2,1)S(1)} all-gather(bf16[1,1,384]{2,1,0:T(2,128)(2,1)S(1)} %reshape.433), channel_id=1, replica_groups=mesh['rep'=4,'shard'=8] {'shard'}, dimensions={0}, use_global_device_ids=true | all-gather | bytes 6912 | tf_op jit(solution)/shard_map/while/body/eval_jaxpr/all_gather | solution.py:251
  104.9 38.4 %all-gather.18.cloned.1.call-done = bf16[768,768]{1,0:T(8,128)(2,1)} async-done(((bf16[96,768]{1,0:T(8,128)(2,1)}), bf16[768,768]{1,0:T(8,128)(2,1)}) %all-gather.18.cloned.1.call-update) | async-done | bytes 1179664 | tf_op jit(solution)/shard_map/while/body/eval_jaxpr/all_gather | solution.py:243
  231.4 76.3 %all-gather.22.cloned.1.call-done = bf16[768,3072]{1,0:T(8,128)(2,1)} async-done(((bf16[96,3072]{1,0:T(8,128)(2,1)}), bf16[768,3072]{1,0:T(8,128)(2,1)}) %all-gather.22.cloned.1.call-update) | async-done | bytes 4718608 | tf_op jit(solution)/shard_map/while/body/eval_jaxpr/all_gather | solution.py:250
  307.7 35.9 %multiply_convert_fusion.8 = (bf16[1024,3072]{1,0:T(8,128)(2,1)}, f32[1024,3072]{1,0:T(8,128)}, f32[1024,3072]{1,0:T(8,128)}) fusion(f32[3072]{0:T(1024)S(1)} %bitcast.336, bf16[768,3072]{1,0:T(8,128)(2,1)} %all-gather.22.cloned.1.call-done, f32[1024,768]{1,0:T(8,128)S(1)} %get-tuple-element.865, f32[768]{0:T(1024)S(1)} %convert_element_type.417, ...), kind=kOutput, calls=%fused_computation.14.clone.1 | convolution fusion | flops 5043388416 | bytes 39348224 | tf_op jit(solution)/shard_map/while/body/eval_jaxpr/dot_general | solution.py:105
  343.6 44.4 %all-gather.24.cloned.1.call-done = bf16[3072,768]{1,0:T(8,128)(2,1)} async-done(((bf16[384,768]{1,0:T(8,128)(2,1)}), bf16[3072,768]{1,0:T(8,128)(2,1)}) %all-gather.24.cloned.1.call-update) | async-done | bytes 4718608 | tf_op jit(solution)/shard_map/while/body/eval_jaxpr/all_gather | solution.py:252
  434.7 22.0 %multiply_reduce_fusion.14 = (f32[12,512]{1,0:T(8,128)S(1)}, f32[12,512,1024]{2,1,0:T(8,128)}) fusion(f32[12,512]{1,0:T(8,128)S(1)} %copy-done.31, f32[12,512,1024]{2,1,0:T(8,128)} %get-tuple-element.864, pred[512,1024]{1,0:T(8,128)(4,1)S(1)} %copy-done.12, bf16[512,12,64]{0,2,1:T(8,128)(2,1)S(1)} %bitcast.334, bf16[1024,12,64]{0,2,1:T(8,128)(2,1)S(1)} %bitcast.342), kind=kOutput, calls=%fused_computation.3.clone.1 | convolution fusion | flops 843048960 | bytes 53264384 | tf_op jit(solution)/shard_map/while/body/eval_jaxpr/qhd,khd->hqk/dot_general | solution.py:140
  637.1 34.6 %all-reduce.30 = (bf16[768]{0:T(1024)(128)(2,1)S(1)}, bf16[768]{0:T(1024)(128)(2,1)S(1)}, bf16[768]{0:T(1024)(128)(2,1)S(1)}, bf16[768]{0:T(1024)(128)(2,1)S(1)}...) all-reduce(bf16[768]{0:T(1024)(128)(2,1)S(1)} %dynamic-update-slice, ...), channel_id=1, replica_groups=mesh['rep'=4,'shard'=8] {'shard'}, use_global_device_ids=true, to_apply=%add.2 | all-reduce | flops 6144 | bytes 24576 | tf_op jit(solution)/shard_map/while
  673.9 25.9 %all-gather.3 = bf16[8,1,384]{2,1,0:T(2,128)(2,1)S(1)} all-gather(bf16[1,1,384]{2,1,0:T(2,128)(2,1)S(1)} %reshape.433), channel_id=1, replica_groups=mesh['rep'=4,'shard'=8] {'shard'}, dimensions={0}, use_global_device_ids=true | all-gather | bytes 6912 | tf_op jit(solution)/shard_map/while/body/eval_jaxpr/all_gather | solution.py:251
  710.6 38.2 %all-gather.18.cloned.1.call-done = bf16[768,768]{1,0:T(8,128)(2,1)} async-done(((bf16[96,768]{1,0:T(8,128)(2,1)}), bf16[768,768]{1,0:T(8,128)(2,1)}) %all-gather.18.cloned.1.call-update) | async-done | bytes 1179664 | tf_op jit(solution)/shard_map/while/body/eval_jaxpr/all_gather | solution.py:243
  837.2 76.4 %all-gather.22.cloned.1.call-done = bf16[768,3072]{1,0:T(8,128)(2,1)} async-done(((bf16[96,3072]{1,0:T(8,128)(2,1)}), bf16[768,3072]{1,0:T(8,128)(2,1)}) %all-gather.22.cloned.1.call-update) | async-done | bytes 4718608 | tf_op jit(solution)/shard_map/while/body/eval_jaxpr/all_gather | solution.py:250
  913.6 36.1 %multiply_convert_fusion.8 = (bf16[1024,3072]{1,0:T(8,128)(2,1)}, f32[1024,3072]{1,0:T(8,128)}, f32[1024,3072]{1,0:T(8,128)}) fusion(f32[3072]{0:T(1024)S(1)} %bitcast.336, bf16[768,3072]{1,0:T(8,128)(2,1)} %all-gather.22.cloned.1.call-done, f32[1024,768]{1,0:T(8,128)S(1)} %get-tuple-element.865, f32[768]{0:T(1024)S(1)} %convert_element_type.417, ...), kind=kOutput, calls=%fused_computation.14.clone.1 | convolution fusion | flops 5043388416 | bytes 39348224 | tf_op jit(solution)/shard_map/while/body/eval_jaxpr/dot_general | solution.py:105
  949.8 43.9 %all-gather.24.cloned.1.call-done = bf16[3072,768]{1,0:T(8,128)(2,1)} async-done(((bf16[384,768]{1,0:T(8,128)(2,1)}), bf16[3072,768]{1,0:T(8,128)(2,1)}) %all-gather.24.cloned.1.call-update) | async-done | bytes 4718608 | tf_op jit(solution)/shard_map/while/body/eval_jaxpr/all_gather | solution.py:252
  1040.5 22.0 %multiply_reduce_fusion.14 = (f32[12,512]{1,0:T(8,128)S(1)}, f32[12,512,1024]{2,1,0:T(8,128)}) fusion(f32[12,512]{1,0:T(8,128)S(1)} %copy-done.31, f32[12,512,1024]{2,1,0:T(8,128)} %get-tuple-element.864, pred[512,1024]{1,0:T(8,128)(4,1)S(1)} %copy-done.12, bf16[512,12,64]{0,2,1:T(8,128)(2,1)S(1)} %bitcast.334, bf16[1024,12,64]{0,2,1:T(8,128)(2,1)S(1)} %bitcast.342), kind=kOutput, calls=%fused_computation.3.clone.1 | convolution fusion | flops 843048960 | bytes 53264384 | tf_op jit(solution)/shard_map/while/body/eval_jaxpr/qhd,khd->hqk/dot_general | solution.py:140
  1236.6 66.4 %reduce-scatter.10.cloned.1.call-done = f32[96,768]{1,0:T(8,128)} async-done(((f32[768,768]{1,0:T(8,128)}), f32[96,768]{1,0:T(8,128)}) %reduce-scatter.10.cloned.1.call-update) | async-done | bytes 294928 | tf_op jit(solution)/shard_map/reduce_scatter | solution.py:288
  1303.0 71.7 %reduce-scatter.12.cloned.1.call-done = f32[96,768]{1,0:T(8,128)} async-done(((f32[768,768]{1,0:T(8,128)}), f32[96,768]{1,0:T(8,128)}) %reduce-scatter.12.cloned.1.call-update) | async-done | bytes 294928 | tf_op jit(solution)/shard_map/reduce_scatter | solution.py:290
  1374.7 71.4 %reduce-scatter.14.cloned.1.call-done = f32[96,768]{1,0:T(8,128)} async-done(((f32[768,768]{1,0:T(8,128)}), f32[96,768]{1,0:T(8,128)}) %reduce-scatter.14.cloned.1.call-update) | async-done | bytes 294928 | tf_op jit(solution)/shard_map/reduce_scatter | solution.py:291
  1446.2 71.5 %reduce-scatter.16.cloned.1.call-done = f32[96,768]{1,0:T(8,128)} async-done(((f32[768,768]{1,0:T(8,128)}), f32[96,768]{1,0:T(8,128)}) %reduce-scatter.16.cloned.1.call-update) | async-done | bytes 294928 | tf_op jit(solution)/shard_map/reduce_scatter | solution.py:293
  1517.7 76.7 %reduce-scatter.8.cloned.1.call-done = f32[128,768]{1,0:T(8,128)} async-done(((f32[1024,768]{1,0:T(8,128)}), f32[128,768]{1,0:T(8,128)}) %reduce-scatter.8.cloned.1.call-update) | async-done | bytes 393232 | tf_op jit(solution)/shard_map/reduce_scatter | solution.py:285
  1594.4 165.8 %reduce-scatter.18.cloned.1.call-done = f32[96,3072]{1,0:T(8,128)} async-done(((f32[768,3072]{1,0:T(8,128)}), f32[96,3072]{1,0:T(8,128)}) %reduce-scatter.18.cloned.1.call-update) | async-done | bytes 1179664 | tf_op jit(solution)/shard_map/reduce_scatter | solution.py:297
  1760.2 165.6 %reduce-scatter.20.cloned.1.call-done = f32[384,768]{1,0:T(8,128)} async-done(((f32[3072,768]{1,0:T(8,128)}), f32[384,768]{1,0:T(8,128)}) %reduce-scatter.20.cloned.1.call-update) | async-done | bytes 1179664 | tf_op jit(solution)/shard_map/reduce_scatter | solution.py:299
  1927.8 35.6 %all-reduce.26 = (f32[768]{0:T(1024)S(1)}, f32[768]{0:T(1024)S(1)}, f32[768]{0:T(1024)S(1)}, f32[768]{0:T(1024)S(1)}, f32[768]{0:T(1024)S(1)}, /*index=5*/f32[76...) all-reduce(f32[768]{0:T(1024)S(1)} %copy-done.73, ...), channel_id=3, replica_groups=mesh['rep'=4,'shard'=8] {'shard'}, use_global_device_ids=true, to_apply=%region_28.29.clone | all-reduce | flops 9216 | bytes 73728
  1970.4 39.5 %all-reduce.33.cloned.1.call-done = (f32[128,768]{1,0:T(8,128)}, f32[96,768]{1,0:T(8,128)}, f32[96,768]{1,0:T(8,128)}, f32[96,768]{1,0:T(8,128)}, f32[96,768]{1,...) async-done(((f32[128,768]{1,0:T(8,128)}, f32[96,768]{1,0:T(8,128)}, f32[96,768]{1,0:T(8,128)}, f32[96,768]{1,0:T(8,128)}, f32[96,768]{1,0:T(8,128)}, ...) | async-done | bytes 3932176 | tf_op jit(solution)/shard_map/psum | solution.py:304
  (628 shorter events, 680.4 us)
Async XLA Ops:
  8.5 86.2 %all-gather.14.cloned.1.call-start = ((), (), s32[]{:S(2)}) async-start(), calls=%async_computation.16 | async-start | bytes 1769472 | tf_op jit(solution)/shard_map/while/body/eval_jaxpr/all_gather | solution.py:238
  9.2 91.9 %all-gather.16.cloned.1.call-start = ((), (), s32[]{:S(2)}) async-start(), calls=%async_computation.17 | async-start | bytes 1327104 | tf_op jit(solution)/shard_map/while/body/eval_jaxpr/all_gather | solution.py:241
  10.0 133.2 %all-gather.18.cloned.1.call-start = ((), (), s32[]{:S(2)}) async-start(), calls=%async_computation.18 | async-start | bytes 1327104 | tf_op jit(solution)/shard_map/while/body/eval_jaxpr/all_gather | solution.py:243
  10.7 183.3 %all-gather.12.cloned.1.call-start = ((), (), s32[]{:S(2)}) async-start(), calls=%async_computation.15 | async-start | bytes 1327104 | tf_op jit(solution)/shard_map/while/body/eval_jaxpr/all_gather | solution.py:244
  11.3 215.7 %all-gather.20.cloned.1.call-start = ((), (), s32[]{:S(2)}) async-start(), calls=%async_computation.19 | async-start | bytes 1327104 | tf_op jit(solution)/shard_map/while/body/eval_jaxpr/all_gather | solution.py:246
  11.9 295.9 %all-gather.22.cloned.1.call-start = ((), (), s32[]{:S(2)}) async-start(), calls=%async_computation.20 | async-start | bytes 5308416 | tf_op jit(solution)/shard_map/while/body/eval_jaxpr/all_gather | solution.py:250
  12.5 375.5 %all-gather.24.cloned.1.call-start = ((), (), s32[]{:S(2)}) async-start(), calls=%async_computation.21 | async-start | bytes 5308416 | tf_op jit(solution)/shard_map/while/body/eval_jaxpr/all_gather | solution.py:252
  619.1 81.5 %all-gather.14.cloned.1.call-start = ((), (), s32[]{:S(2)}) async-start(), calls=%async_computation.16 | async-start | bytes 1769472 | tf_op jit(solution)/shard_map/while/body/eval_jaxpr/all_gather | solution.py:238
  619.9 87.1 %all-gather.16.cloned.1.call-start = ((), (), s32[]{:S(2)}) async-start(), calls=%async_computation.17 | async-start | bytes 1327104 | tf_op jit(solution)/shard_map/while/body/eval_jaxpr/all_gather | solution.py:241
  620.6 128.2 %all-gather.18.cloned.1.call-start = ((), (), s32[]{:S(2)}) async-start(), calls=%async_computation.18 | async-start | bytes 1327104 | tf_op jit(solution)/shard_map/while/body/eval_jaxpr/all_gather | solution.py:243
  621.2 178.3 %all-gather.12.cloned.1.call-start = ((), (), s32[]{:S(2)}) async-start(), calls=%async_computation.15 | async-start | bytes 1327104 | tf_op jit(solution)/shard_map/while/body/eval_jaxpr/all_gather | solution.py:244
  621.9 210.9 %all-gather.20.cloned.1.call-start = ((), (), s32[]{:S(2)}) async-start(), calls=%async_computation.19 | async-start | bytes 1327104 | tf_op jit(solution)/shard_map/while/body/eval_jaxpr/all_gather | solution.py:246
  622.5 291.1 %all-gather.22.cloned.1.call-start = ((), (), s32[]{:S(2)}) async-start(), calls=%async_computation.20 | async-start | bytes 5308416 | tf_op jit(solution)/shard_map/while/body/eval_jaxpr/all_gather | solution.py:250
  623.3 370.5 %all-gather.24.cloned.1.call-start = ((), (), s32[]{:S(2)}) async-start(), calls=%async_computation.21 | async-start | bytes 5308416 | tf_op jit(solution)/shard_map/while/body/eval_jaxpr/all_gather | solution.py:252
  1231.9 71.1 %reduce-scatter.10.cloned.1.call-start = ((), (), s32[]{:S(2)}) async-start(), calls=%async_computation.8 | async-start | bytes 2654208 | tf_op jit(solution)/shard_map/reduce_scatter | solution.py:288
  1232.4 142.3 %reduce-scatter.12.cloned.1.call-start = ((), (), s32[]{:S(2)}) async-start(), calls=%async_computation.9 | async-start | bytes 2654208 | tf_op jit(solution)/shard_map/reduce_scatter | solution.py:290
  1233.0 213.1 %reduce-scatter.14.cloned.1.call-start = ((), (), s32[]{:S(2)}) async-start(), calls=%async_computation.10 | async-start | bytes 2654208 | tf_op jit(solution)/shard_map/reduce_scatter | solution.py:291
  1233.6 284.1 %reduce-scatter.16.cloned.1.call-start = ((), (), s32[]{:S(2)}) async-start(), calls=%async_computation.11 | async-start | bytes 2654208 | tf_op jit(solution)/shard_map/reduce_scatter | solution.py:293
  1234.4 360.0 %reduce-scatter.8.cloned.1.call-start = ((), (), s32[]{:S(2)}) async-start(), calls=%async_computation.7 | async-start | bytes 3538944 | tf_op jit(solution)/shard_map/reduce_scatter | solution.py:285
  1235.1 525.1 %reduce-scatter.18.cloned.1.call-start = ((), (), s32[]{:S(2)}) async-start(), calls=%async_computation.12 | async-start | bytes 10616832 | tf_op jit(solution)/shard_map/reduce_scatter | solution.py:297
  1235.8 690.0 %reduce-scatter.20.cloned.1.call-start = ((), (), s32[]{:S(2)}) async-start(), calls=%async_computation.13 | async-start | bytes 10616832 | tf_op jit(solution)/shard_map/reduce_scatter | solution.py:299
  1236.4 691.3 %copy-start.42 = (f32[3072]{0:T(1024)S(1)}, f32[3072]{0:T(1024)}, u32[]{:S(2)}) copy-start(f32[3072]{0:T(1024)} %get-tuple-element.252) | copy-start | bytes 36868
  1236.5 691.3 %copy-start.52 = (f32[768]{0:T(1024)S(1)}, f32[768]{0:T(1024)}, u32[]{:S(2)}) copy-start(f32[768]{0:T(1024)} %get-tuple-element.254) | copy-start | bytes 9220
  1236.5 773.4 %all-reduce.33.cloned.1.call-start = ((), (), s32[]{:S(2)}) async-start(), calls=%async_computation.14 | async-start | bytes 7864320 | tf_op jit(solution)/shard_map/psum | solution.py:304
  (170 other events, 8497.9 us)
Sparse Core Ops, SparseCore 0:
  11.5 47.1 all-gather.13
  60.9 40.2 all-gather.15
  103.3 39.8 all-gather.17
  145.2 39.8 all-gather.11
  187.2 39.8 all-gather.19
  229.1 78.6 all-gather.21
  309.9 78.0 all-gather.23
  622.1 42.4 all-gather.13
  666.8 40.1 all-gather.15
  709.0 39.8 all-gather.17
  751.0 39.8 all-gather.11
  792.9 39.8 all-gather.19
  835.0 78.6 all-gather.21
  915.7 78.0 all-gather.23
Sparse Core Ops, SparseCore 1:
  1235.8 67.1 reduce-scatter.9
  1306.4 68.3 reduce-scatter.11
  1378.1 68.0 reduce-scatter.13
  1449.7 68.0 reduce-scatter.15
  1521.3 73.0 reduce-scatter.7
  1598.0 162.1 reduce-scatter.17
  1763.7 162.1 reduce-scatter.19
  1928.5 81.3 all-reduce.32
where the time goes:
time: 2030 us
  waiting for transfers between devices  1070 us (53%)
  matrix products  553 us (27%)
  blocking collectives  168 us (8%)
  other arithmetic  148 us (7%)
  local copies, waits for them, and re-layouts  63.1 us (3%)
    reduce_scatter x1, waiting for transfers between devices, on_device(): lax.psum_scatter(rest_acc[11], 'shard', scatter_dimension=0, tiled=True)  166 us
    reduce_scatter x1, waiting for transfers between devices, on_device(): lax.psum_scatter(rest_acc[13], 'shard', scatter_dimension=0, tiled=True)  166 us
    all_gather x2, waiting for transfers between devices, fetch_all(): lax.all_gather(w_up, 'shard', axis=0, tiled=True)  153 us
    all_gather x2, waiting for transfers between devices, fetch_all(): lax.all_gather(w_down, 'shard', axis=0, tiled=True)  88.3 us
    dot_general x4, matrix products, sequence_pass(): jnp.einsum('qhd,khd->hqk', grad_rows, value_heads, preferred_element_type...  88 us
    reduce_scatter x1, waiting for transfers between devices, on_device(): lax.psum_scatter(table_acc, 'shard', scatter_dimension=0, tiled=True)  76.7 us
    all_gather x2, waiting for transfers between devices, fetch_all(): lax.all_gather(w_key, 'shard', axis=0, tiled=True)  76.6 us
    while x2, blocking collectives  73.8 us
  transfers between devices with their start and end apart: 22, of which 18 were waited for; matrix products, arithmetic and copies ran while one was open for 14% of the time, Pallas kernels for 0%

commit v1 on v0

v1 whole, which is shorter than its diff:
```python
import jax
import jax.numpy as jnp
from jax import lax
from jax.experimental import pallas as pl
from jax.experimental.pallas import tpu as pltpu
from jax.sharding import Mesh, PartitionSpec as P

HEADS = 12
HD = 64
QT = 256
KT = 256
RT = 512
FC = 512
EPS = 1e-05
NEG = -1e30
f32 = jnp.float32
bf16 = jnp.bfloat16
VMEM_BYTES = 60 * 1000 * 1024


def dg(x, y, cx, cy):
    return lax.dot_general(x, y, (((cx,), (cy,)), ((), ())), preferred_element_type=f32)


def normalize(values):
    center = values - jnp.mean(values, axis=-1, keepdims=True)
    inv_dev = lax.rsqrt(jnp.mean(center * center, axis=-1, keepdims=True) + EPS)
    return center * inv_dev, inv_dev


def norm_back(grad_hidden, normed, inv_dev, gain_row):
    grad_normed = grad_hidden * gain_row
    return inv_dev * (
        grad_normed
        - jnp.mean(grad_normed, axis=-1, keepdims=True)
        - normed * jnp.mean(grad_normed * normed, axis=-1, keepdims=True)
    )


def col_sum(values):
    return jnp.sum(values, axis=0, keepdims=True)


def gelu_parts(x):
    density = jnp.exp(-0.5 * x * x)
    t = 1.0 / (1.0 + 0.2316418882 * jnp.abs(x))
    poly = t * (0.127414796 + t * (-0.142248368 + t * (0.7107068705 + t * (-0.7265760135 + t * 0.5307027145))))
    tail = density * poly
    cdf = jnp.where(x >= 0.0, 1.0 - tail, tail)
    return x * cdf, cdf + x * (density * 0.3989422804014327)


def place_halves(mine, other, full, core, sems):
    half = mine.shape[1]
    at = pl.multiple_of(core * half, 128)
    rest = pl.multiple_of((1 - core) * half, 128)
    return (
        pltpu.make_async_copy(mine, full.at[:, pl.ds(at, half)], sems.at[0]),
        pltpu.make_async_copy(other, full.at[:, pl.ds(rest, half)], sems.at[1]),
    )


def params(**kw):
    return pltpu.CompilerParams(vmem_limit_bytes=VMEM_BYTES, **kw)


def qkv_kernel(core_ref, tok_ref, row_ref, vec_ref, bias_ref, mine_ref, other_ref,
               q_ref, k_ref, v_ref, qT_ref, kT_ref, vT_ref, w_ref, sems):
    @pl.when((pl.program_id(0) == 0) & (pl.program_id(1) == 0))
    def _():
        copies = place_halves(mine_ref, other_ref, w_ref, core_ref[0], sems)
        for c in copies:
            c.start()
        for c in copies:
            c.wait()

    width = tok_ref.shape[2]
    base = tok_ref[0].astype(f32) + row_ref[0]
    normed, unused = normalize(base)
    hidden = (normed * vec_ref[0:1, :] + vec_ref[1:2, :]).astype(bf16)
    scale = HD ** (-0.5)
    for n, (out, outT) in enumerate(((q_ref, qT_ref), (k_ref, kT_ref), (v_ref, vT_ref))):
        cols = slice(n * width, (n + 1) * width)
        rows = (dg(hidden, w_ref[:, cols], 1, 0) + bias_ref[:, cols]).astype(bf16)
        scaled = (rows.astype(f32) * scale).astype(bf16)
        out[0] = scaled if n == 0 else rows
        outT[0] = (rows if n == 2 else scaled).T


def qkv_call(core, tokens, trow, vec, bias, mine, other):
    B, S, D = tokens.shape
    row = pl.BlockSpec((1, RT, D), lambda b, i: (b, i, 0))
    col = pl.BlockSpec((1, D, RT), lambda b, i: (b, 0, i))
    anyspec = pl.BlockSpec(memory_space=pl.ANY)
    return pl.pallas_call(
        qkv_kernel,
        grid=(B, S // RT),
        in_specs=[
            pl.BlockSpec(memory_space=pltpu.SMEM),
            row,
            pl.BlockSpec((1, 1, D), lambda b, i: (b, 0, 0)),
            pl.BlockSpec(vec.shape, lambda b, i: (0, 0)),
            pl.BlockSpec(bias.shape, lambda b, i: (0, 0)),
            anyspec,
            anyspec,
        ],
        out_specs=[row, row, row, col, col, col],
        out_shape=[jax.ShapeDtypeStruct((B, S, D), bf16)] * 3 + [jax.ShapeDtypeStruct((B, D, S), bf16)] * 3,
        scratch_shapes=[pltpu.VMEM((D, 3 * D), bf16), pltpu.SemaphoreType.DMA((2,))],
        compiler_params=params(),
        name="norm_qkv",
    )(core, tokens, trow, vec, bias, mine, other)

def head_mask(h, rows):
    lane=lax.broadcasted_iota(jnp.int32,(rows,256),1)
    return (lane//64)==h

def fwd_kernel(lo_ref, hi_ref, q_ref, k_ref, vT_ref, segk_ref, segq_ref, mixed_ref, mixedT_ref, lse_ref, acc, mrow, lrow):
    b=pl.program_id(0); i=pl.program_id(1)
    nq=pl.num_programs(1)
    lo=lo_ref[b*nq+i]; hi=hi_ref[b*nq+i]
    segq=segq_ref[0]
    acc[...]=jnp.zeros_like(acc)
    mrow[...]=jnp.full_like(mrow,NEG); lrow[...]=jnp.zeros_like(lrow)
    def body(c,carry):
        c0=pl.multiple_of(c*KT,KT)
        segk=segk_ref[0,pl.ds(c0,KT),:]
        same=jnp.concatenate([segk,segk],axis=1)==segq
        bias=jnp.where(same,0.0,NEG)
        def scores(quad):
            k4=k_ref[0,pl.ds(c0,KT),quad*256:(quad+1)*256]
            km=jnp.concatenate([jnp.where(head_mask(j,KT),k4,jnp.zeros_like(k4)) for j in range(4)],axis=0)
            return dg(km,q_ref[0,:,quad*256:(quad+1)*256],1,1)
        s_next=scores(0)
        for quad in range(HEADS//4):
            s4=s_next
            if quad+1<HEADS//4: s_next=scores(quad+1)
            for j in range(4):
                h=quad*4+j
                s=s4[j*KT:(j+1)*KT]+bias
                m_old=mrow[h:h+1,:]
                m_new=jnp.maximum(m_old,jnp.max(s,axis=0,keepdims=True))
                p=jnp.exp(s-m_new)
                alpha=jnp.exp(m_old-m_new)
                mrow[h:h+1,:]=m_new
                lrow[h:h+1,:]=lrow[h:h+1,:]*alpha+jnp.sum(p,axis=0,keepdims=True)
                o=dg(vT_ref[0,h*HD:(h+1)*HD,pl.ds(c0,KT)],p.astype(bf16),1,0)
                acc[h*HD:(h+1)*HD,:]=acc[h*HD:(h+1)*HD,:]*alpha+o
        return carry
    lax.fori_loop(lo,hi,body,0)
    inv=1.0/lrow[...]
    lse_ref[0]=mrow[...]+jnp.log(lrow[...])
    for h in range(HEADS):
        o=acc[h*HD:(h+1)*HD,:]*inv[h:h+1,:]
        mixedT_ref[0,h*HD:(h+1)*HD,:]=o
    mixed_ref[0]=mixedT_ref[0].astype(bf16).T

def attn_fwd(lo,hi,q,k,vT,segk,segq):
    B,S,D=q.shape; nq=S//QT
    return pl.pallas_call(fwd_kernel,
      grid_spec=pltpu.PrefetchScalarGridSpec(num_scalar_prefetch=2, grid=(B,nq),
        in_specs=[pl.BlockSpec((1,QT,D),lambda b,i,*_:(b,i,0)),
                  pl.BlockSpec((1,S,D),lambda b,i,*_:(b,0,0)),
                  pl.BlockSpec((1,D,S),lambda b,i,*_:(b,0,0)),
                  pl.BlockSpec((1,S,128),lambda b,i,*_:(b,0,0)),
                  pl.BlockSpec((1,1,QT),lambda b,i,*_:(b,0,i))],
        out_specs=[pl.BlockSpec((1,QT,D),lambda b,i,*_:(b,i,0)),
                   pl.BlockSpec((1,D,QT),lambda b,i,*_:(b,0,i)),
                   pl.BlockSpec((1,HEADS,QT),lambda b,i,*_:(b,0,i))],
        scratch_shapes=[pltpu.VMEM((D,QT),f32),pltpu.VMEM((HEADS,QT),f32),pltpu.VMEM((HEADS,QT),f32)]),
      out_shape=[jax.ShapeDtypeStruct((B,S,D),bf16),jax.ShapeDtypeStruct((B,D,S),f32),jax.ShapeDtypeStruct((B,HEADS,S),f32)],
      compiler_params=params(),
      name="attn_fwd")(lo,hi,q,k,vT,segk,segq)

def bwd_kernel(lo_ref, hi_ref, q_ref, qT_ref, k_ref, kT_ref, v_ref, do_ref, doT_ref, oT_ref, lse_ref, segk_ref, segq_ref,
               dq_ref, dk_ref, dv_ref, dqT, dkT, dvT, dlt):
    b=pl.program_id(0); i=pl.program_id(1)
    nq=pl.num_programs(1)
    lo=lo_ref[b*nq+i]; hi=hi_ref[b*nq+i]
    segq=segq_ref[0]
    @pl.when(i==0)
    def _():
        dkT[...]=jnp.zeros_like(dkT); dvT[...]=jnp.zeros_like(dvT)
    dqT[...]=jnp.zeros_like(dqT)
    for h in range(HEADS):
        sl=slice(h*HD,(h+1)*HD)
        dlt[h:h+1,:]=jnp.sum(doT_ref[0,sl,:]*oT_ref[0,sl,:],axis=0,keepdims=True)
    def body(c,carry):
        c0=pl.multiple_of(c*KT,KT)
        segk=segk_ref[0,pl.ds(c0,KT),:]
        same=jnp.concatenate([segk,segk],axis=1)==segq
        bias=jnp.where(same,0.0,NEG)
        def two(quad):
            ql=slice(quad*256,(quad+1)*256)
            k4=k_ref[0,pl.ds(c0,KT),ql]; v4=v_ref[0,pl.ds(c0,KT),ql]
            km=jnp.concatenate([jnp.where(head_mask(j,KT),k4,jnp.zeros_like(k4)) for j in range(4)],axis=0)
            vm=jnp.concatenate([jnp.where(head_mask(j,KT),v4,jnp.zeros_like(v4)) for j in range(4)],axis=0)
            return dg(km,q_ref[0,:,ql],1,1), dg(vm,do_ref[0,:,ql],1,1)
        nxt=two(0)
        for quad in range(HEADS//4):
            s4,dp4=nxt
            if quad+1<HEADS//4: nxt=two(quad+1)
            for j in range(4):
                h=quad*4+j; sl=slice(h*HD,(h+1)*HD)
                p=jnp.exp(s4[j*KT:(j+1)*KT]+bias-lse_ref[0,h:h+1,:])
                ds=(p*(dp4[j*KT:(j+1)*KT]-dlt[h:h+1,:])).astype(bf16)
                pb=p.astype(bf16)
                dvT[sl,pl.ds(c0,KT)]+=dg(doT_ref[0,sl,:],pb,1,1)
                dkT[sl,pl.ds(c0,KT)]+=dg(qT_ref[0,sl,:],ds,1,1)
                dqT[sl,:]+=dg(kT_ref[0,sl,pl.ds(c0,KT)],ds,1,0)
        return carry
    lax.fori_loop(lo,hi,body,0)
    dq_ref[0]=dqT[...].astype(bf16).T
    @pl.when(i==nq-1)
    def _():
        dk_ref[0]=dkT[...].astype(bf16).T
        dv_ref[0]=dvT[...].astype(bf16).T

def attn_bwd(lo,hi,q,qT,k,kT,v,do,doT,oT,lse,segk,segq):
    B,S,D=q.shape; nq=S//QT
    row=pl.BlockSpec((1,QT,D),lambda b,i,*_:(b,i,0))
    col=pl.BlockSpec((1,D,QT),lambda b,i,*_:(b,0,i))
    full=pl.BlockSpec((1,S,D),lambda b,i,*_:(b,0,0))
    fullT=pl.BlockSpec((1,D,S),lambda b,i,*_:(b,0,0))
    return pl.pallas_call(bwd_kernel,
      grid_spec=pltpu.PrefetchScalarGridSpec(num_scalar_prefetch=2, grid=(B,nq),
        in_specs=[row,col,full,fullT,full,row,col,col,
                  pl.BlockSpec((1,HEADS,QT),lambda b,i,*_:(b,0,i)),
                  pl.BlockSpec((1,S,128),lambda b,i,*_:(b,0,0)),
                  pl.BlockSpec((1,1,QT),lambda b,i,*_:(b,0,i))],
        out_specs=[row,full,full],
        scratch_shapes=[pltpu.VMEM((D,QT),f32),pltpu.VMEM((D,S),f32),pltpu.VMEM((D,S),f32),pltpu.VMEM((HEADS,QT),f32)]),
      out_shape=[jax.ShapeDtypeStruct((B,S,D),bf16)]*3,
      compiler_params=params(),
      name="attn_bwd")(lo,hi,q,qT,k,kT,v,do,doT,oT,lse,segk,segq)


def mlp_kernel(core_ref, tok_ref, row_ref, cot_ref, mix_ref, vec_ref, bup_ref,
               ou_mine, ou_other, d_mine, d_other,
               out_ref, gmid_ref, gmix_ref, gmixT_ref, vecg_ref, bupg_ref,
               ou_keep, ou_send, d_keep, d_send,
               wout, wup, wdown, aout, aup, adown, acc, gh2, hid, sems):
    i = pl.program_id(0)
    core = core_ref[0]
    D = tok_ref.shape[2]
    FF = wup.shape[1]
    hd, hf = D // 2, FF // 2
    at = (core, 1 - core)

    def weight_copies(out, refs_ou, refs_d):
        made = []
        for n in range(2):
            cd = pl.multiple_of(at[n] * hd, 128)
            cf = pl.multiple_of(at[n] * hf, 128)
            pairs = (
                (refs_ou[n].at[:, pl.ds(0, hd)], wout.at[:, pl.ds(cd, hd)]),
                (refs_ou[n].at[:, pl.ds(hd, hf)], wup.at[:, pl.ds(cf, hf)]),
                (refs_d[n], wdown.at[:, pl.ds(cd, hd)]),
            )
            for m, (hbm, vmem) in enumerate(pairs):
                src, dst = (vmem, hbm) if out else (hbm, vmem)
                made.append(pltpu.make_async_copy(src, dst, sems.at[n * 3 + m]))
        return made

    @pl.when(i == 0)
    def _():
        copies = weight_copies(False, (ou_mine, ou_other), (d_mine, d_other))
        for c in copies:
            c.start()
        aout[...] = jnp.zeros_like(aout)
        aup[...] = jnp.zeros_like(aup)
        adown[...] = jnp.zeros_like(adown)
        vecg_ref[...] = jnp.zeros_like(vecg_ref)
        bupg_ref[...] = jnp.zeros_like(bupg_ref)
        for c in copies:
            c.wait()

    base = tok_ref[0].astype(f32) + row_ref[0]
    middle = base + dg(mix_ref[0], wout[...], 1, 0) + vec_ref[0:1, :]
    normed, inv = normalize(middle)
    hid[...] = (normed * vec_ref[1:2, :] + vec_ref[2:3, :]).astype(bf16)
    acc[...] = middle + vec_ref[3:4, :]
    gh2[...] = jnp.zeros_like(gh2)
    cot = cot_ref[0]

    def chunk(j, carry):
        c0 = pl.multiple_of(j * FC, FC)
        cols = pl.ds(c0, FC)
        up = dg(hid[...], wup[:, cols], 1, 0) + bup_ref[:, cols]
        ga = dg(cot, wdown[cols, :], 1, 1)
        active, slope = gelu_parts(up)
        active = active.astype(bf16)
        gu = (ga * slope).astype(bf16)
        acc[...] += dg(active, wdown[cols, :], 1, 0)
        adown[cols, :] += dg(active, cot, 0, 0)
        gh2[...] += dg(gu, wup[:, cols], 1, 1)
        aup[:, cols] += dg(hid[...], gu, 0, 0)
        bupg_ref[:, cols] += col_sum(gu.astype(f32))
        return carry

    lax.fori_loop(0, FF // FC, chunk, 0)
    out_ref[0] = acc[...].astype(bf16)
    grad_hidden = gh2[...]
    base = tok_ref[0].astype(f32) + row_ref[0]
    middle = base + dg(mix_ref[0], wout[...], 1, 0) + vec_ref[0:1, :]
    normed, inv = normalize(middle)
    cotf = cot.astype(f32)
    gmid = cotf + norm_back(grad_hidden, normed, inv, vec_ref[1:2, :])
    gmid_ref[0] = gmid
    branch = gmid.astype(bf16)
    vecg_ref[0:1, :] += col_sum(branch.astype(f32))
    vecg_ref[1:2, :] += col_sum(grad_hidden * normed)
    vecg_ref[2:3, :] += col_sum(grad_hidden)
    vecg_ref[3:4, :] += col_sum(cotf)
    aout[...] += dg(mix_ref[0], branch, 0, 0)
    gmix = dg(branch, wout[...], 1, 1).astype(bf16)
    gmix_ref[0] = gmix
    gmixT_ref[0] = gmix.T

    @pl.when(i == pl.num_programs(0) - 1)
    def _():
        wout[...] = aout[...].astype(bf16)
        wup[...] = aup[...].astype(bf16)
        wdown[...] = adown[...].astype(bf16)
        copies = weight_copies(True, (ou_keep, ou_send), (d_keep, d_send))
        for c in copies:
            c.start()
        for c in copies:
            c.wait()


def mlp_call(core, tokens, trow, cot, mixed, vec, bup, ou_mine, ou_other, d_mine, d_other):
    B, S, D = tokens.shape
    FF = bup.shape[1]
    per = S // RT
    row = pl.BlockSpec((1, RT, D), lambda i: (i // per, i % per, 0))
    col = pl.BlockSpec((1, D, RT), lambda i: (i // per, 0, i % per))
    whole = lambda shape: pl.BlockSpec(shape, lambda i: (0,) * len(shape))
    anyspec = pl.BlockSpec(memory_space=pl.ANY)
    sds = jax.ShapeDtypeStruct
    return pl.pallas_call(
        mlp_kernel,
        grid=(B * per,),
        in_specs=[
            pl.BlockSpec(memory_space=pltpu.SMEM),
            row,
            pl.BlockSpec((1, 1, D), lambda i: (i // per, 0, 0)),
            row,
            row,
            whole(vec.shape),
            whole(bup.shape),
        ] + [anyspec] * 4,
        out_specs=[row, row, row, col, whole((4, D)), whole((1, FF))] + [anyspec] * 4,
        out_shape=[
            sds((B, S, D), bf16),
            sds((B, S, D), f32),
            sds((B, S, D), bf16),
            sds((B, D, S), bf16),
            sds((4, D), f32),
            sds((1, FF), f32),
            sds(ou_mine.shape, bf16),
            sds(ou_mine.shape, bf16),
            sds(d_mine.shape, bf16),
            sds(d_mine.shape, bf16),
        ],
        scratch_shapes=[
            pltpu.VMEM((D, D), bf16),
            pltpu.VMEM((D, FF), bf16),
            pltpu.VMEM((FF, D), bf16),
            pltpu.VMEM((D, D), f32),
            pltpu.VMEM((D, FF), f32),
            pltpu.VMEM((FF, D), f32),
            pltpu.VMEM((RT, D), f32),
            pltpu.VMEM((RT, D), f32),
            pltpu.VMEM((RT, D), bf16),
            pltpu.SemaphoreType.DMA((6,)),
        ],
        compiler_params=params(),
        name="mlp_both",
    )(core, tokens, trow, cot, mixed, vec, bup, ou_mine, ou_other, d_mine, d_other)


def qkv_back_kernel(core_ref, tok_ref, row_ref, gmid_ref, dq_ref, dk_ref, dv_ref, vec_ref, mine_ref, other_ref,
                    gin_ref, rsum_ref, vecg_ref, keep_ref, send_ref, w_ref, aw_ref, sems):
    b = pl.program_id(0)
    i = pl.program_id(1)
    core = core_ref[0]
    D = tok_ref.shape[2]

    @pl.when((b == 0) & (i == 0))
    def _():
        copies = place_halves(mine_ref, other_ref, w_ref, core, sems)
        for c in copies:
            c.start()
        aw_ref[...] = jnp.zeros_like(aw_ref)
        vecg_ref[...] = jnp.zeros_like(vecg_ref)
        for c in copies:
            c.wait()

    @pl.when(i == 0)
    def _():
        rsum_ref[...] = jnp.zeros_like(rsum_ref)

    base = tok_ref[0].astype(f32) + row_ref[0]
    normed, inv = normalize(base)
    hidden = (normed * vec_ref[0:1, :] + vec_ref[1:2, :]).astype(bf16)
    grads = (dq_ref[0], dk_ref[0], dv_ref[0])
    grad_hidden = None
    for n, g in enumerate(grads):
        cols = slice(n * D, (n + 1) * D)
        part = dg(g, w_ref[:, cols], 1, 1)
        grad_hidden = part if grad_hidden is None else grad_hidden + part
        aw_ref[:, cols] += dg(hidden, g, 0, 0)
    gbase = gmid_ref[0] + norm_back(grad_hidden, normed, inv, vec_ref[0:1, :])
    gin_ref[0] = gbase.astype(bf16)
    rsum_ref[0] += col_sum(gbase)
    vecg_ref[0:1, :] += col_sum(grad_hidden * normed)
    vecg_ref[1:2, :] += col_sum(grad_hidden)
    vecg_ref[2:3, :] += col_sum(grads[0].astype(f32))
    vecg_ref[3:4, :] += col_sum(grads[2].astype(f32))

    @pl.when((b == pl.num_programs(0) - 1) & (i == pl.num_programs(1) - 1))
    def _():
        w_ref[...] = aw_ref[...].astype(bf16)
        half = keep_ref.shape[1]
        at = pl.multiple_of(core * half, 128)
        rest = pl.multiple_of((1 - core) * half, 128)
        copies = (
            pltpu.make_async_copy(w_ref.at[:, pl.ds(at, half)], keep_ref, sems.at[0]),
            pltpu.make_async_copy(w_ref.at[:, pl.ds(rest, half)], send_ref, sems.at[1]),
        )
        for c in copies:
            c.start()
        for c in copies:
            c.wait()


def qkv_back_call(core, tokens, trow, gmid, dq, dk, dv, vec, mine, other):
    B, S, D = tokens.shape
    row = pl.BlockSpec((1, RT, D), lambda b, i: (b, i, 0))
    seq = pl.BlockSpec((1, 1, D), lambda b, i: (b, 0, 0))
    anyspec = pl.BlockSpec(memory_space=pl.ANY)
    sds = jax.ShapeDtypeStruct
    return pl.pallas_call(
        qkv_back_kernel,
        grid=(B, S // RT),
        in_specs=[
            pl.BlockSpec(memory_space=pltpu.SMEM),
            row,
            seq,
            row,
            row,
            row,
            row,
            pl.BlockSpec(vec.shape, lambda b, i: (0, 0)),
            anyspec,
            anyspec,
        ],
        out_specs=[row, seq, pl.BlockSpec((4, D), lambda b, i: (0, 0)), anyspec, anyspec],
        out_shape=[
            sds((B, S, D), bf16),
            sds((B, 1, D), f32),
            sds((4, D), f32),
            sds(mine.shape, bf16),
            sds(mine.shape, bf16),
        ],
        scratch_shapes=[
            pltpu.VMEM((D, 3 * D), bf16),
            pltpu.VMEM((D, 3 * D), f32),
            pltpu.SemaphoreType.DMA((2,)),
        ],
        compiler_params=params(),
        name="norm_qkv_back",
    )(core, tokens, trow, gmid, dq, dk, dv, vec, mine, other)


def key_ranges(segment_ids):
    B, S = segment_ids.shape
    tiles = segment_ids.reshape(B, S // QT, QT)
    before = jnp.sum((segment_ids[:, None, :] < tiles[:, :, :1]).astype(jnp.int32), axis=-1)
    upto = jnp.sum((segment_ids[:, None, :] <= tiles[:, :, -1:]).astype(jnp.int32), axis=-1)
    return (before // KT).reshape(-1), ((upto + KT - 1) // KT).reshape(-1)


def own_slice(array, index, size, axis):
    return lax.dynamic_slice_in_dim(array, index * size, size, axis)


def swap(array, axis):
    return lax.ppermute(array, axis, [(0, 1), (1, 0)])


def all_sum(array, axis):
    size = lax.axis_size(axis)
    step = 1
    while step < size:
        array = array + lax.ppermute(array, axis, [(i, i ^ step) for i in range(size)])
        step *= 2
    return array


def on_device(
    tokens,
    cot,
    segment_ids,
    block_map,
    timesteps,
    step_table,
    ln1_gain,
    ln1_bias,
    w_query,
    b_query,
    w_key,
    w_value,
    b_value,
    w_out,
    b_out,
    ln2_gain,
    ln2_bias,
    w_up,
    b_up,
    w_down,
    b_down,
):
    B, S, D = tokens.shape
    every = ("xrep", "core", "shard")
    n = lax.axis_size("shard")
    me = lax.axis_index("shard")
    core = lax.axis_index("core")
    own = ln1_gain.shape[0]
    FF = b_up.shape[0] * n
    hd, hf = D // 2, FF // 2
    core1 = core.reshape(1).astype(jnp.int32)

    qkv_local = jnp.concatenate([w_query, w_key, w_value], axis=1)
    qkv_mine = lax.all_gather(own_slice(qkv_local, core, 3 * hd, 1), "shard", axis=0, tiled=True)
    qkv_other = swap(qkv_mine, "core")
    ou_local = jnp.concatenate([own_slice(w_out, core, hd, 1), own_slice(w_up, core, hf, 1)], axis=1)
    ou_mine = lax.all_gather(ou_local, "shard", axis=0, tiled=True)
    ou_other = swap(ou_mine, "core")
    d_mine = lax.all_gather(own_slice(w_down, core, hd, 1), "shard", axis=0, tiled=True)
    d_other = swap(d_mine, "core")

    small = (ln1_gain, ln1_bias, b_query, b_value, b_out, ln2_gain, ln2_bias, b_down)
    packed = lax.all_gather(jnp.concatenate(small + (b_up,)), "shard", axis=0).astype(f32)
    g1, s1, bq, bv, bo, g2, s2, bd = [packed[:, i * own : (i + 1) * own].reshape(1, D) for i in range(8)]
    bup = packed[:, 8 * own :].reshape(1, FF)
    vec1 = jnp.concatenate([g1, s1], axis=0)
    bias = jnp.concatenate([bq, jnp.zeros_like(bq), bv], axis=1)
    vec2 = jnp.concatenate([bo, g2, s2, bd], axis=0)

    steps = lax.all_gather(timesteps, every, axis=0, tiled=True)
    own_rows = step_table.shape[0]
    group = lax.all_gather(timesteps, "shard", axis=0, tiled=True)
    spots = me * own_rows + lax.broadcasted_iota(jnp.int32, (1, own_rows), 1)
    picker = (group[:, None] == spots).astype(bf16)
    found = jnp.dot(picker, step_table, preferred_element_type=f32)
    trow = lax.psum_scatter(found, "shard", scatter_dimension=0, tiled=True).reshape(B, 1, D)

    lo, hi = key_ranges(segment_ids)
    segk = jnp.broadcast_to(segment_ids[:, :, None], (B, S, 128))
    segq = segment_ids[:, None, :]

    q, k, v, qT, kT, vT = qkv_call(core1, tokens, trow, vec1, bias, qkv_mine, qkv_other)
    mixed, mixedT, lse = attn_fwd(lo, hi, q, k, vT, segk, segq)
    out, gmid, gmix, gmixT, vecg2, bupg, ou_keep, ou_send, d_keep, d_send = mlp_call(
        core1, tokens, trow, cot, mixed, vec2, bup, ou_mine, ou_other, d_mine, d_other
    )

    def reduce_half(keep, send):
        half = (keep.astype(f32) + swap(send, "core").astype(f32)).astype(bf16)
        return lax.psum_scatter(half, "shard", scatter_dimension=0, tiled=True)

    def finish(part):
        half = all_sum(part.astype(f32), "xrep").astype(bf16)
        other = swap(half, "core").astype(f32)
        half = half.astype(f32)
        return jnp.where(core == 0, half, other), jnp.where(core == 0, other, half)

    d_part = reduce_half(d_keep, d_send)
    ou_part = reduce_half(ou_keep, ou_send)
    dq, dk, dv = attn_bwd(lo, hi, q, qT, k, kT, v, gmix, gmixT, mixedT, lse, segk, segq)
    gin, rsum, vecg1, qkv_keep, qkv_send = qkv_back_call(
        core1, tokens, trow, gmid, dq, dk, dv, vec1, qkv_mine, qkv_other
    )
    qkv_part = reduce_half(qkv_keep, qkv_send)

    flat = jnp.concatenate([vecg1, vecg2], axis=0)
    flat = lax.psum(jnp.concatenate([flat.reshape(-1), bupg.reshape(-1)]), every)
    vg = [own_slice(flat[i * D : (i + 1) * D], me, own, 0) for i in range(8)]
    g_bup = own_slice(flat[8 * D :], me, FF // n, 0)
    sums = lax.all_gather(rsum.reshape(B, D), every, axis=0, tiled=True)
    owners = me * own_rows + lax.broadcasted_iota(jnp.int32, (own_rows, 1), 0)
    g_table = jnp.dot(
        (owners == steps[None, :]).astype(f32), sums, precision=lax.Precision.HIGHEST, preferred_element_type=f32
    )

    d_left, d_right = finish(d_part)
    ou_left, ou_right = finish(ou_part)
    q_left, q_right = finish(qkv_part)
    g_down = jnp.concatenate([d_left, d_right], axis=1)
    g_out = jnp.concatenate([ou_left[:, :hd], ou_right[:, :hd]], axis=1)
    g_up = jnp.concatenate([ou_left[:, hd:], ou_right[:, hd:]], axis=1)
    g_qkv = jnp.concatenate([q_left, q_right], axis=1)
    g_q, g_k, g_v = g_qkv[:, :D], g_qkv[:, D : 2 * D], g_qkv[:, 2 * D :]
    return (
        out, gin, g_table, vg[0], vg[1], g_q, vg[2], g_k, g_v, vg[3], g_out, vg[4], vg[5], vg[6], g_up, g_bup, g_down, vg[7],
    )


def solution(mesh):
    rep, shard = mesh.shape["rep"], mesh.shape["shard"]
    fine = Mesh(mesh.devices.reshape(rep // 2, 2, shard), ("xrep", "core", "shard"))
    seqs = ("xrep", "core", "shard")
    mat, vec = P("shard", None), P("shard")
    rows3, rows2 = P(seqs, None, None), P(seqs, None)
    weights = (mat, vec, vec, mat, vec, mat, mat, vec, mat, vec, vec, vec, mat, vec, mat, vec)
    return jax.shard_map(
        on_device,
        mesh=fine,
        in_specs=(rows3, rows3, rows2, rows3, P(seqs)) + weights,
        out_specs=(rows3, rows3) + weights,
        check_vma=False,
    )
```

time: 2030 us -> 730 us (0.36)
  waiting for transfers between devices: 1070 us -> 182 us
  matrix products: 553 us -> 1.3 us
  Pallas kernels: 0 us -> 266 us
  other arithmetic: 148 us -> 23.1 us
  blocking collectives: 168 us -> 224 us
  local copies, waits for them, and re-layouts: 63.1 us -> 15 us
    reduce_scatter x7 -> x3, waiting for transfers between devices: 689 us -> 34.7 us  [reduce_half(): return lax.psum_scatter(half, 'shard', scatter_dimension=0, tiled=True)]
    dot_general x62 -> x2, matrix products: 553 us -> 1.3 us  [the longest x1 1.1 us: on_device(): jnp.dot((owners == steps[None, :]).astype(f32), sums, precision=lax.Preci...]
    pallas_call x0 -> x5, Pallas kernels: none -> 266 us  [the longest x1 107 us: mlp_call(): pl.pallas_call(mlp_kernel, grid=(B * per,), in_specs=[pl.BlockSpec(memory...]
    all_gather x14 -> x3, waiting for transfers between devices: 330 us -> 118 us  [the longest x1 59.1 us: on_device(): ou_mine = lax.all_gather(ou_local, 'shard', axis=0, tiled=True)]
    while x2 -> x0, blocking collectives: 73.8 us -> none
    reduce_sum x16 -> x1, other arithmetic: 63.8 us -> 0.23 us  [key_ranges(): jnp.sum((segment_ids[:, None, :] <= tiles[:, :, -1:]).astype(jnp.int32),...]
    convert_element_type x24 -> x9, other arithmetic: 73.9 us -> 13.8 us  [the longest x3 9.55 us: reduce_half(): half = (keep.astype(f32) + swap(send, 'core').astype(f32)).astype(bf16)]
    unnamed x1 -> x3, blocking collectives: 35.6 us -> 82.4 us
  transfers between devices with their start and end apart: 22 -> 18, of which waited for: 18 -> 10; matrix products, arithmetic and copies ran while one was open for 14% -> 4% of each run, Pallas kernels for 0% -> 8%
where the time goes in v1:
time: 730 us; the launch traced here: 731 us
  Pallas kernels  266 us (36%)
  blocking collectives  224 us (31%)
  waiting for transfers between devices  182 us (25%)
  other arithmetic  23.1 us (3%)
  between operations  15.9 us (2%)
  local copies, waits for them, and re-layouts  15 us (2%)
    pallas_call x1, Pallas kernels, mlp_call(): pl.pallas_call(mlp_kernel, grid=(B * per,), in_specs=[pl.BlockSpec(memory...  107 us
    unnamed x3, blocking collectives  82.4 us
    pallas_call x1, Pallas kernels, attn_bwd(): pl.pallas_call(bwd_kernel, grid_spec=pltpu.PrefetchScalarGridSpec(num_sca...  71.5 us
    all_gather x1, blocking collectives, on_device(): sums = lax.all_gather(rsum.reshape(B, D), every, axis=0, tiled=True)  68.1 us
    all_gather x1, waiting for transfers between devices, on_device(): ou_mine = lax.all_gather(ou_local, 'shard', axis=0, tiled=True)  59.1 us
    all_gather x1, waiting for transfers between devices, on_device(): lax.all_gather(own_slice(w_down, core, hd, 1), 'shard', axis=0, tiled=True)  53.5 us
    pallas_call x1, Pallas kernels, attn_fwd(): pl.pallas_call(fwd_kernel, grid_spec=pltpu.PrefetchScalarGridSpec(num_sca...  46 us
    psum x1, blocking collectives, on_device(): lax.psum(jnp.concatenate([flat.reshape(-1), bupg.reshape(-1)]), every)  43 us
  transfers between devices with their start and end apart: 18, of which 10 were waited for; matrix products, arithmetic and copies ran while one was open for 4% of the time, Pallas kernels for 8%

profile of v1, /device:TPU:0, one launch (start us, length us, event | category | flops | bytes accessed | tf_op | source)
XLA Modules:
  0.0 731.1 jit_solution(14526844894734677651)
XLA Ops:
  11.1 1.8 fusion.1
  13.0 59.1 %all-gather.9.cloned.1.call-done.ou_mine = bf16[768,1920]{1,0:T(8,128)(2,1)} async-done(((bf16[96,1920]{1,0:T(8,128)(2,1)}), bf16[768,1920]{1,0:T(8,128)(2,1)}) %all-gather.9.cloned.1.call-update) | async-done | bytes 2949136 | tf_op jit(solution)/shard_map/all_gather | solution.py:539
  72.0 53.5 %all-gather.11.cloned.1.call-done.d_mine = bf16[3072,384]{1,0:T(8,128)(2,1)} async-done(((bf16[384,384]{1,0:T(8,128)(2,1)}), bf16[3072,384]{1,0:T(8,128)(2,1)}) %all-gather.11.cloned.1.call-update) | async-done | bytes 2359312 | tf_op jit(solution)/shard_map/all_gather | solution.py:541
  127.0 9.9 %all-reduce = s32[16]{0:T(128)S(1)} all-reduce(s32[16]{0:T(128)S(1)} %dynamic-update-slice), channel_id=1, replica_groups=mesh['xrep'=2,'core'=2,'shard'=8] {'shard'}, use_global_device_ids=true, to_apply=%add | all-reduce | flops 16 | bytes 128
  137.1 30.6 %all-gather.2 = bf16[8,1,1152]{2,1,0:T(2,128)(2,1)S(1)} all-gather(bf16[1,1,1152]{2,1,0:T(2,128)(2,1)S(1)} %reshape.124), channel_id=2, replica_groups=mesh['xrep'=2,'core'=2,'shard'=8] {'shard'}, dimensions={0}, use_global_device_ids=true | all-gather | bytes 20736 | tf_op jit(solution)/shard_map/all_gather | solution.py:545
  167.9 5.0 all-gather.7.cloned.1.call-done.mine_ref
  174.5 35.7 %all-reduce.2 = f32[16,768]{1,0:T(8,128)S(1)} all-reduce(f32[16,768]{1,0:T(8,128)S(1)} %fusion.9), channel_id=4, replica_groups=mesh['xrep'=2,'core'=2,'shard'=8] {'shard'}, use_global_device_ids=true, to_apply=%region_0.0.clone | all-reduce | flops 12288 | bytes 98304
  216.0 14.9 %norm_qkv.1 = (bf16[2,1024,768]{2,1,0:T(8,128)(2,1)}, bf16[2,1024,768]{2,1,0:T(8,128)(2,1)}, bf16[2,1024,768]{2,1,0:T(8,128)(2,1)}, bf16[2,768,1024]{2,1,0:T(8,1...) custom-call(s32[1]{0:T(128)} %bitcast.core_ref, bf16[2,1024,768]{2,1,0:T(8,128)(2,1)} %tok_ref.5, ...), custom_call_target="tpu_custom_call" | custom-call | tf_op jit(solution)/shard_map/norm_qkv/pallas_call | solution.py:95
  232.2 46.0 %attn_fwd.1 = (bf16[2,1024,768]{2,1,0:T(8,128)(2,1)}, f32[2,768,1024]{2,1,0:T(8,128)}, f32[2,12,1024]{2,1,0:T(8,128)}) custom-call(s32[8]{0:T(128)} %get-tuple-element.104.lo_ref, s32[8]{0:T(128)} %get-tuple-element.103.hi_ref, bf16[2,1024,768]{2,1,0:T(8,128)(2,1)} %get-tuple-element.45.q_ref, bf16[2,1024,768]{2,1,0:T(8,128)(2,1)} %get-tuple-element.46.k_ref, ...), custom_call_target="tpu_custom_call" | custom-call | tf_op jit(solution)/shard_map/attn_fwd/pallas_call | solution.py:160
  278.2 107.0 %mlp_both.1 = (bf16[2,1024,768]{2,1,0:T(8,128)(2,1)}, f32[2,1024,768]{2,1,0:T(8,128)}, bf16[2,1024,768]{2,1,0:T(8,128)(2,1)}, bf16[2,768,1024]{2,1,0:T(8,128)(2,...) custom-call(s32[1]{0:T(128)} %bitcast.core_ref, ...), custom_call_target="tpu_custom_call" | custom-call | tf_op jit(solution)/shard_map/mlp_both/pallas_call | solution.py:341
  385.2 71.5 %attn_bwd.1 = (bf16[2,1024,768]{2,1,0:T(8,128)(2,1)}, bf16[2,1024,768]{2,1,0:T(8,128)(2,1)}, bf16[2,1024,768]{2,1,0:T(8,128)(2,1)}) custom-call(s32[8]{0:T(128)} %get-tuple-element.104.lo_ref, s32[8]{0:T(128)} %get-tuple-element.103.hi_ref, bf16[2,1024,768]{2,1,0:T(8,128)(2,1)} %get-tuple-element.45.q_ref, bf16[2,768,1024]{2,1,0:T(8,128)(2,1)} %get-tuple-element.51.qT_ref, ...), custom_call_target="tpu_custom_call" | custom-call | tf_op jit(solution)/shard_map/attn_bwd/pallas_call | solution.py:225
  456.7 26.5 %norm_qkv_back.1 = (bf16[2,1024,768]{2,1,0:T(8,128)(2,1)}, f32[2,1,768]{2,1,0:T(1,128)}, f32[4,768]{1,0:T(4,128)}, bf16[768,1152]{1,0:T(8,128)(2,1)}, bf16[768,1152]{1,0:T(8,128)(2,1)}) custom-call(s32[1]{0:T(128)} %bitcast.core_ref, bf16[2,1024,768]{2,1,0:T(8,128)(2,1)} %tok_ref.5, f32[2,1,768]{2,1,0:T(1,128)} %reshape.102.row_ref, ...), custom_call_target="tpu_custom_call" | custom-call | tf_op jit(solution)/shard_map/norm_qkv_back/pallas_call | solution.py:444
  483.3 3.9 collective-permute-done.3
  487.2 3.3 add_convert_fusion.2
  490.8 4.4 collective-permute-done.9
  495.2 3.9 add_convert_fusion.1
  499.4 5.5 collective-permute-done.6
  504.8 2.3 add_convert_fusion
  507.5 36.9 %all-reduce.1 = s32[64]{0:T(128)S(1)} all-reduce(s32[64]{0:T(128)S(1)} %dynamic-update-slice.1), channel_id=1, replica_groups=mesh['xrep'=2,'core'=2,'shard'=8] {'xrep','core','shard'}, use_global_device_ids=true, to_apply=%add.1 | all-reduce | flops 64 | bytes 512
  544.4 8.9 %reduce-scatter.4.cloned.1.call-done = bf16[96,1152]{1,0:T(8,128)(2,1)} async-done(((bf16[768,1152]{1,0:T(8,128)(2,1)}), bf16[96,1152]{1,0:T(8,128)(2,1)}) %reduce-scatter.4.cloned.1.call-update) | async-done | bytes 221200 | tf_op jit(solution)/shard_map/reduce_scatter | solution.py:572
  555.5 43.0 %psum.7 = f32[9216]{0:T(1024)S(1)} all-reduce(f32[9216]{0:T(1024)S(1)} %pad_maximum_fusion.5), channel_id=1, replica_groups=mesh['xrep'=2,'core'=2,'shard'=8] {'xrep','core','shard'}, use_global_device_ids=true, to_apply=%region_3.4 | all-reduce | flops 9216 | bytes 73728 | tf_op jit(solution)/shard_map/psum | solution.py:589
  603.8 68.1 %all-gather.1 = f32[64,1,768]{2,1,0:T(1,128)S(1)} all-gather(f32[2,1,768]{2,1,0:T(1,128)S(1)} %copy-done.11), channel_id=3, replica_groups=mesh['xrep'=2,'core'=2,'shard'=8] {'xrep','core','shard'}, dimensions={0}, use_global_device_ids=true | all-gather | bytes 202752 | tf_op jit(solution)/shard_map/all_gather | solution.py:592
  675.7 25.8 %reduce-scatter.6.cloned.1.call-done = bf16[96,1920]{1,0:T(8,128)(2,1)} async-done(((bf16[768,1920]{1,0:T(8,128)(2,1)}), bf16[96,1920]{1,0:T(8,128)(2,1)}) %reduce-scatter.6.cloned.1.call-update) | async-done | bytes 368656 | tf_op jit(solution)/shard_map/reduce_scatter | solution.py:572
  705.3 15.0 %collective-permute-done.7 = f32[96,1920]{1,0:T(8,128)S(1)} collective-permute-done((f32[96,1920]{1,0:T(8,128)S(1)}, f32[96,1920]{1,0:T(8,128)S(1)}, u32[]{:S(2)}, u32[]{:S(2)}) %collective-permute-start.7) | collective-permute-done | bytes 737312 | tf_op jit(solution)/shard_map/ppermute | solution.py:497
  (156 shorter events, 32.9 us)
Async XLA Ops:
  7.2 129.7 %copy-start.14 = (bf16[96]{0:T(256)(128)(2,1)S(1)}, bf16[96]{0:T(256)(128)(2,1)}, u32[]{:S(2)}) copy-start(bf16[96]{0:T(256)(128)(2,1)} %param.26) | copy-start | bytes 580
  7.2 129.7 %copy-start.15 = (bf16[96]{0:T(256)(128)(2,1)S(1)}, bf16[96]{0:T(256)(128)(2,1)}, u32[]{:S(2)}) copy-start(bf16[96]{0:T(256)(128)(2,1)} %param.27) | copy-start | bytes 580
  7.3 129.7 %copy-start.16 = (bf16[96]{0:T(256)(128)(2,1)S(1)}, bf16[96]{0:T(256)(128)(2,1)}, u32[]{:S(2)}) copy-start(bf16[96]{0:T(256)(128)(2,1)} %param.29) | copy-start | bytes 580
  7.3 129.7 %copy-start.17 = (bf16[96]{0:T(256)(128)(2,1)S(1)}, bf16[96]{0:T(256)(128)(2,1)}, u32[]{:S(2)}) copy-start(bf16[96]{0:T(256)(128)(2,1)} %param.32) | copy-start | bytes 580
  7.3 160.4 %copy-start.6 = (bf16[128,768]{1,0:T(8,128)(2,1)S(1)}, bf16[128,768]{1,0:T(8,128)(2,1)}, u32[]{:S(2)}) copy-start(bf16[128,768]{1,0:T(8,128)(2,1)} %param.25) | copy-start | bytes 589828
  7.3 165.6 %copy-start.7 = (s32[2,1024]{1,0:T(2,128)S(1)}, s32[2,1024]{1,0:T(2,128)}, u32[]{:S(2)}) copy-start(s32[2,1024]{1,0:T(2,128)} %param.23) | copy-start | bytes 24580
  7.3 64.7 %all-gather.9.cloned.1.call-start = ((), (), s32[]{:S(2)}) async-start(), calls=%async_computation.4 | async-start | bytes 3317760 | tf_op jit(solution)/shard_map/all_gather | solution.py:539
  9.3 116.2 %all-gather.11.cloned.1.call-start = ((), (), s32[]{:S(2)}) async-start(), calls=%async_computation.5 | async-start | bytes 2654208 | tf_op jit(solution)/shard_map/all_gather | solution.py:541
  11.1 161.8 %all-gather.7.cloned.1.call-start = ((), (), s32[]{:S(2)}) async-start(), calls=%async_computation.3 | async-start | bytes 1990656 | tf_op jit(solution)/shard_map/all_gather | solution.py:536
  12.9 540.4 %reduce-scatter.4.cloned.1.call-start = ((), (), s32[]{:S(2)}) async-start(), calls=%async_computation.6 | async-start | bytes 1990656 | tf_op jit(solution)/shard_map/reduce_scatter | solution.py:572
  72.0 206.1 %collective-permute-start.1 = (bf16[768,1920]{1,0:T(8,128)(2,1)}, bf16[768,1920]{1,0:T(8,128)(2,1)}, u32[]{:S(2)}, u32[]{:S(2)}) collective-permute-start(bf16[768,1920]{1,0:T(8,128)(2,1)} %all-gather.9.cloned.1.call-done.ou_mine), channel_id=1, source_target_pairs={{0,8},{8,0},{1,9},{9,1},{2,10},{10,2},{3,11},{11,3},{4,12},{12,4},... | collective-permute-start | bytes 8847368 | tf_op jit(solution)/shard_map/ppermute | solution.py:490
  125.5 152.6 %collective-permute-start.2 = (bf16[3072,384]{1,0:T(8,128)(2,1)}, bf16[3072,384]{1,0:T(8,128)(2,1)}, u32[]{:S(2)}, u32[]{:S(2)}) collective-permute-start(bf16[3072,384]{1,0:T(8,128)(2,1)} %all-gather.11.cloned.1.call-done.d_mine), channel_id=1, source_target_pairs={{0,8},{8,0},{1,9},{9,1},{2,10},{10,2},{3,11},{11,3},{4,12},{12,4},... | collective-permute-start | bytes 7077896 | tf_op jit(solution)/shard_map/ppermute | solution.py:490
  172.9 41.9 %collective-permute-start = (bf16[768,1152]{1,0:T(8,128)(2,1)}, bf16[768,1152]{1,0:T(8,128)(2,1)S(1)}, u32[]{:S(2)}, u32[]{:S(2)}) collective-permute-start(bf16[768,1152]{1,0:T(8,128)(2,1)} %all-gather.7.cloned.1.call-done.mine_ref), channel_id=1, source_target_pairs={{0,8},{8,0},{1,9},{9,1},{2,10},{10,2},{3,11},{11,3},{4,12},{12,4},... | collective-permute-start | bytes 5308424 | tf_op jit(solution)/shard_map/ppermute | solution.py:490
  483.2 4.0 collective-permute-start.3
  490.5 183.5 %reduce-scatter.8.cloned.1.call-start = ((), (), s32[]{:S(2)}) async-start(), calls=%async_computation.8 | async-start | bytes 2654208 | tf_op jit(solution)/shard_map/reduce_scatter | solution.py:572
  490.6 4.6 collective-permute-start.9
  499.1 202.4 %reduce-scatter.6.cloned.1.call-start = ((), (), s32[]{:S(2)}) async-start(), calls=%async_computation.7 | async-start | bytes 3317760 | tf_op jit(solution)/shard_map/reduce_scatter | solution.py:572
  499.2 5.7 collective-permute-start.6
  554.3 117.6 %collective-permute-start.4 = (f32[96,1152]{1,0:T(8,128)S(1)}, f32[96,1152]{1,0:T(8,128)S(1)}, u32[]{:S(2)}, u32[]{:S(2)}) collective-permute-start(f32[96,1152]{1,0:T(8,128)S(1)} %convert_element_type.80), channel_id=1, source_target_pairs={{0,16},{16,0},{1,17},{17,1},{2,18},{18,2},{3,19},{19,3},{4,20},{20... | collective-permute-start | bytes 1327112 | tf_op jit(solution)/shard_map/ppermute | solution.py:497
  672.9 31.3 %collective-permute-start.5 = (bf16[96,1152]{1,0:T(8,128)(2,1)S(1)}, bf16[96,1152]{1,0:T(8,128)(2,1)S(1)}, u32[]{:S(2)}, u32[]{:S(2)}) collective-permute-start(bf16[96,1152]{1,0:T(8,128)(2,1)S(1)} %add_convert_fusion.5), channel_id=1, source_target_pairs={{0,8},{8,0},{1,9},{9,1},{2,10},{10,2},{3,11},{11,3},{4,12},{12,4},... | collective-permute-start | bytes 663560 | tf_op jit(solution)/shard_map/ppermute | solution.py:490
  675.2 30.0 %collective-permute-start.10 = (f32[384,384]{1,0:T(8,128)S(1)}, f32[384,384]{1,0:T(8,128)S(1)}, u32[]{:S(2)}, u32[]{:S(2)}) collective-permute-start(f32[384,384]{1,0:T(8,128)S(1)} %convert_element_type.94), channel_id=1, source_target_pairs={{0,16},{16,0},{1,17},{17,1},{2,18},{18,2},{3,19},{19,3},{4,20},{20... | collective-permute-start | bytes 1769480 | tf_op jit(solution)/shard_map/ppermute | solution.py:497
  702.6 17.6 %collective-permute-start.7 = (f32[96,1920]{1,0:T(8,128)S(1)}, f32[96,1920]{1,0:T(8,128)S(1)}, u32[]{:S(2)}, u32[]{:S(2)}) collective-permute-start(f32[96,1920]{1,0:T(8,128)S(1)} %convert_element_type.87), channel_id=1, source_target_pairs={{0,16},{16,0},{1,17},{17,1},{2,18},{18,2},{3,19},{19,3},{4,20},{20... | collective-permute-start | bytes 2211848 | tf_op jit(solution)/shard_map/ppermute | solution.py:497
  705.2 15.2 %collective-permute-start.11 = (bf16[384,384]{1,0:T(8,128)(2,1)S(1)}, bf16[384,384]{1,0:T(8,128)(2,1)S(1)}, u32[]{:S(2)}, u32[]{:S(2)}) collective-permute-start(bf16[384,384]{1,0:T(8,128)(2,1)S(1)} %add_convert_fusion.4), channel_id=1, source_target_pairs={{0,8},{8,0},{1,9},{9,1},{2,10},{10,2},{3,11},{11,3},{4,12},{12,4},... | collective-permute-start | bytes 884744 | tf_op jit(solution)/shard_map/ppermute | solution.py:490
  720.4 1.8 collective-permute-start.8
  (18 other events, 1172.9 us)
Sparse Core Ops, SparseCore 0:
  10.9 61.0 all-gather.8
  74.8 50.6 all-gather.10
  128.3 44.5 all-gather.6
  490.7 62.6 reduce-scatter.3
  557.1 68.0 reduce-scatter.7
  629.0 72.5 reduce-scatter.5

commit v2 on v1

--- a/solution.py
+++ b/solution.py
@@ -1,3 +1,5 @@
+import functools
+
 import jax
 import jax.numpy as jnp
 from jax import lax
@@ -108,6 +110,7 @@
         out_shape=[jax.ShapeDtypeStruct((B, S, D), bf16)] * 3 + [jax.ShapeDtypeStruct((B, D, S), bf16)] * 3,
         scratch_shapes=[pltpu.VMEM((D, 3 * D), bf16), pltpu.SemaphoreType.DMA((2,))],
         compiler_params=params(),
+        cost_estimate=pl.CostEstimate(flops=6 * B * S * D * D, bytes_accessed=30 * 10**6, transcendentals=0),
         name="norm_qkv",
     )(core, tokens, trow, vec, bias, mine, other)
 
@@ -170,9 +173,10 @@
         scratch_shapes=[pltpu.VMEM((D,QT),f32),pltpu.VMEM((HEADS,QT),f32),pltpu.VMEM((HEADS,QT),f32)]),
       out_shape=[jax.ShapeDtypeStruct((B,S,D),bf16),jax.ShapeDtypeStruct((B,D,S),f32),jax.ShapeDtypeStruct((B,HEADS,S),f32)],
       compiler_params=params(),
+      cost_estimate=pl.CostEstimate(flops=16 * B * S * S * D, bytes_accessed=30 * 10**6, transcendentals=0),
       name="attn_fwd")(lo,hi,q,k,vT,segk,segq)
 
-def bwd_kernel(lo_ref, hi_ref, q_ref, qT_ref, k_ref, kT_ref, v_ref, do_ref, doT_ref, oT_ref, lse_ref, segk_ref, segq_ref,
+def bwd_kernel(lo_ref, hi_ref, q_ref, qT_ref, k_ref, kT_ref, v_ref, do_ref, doT_ref, oT_ref, lse_ref, segk_ref, segq_ref, after_ref,
                dq_ref, dk_ref, dv_ref, dqT, dkT, dvT, dlt):
     b=pl.program_id(0); i=pl.program_id(1)
     nq=pl.num_programs(1)
@@ -216,7 +220,7 @@
         dk_ref[0]=dkT[...].astype(bf16).T
         dv_ref[0]=dvT[...].astype(bf16).T
 
-def attn_bwd(lo,hi,q,qT,k,kT,v,do,doT,oT,lse,segk,segq):
+def attn_bwd(lo,hi,q,qT,k,kT,v,do,doT,oT,lse,segk,segq,after):
     B,S,D=q.shape; nq=S//QT
     row=pl.BlockSpec((1,QT,D),lambda b,i,*_:(b,i,0))
     col=pl.BlockSpec((1,D,QT),lambda b,i,*_:(b,0,i))
@@ -227,44 +231,110 @@
         in_specs=[row,col,full,fullT,full,row,col,col,
                   pl.BlockSpec((1,HEADS,QT),lambda b,i,*_:(b,0,i)),
                   pl.BlockSpec((1,S,128),lambda b,i,*_:(b,0,0)),
-                  pl.BlockSpec((1,1,QT),lambda b,i,*_:(b,0,i))],
+                  pl.BlockSpec((1,1,QT),lambda b,i,*_:(b,0,i)),
+                  pl.BlockSpec(memory_space=pl.ANY)],
         out_specs=[row,full,full],
         scratch_shapes=[pltpu.VMEM((D,QT),f32),pltpu.VMEM((D,S),f32),pltpu.VMEM((D,S),f32),pltpu.VMEM((HEADS,QT),f32)]),
       out_shape=[jax.ShapeDtypeStruct((B,S,D),bf16)]*3,
       compiler_params=params(),
-      name="attn_bwd")(lo,hi,q,qT,k,kT,v,do,doT,oT,lse,segk,segq)
-
-
-def mlp_kernel(core_ref, tok_ref, row_ref, cot_ref, mix_ref, vec_ref, bup_ref,
-               ou_mine, ou_other, d_mine, d_other,
-               out_ref, gmid_ref, gmix_ref, gmixT_ref, vecg_ref, bupg_ref,
-               ou_keep, ou_send, d_keep, d_send,
-               wout, wup, wdown, aout, aup, adown, acc, gh2, hid, sems):
+      cost_estimate=pl.CostEstimate(flops=32 * B * S * S * D, bytes_accessed=40 * 10**6, transcendentals=0),
+      name="attn_bwd")(lo,hi,q,qT,k,kT,v,do,doT,oT,lse,segk,segq,after)
+
+
+def mlp_chunks(hid, cot, wup, wdown, bup_ref, acc, gh2, aup, adown, bupg_ref):
+    def chunk(j, carry):
+        c0 = pl.multiple_of(j * FC, FC)
+        cols = pl.ds(c0, FC)
+        up = dg(hid, wup[:, cols], 1, 0) + bup_ref[:, cols]
+        ga = dg(cot, wdown[cols, :], 1, 1)
+        active, slope = gelu_parts(up)
+        active = active.astype(bf16)
+        gu = (ga * slope).astype(bf16)
+        acc[0] += dg(active, wdown[cols, :], 1, 0)
+        adown[cols, :] += dg(active, cot, 0, 0)
+        gh2[0] += dg(gu, wup[:, cols], 1, 1)
+        aup[:, cols] += dg(hid, gu, 0, 0)
+        bupg_ref[:, cols] += col_sum(gu.astype(f32))
+        return carry
+
+    lax.fori_loop(0, wup.shape[1] // FC, chunk, 0)
+
+
+def mlp_load(first, w_ref, extra, wup, wdown, sems):
+    D, H = wup.shape
+    at = D if first else 0
+    pairs = [(w_ref.at[:, pl.ds(at, H)], wup)]
+    pairs += [(w_ref.at[:, pl.ds(at + H + j * D, D)], wdown.at[pl.ds(j * D, D), :]) for j in range(H // D)]
+    pairs += extra
+    return [pltpu.make_async_copy(src, dst, sems.at[n]) for n, (src, dst) in enumerate(pairs)]
+
+
+def mlp_store(core, wup, wdown, keep_ref, send_ref, extra, sems):
+    D, H = wup.shape
+
+    def run(up_to, down_to):
+        pairs = [(wup, up_to.at[:, pl.ds(0, H)])]
+        pairs += [(wdown.at[pl.ds(j * D, D), :], down_to.at[:, pl.ds(j * D, D)]) for j in range(H // D)]
+        pairs += extra
+        made = [pltpu.make_async_copy(src, dst, sems.at[n]) for n, (src, dst) in enumerate(pairs)]
+        for c in made:
+            c.start()
+        for c in made:
+            c.wait()
+
+    @pl.when(core == 0)
+    def _():
+        run(keep_ref, send_ref)
+
+    @pl.when(core != 0)
+    def _():
+        run(send_ref, keep_ref)
+
+
+def mlp_first_kernel(core_ref, tok_ref, row_ref, cot_ref, mix_ref, vec_ref, bup_ref, w_ref,
+                     acc_ref, gh2_ref, mid_ref, hid_ref, bupg_ref, keep_ref, send_ref,
+                     wout, wup, wdown, aup, adown, sems):
+    i = pl.program_id(0)
+    D = tok_ref.shape[2]
+
+    @pl.when(i == 0)
+    def _():
+        copies = mlp_load(True, w_ref, [(w_ref.at[:, pl.ds(0, D)], wout)], wup, wdown, sems)
+        for c in copies:
+            c.start()
+        aup[...] = jnp.zeros_like(aup)
+        adown[...] = jnp.zeros_like(adown)
+        bupg_ref[...] = jnp.zeros_like(bupg_ref)
+        for c in copies:
+            c.wait()
+
+    base = tok_ref[0].astype(f32) + row_ref[0]
+    middle = base + dg(mix_ref[0], wout[...], 1, 0) + vec_ref[0:1, :]
+    mid_ref[0] = middle
+    normed, unused = normalize(middle)
+    hid_ref[0] = (normed * vec_ref[1:2, :] + vec_ref[2:3, :]).astype(bf16)
+    acc_ref[0] = middle + vec_ref[3:4, :]
+    gh2_ref[...] = jnp.zeros_like(gh2_ref)
+    mlp_chunks(hid_ref[0], cot_ref[0], wup, wdown, bup_ref, acc_ref, gh2_ref, aup, adown, bupg_ref)
+
+    @pl.when(i == pl.num_programs(0) - 1)
+    def _():
+        wup[...] = aup[...].astype(bf16)
+        wdown[...] = adown[...].astype(bf16)
+        mlp_store(core_ref[0], wup, wdown, keep_ref, send_ref, [], sems)
+
+
+def mlp_second_kernel(core_ref, accin_ref, gh2in_ref, mid_ref, hid_ref, cot_ref, mix_ref, vec_ref, bup_ref, wfirst_ref, w_ref,
+                      out_ref, gmid_ref, gmix_ref, gmixT_ref, vecg_ref, bupg_ref, keep_ref, send_ref,
+                      wout, wup, wdown, aout, aup, adown, acc, gh2, sems):
     i = pl.program_id(0)
     core = core_ref[0]
-    D = tok_ref.shape[2]
-    FF = wup.shape[1]
-    hd, hf = D // 2, FF // 2
-    at = (core, 1 - core)
-
-    def weight_copies(out, refs_ou, refs_d):
-        made = []
-        for n in range(2):
-            cd = pl.multiple_of(at[n] * hd, 128)
-            cf = pl.multiple_of(at[n] * hf, 128)
-            pairs = (
-                (refs_ou[n].at[:, pl.ds(0, hd)], wout.at[:, pl.ds(cd, hd)]),
-                (refs_ou[n].at[:, pl.ds(hd, hf)], wup.at[:, pl.ds(cf, hf)]),
-                (refs_d[n], wdown.at[:, pl.ds(cd, hd)]),
-            )
-            for m, (hbm, vmem) in enumerate(pairs):
-                src, dst = (vmem, hbm) if out else (hbm, vmem)
-                made.append(pltpu.make_async_copy(src, dst, sems.at[n * 3 + m]))
-        return made
+    D, H = wup.shape
+    hd = D // 2
 
     @pl.when(i == 0)
     def _():
-        copies = weight_copies(False, (ou_mine, ou_other), (d_mine, d_other))
+        copies = mlp_load(False, w_ref, [(wfirst_ref.at[:, pl.ds(0, D)], wout)], wup, wdown, sems)
         for c in copies:
             c.start()
         aout[...] = jnp.zeros_like(aout)
@@ -275,35 +345,13 @@
         for c in copies:
             c.wait()
 
-    base = tok_ref[0].astype(f32) + row_ref[0]
-    middle = base + dg(mix_ref[0], wout[...], 1, 0) + vec_ref[0:1, :]
-    normed, inv = normalize(middle)
-    hid[...] = (normed * vec_ref[1:2, :] + vec_ref[2:3, :]).astype(bf16)
-    acc[...] = middle + vec_ref[3:4, :]
-    gh2[...] = jnp.zeros_like(gh2)
+    acc[...] = accin_ref[...]
+    gh2[...] = gh2in_ref[...]
     cot = cot_ref[0]
-
-    def chunk(j, carry):
-        c0 = pl.multiple_of(j * FC, FC)
-        cols = pl.ds(c0, FC)
-        up = dg(hid[...], wup[:, cols], 1, 0) + bup_ref[:, cols]
-        ga = dg(cot, wdown[cols, :], 1, 1)
-        active, slope = gelu_parts(up)
-        active = active.astype(bf16)
-        gu = (ga * slope).astype(bf16)
-        acc[...] += dg(active, wdown[cols, :], 1, 0)
-        adown[cols, :] += dg(active, cot, 0, 0)
-        gh2[...] += dg(gu, wup[:, cols], 1, 1)
-        aup[:, cols] += dg(hid[...], gu, 0, 0)
-        bupg_ref[:, cols] += col_sum(gu.astype(f32))
-        return carry
-
-    lax.fori_loop(0, FF // FC, chunk, 0)
-    out_ref[0] = acc[...].astype(bf16)
-    grad_hidden = gh2[...]
-    base = tok_ref[0].astype(f32) + row_ref[0]
-    middle = base + dg(mix_ref[0], wout[...], 1, 0) + vec_ref[0:1, :]
-    normed, inv = normalize(middle)
+    mlp_chunks(hid_ref[0], cot, wup, wdown, bup_ref, acc, gh2, aup, adown, bupg_ref)
+    out_ref[0] = acc[0].astype(bf16)
+    grad_hidden = gh2[0]
+    normed, inv = normalize(mid_ref[0])
     cotf = cot.astype(f32)
     gmid = cotf + norm_back(grad_hidden, normed, inv, vec_ref[1:2, :])
     gmid_ref[0] = gmid
@@ -322,62 +370,89 @@
         wout[...] = aout[...].astype(bf16)
         wup[...] = aup[...].astype(bf16)
         wdown[...] = adown[...].astype(bf16)
-        copies = weight_copies(True, (ou_keep, ou_send), (d_keep, d_send))
-        for c in copies:
-            c.start()
-        for c in copies:
-            c.wait()
-
-
-def mlp_call(core, tokens, trow, cot, mixed, vec, bup, ou_mine, ou_other, d_mine, d_other):
+        at = pl.multiple_of(core * hd, 128)
+        rest = pl.multiple_of((1 - core) * hd, 128)
+        extra = [
+            (wout.at[:, pl.ds(at, hd)], keep_ref.at[:, pl.ds(H, hd)]),
+            (wout.at[:, pl.ds(rest, hd)], send_ref.at[:, pl.ds(H, hd)]),
+        ]
+        mlp_store(core, wup, wdown, keep_ref, send_ref, extra, sems)
+
+
+def mlp_specs(tokens):
     B, S, D = tokens.shape
-    FF = bup.shape[1]
     per = S // RT
     row = pl.BlockSpec((1, RT, D), lambda i: (i // per, i % per, 0))
     col = pl.BlockSpec((1, D, RT), lambda i: (i // per, 0, i % per))
-    whole = lambda shape: pl.BlockSpec(shape, lambda i: (0,) * len(shape))
-    anyspec = pl.BlockSpec(memory_space=pl.ANY)
+    one = pl.BlockSpec((1, 1, D), lambda i: (i // per, 0, 0))
+    return row, col, one, pl.BlockSpec(memory_space=pl.ANY), pl.BlockSpec(memory_space=pltpu.SMEM)
+
+
+def whole(shape):
+    return pl.BlockSpec(shape, lambda i: (0,) * len(shape))
+
+
+def mlp_first(core, tokens, trow, cot, mixed, vec, bup, weights):
+    B, S, D = tokens.shape
+    H = bup.shape[1]
+    row, col, one, anyspec, smem = mlp_specs(tokens)
     sds = jax.ShapeDtypeStruct
     return pl.pallas_call(
-        mlp_kernel,
-        grid=(B * per,),
-        in_specs=[
-            pl.BlockSpec(memory_space=pltpu.SMEM),
-            row,
-            pl.BlockSpec((1, 1, D), lambda i: (i // per, 0, 0)),
-            row,
-            row,
-            whole(vec.shape),
-            whole(bup.shape),
-        ] + [anyspec] * 4,
-        out_specs=[row, row, row, col, whole((4, D)), whole((1, FF))] + [anyspec] * 4,
+        mlp_first_kernel,
+        grid=(B * S // RT,),
+        in_specs=[smem, row, one, row, row, whole(vec.shape), whole(bup.shape), anyspec],
+        out_specs=[row, row, row, row, whole((1, H)), anyspec, anyspec],
+        out_shape=[sds((B, S, D), f32)] * 3 + [sds((B, S, D), bf16), sds((1, H), f32)] + [sds((D, H), bf16)] * 2,
+        scratch_shapes=[
+            pltpu.VMEM((D, D), bf16),
+            pltpu.VMEM((D, H), bf16),
+            pltpu.VMEM((H, D), bf16),
+            pltpu.VMEM((D, H), f32),
+            pltpu.VMEM((H, D), f32),
+            pltpu.SemaphoreType.DMA((2 + H // D,)),
+        ],
+        compiler_params=params(),
+        cost_estimate=pl.CostEstimate(flops=13 * B * S * D * H, bytes_accessed=60 * 10**6, transcendentals=0),
+        name="mlp_first",
+    )(core, tokens, trow, cot, mixed, vec, bup, weights)
+
+
+def mlp_second(core, acc, gh2, mid, hid, cot, mixed, vec, bup, wfirst, weights):
+    B, S, D = cot.shape
+    H = bup.shape[1]
+    row, col, one, anyspec, smem = mlp_specs(cot)
+    sds = jax.ShapeDtypeStruct
+    wide = sds((D, H + D // 2), bf16)
+    return pl.pallas_call(
+        mlp_second_kernel,
+        grid=(B * S // RT,),
+        in_specs=[smem] + [row] * 6 + [whole(vec.shape), whole(bup.shape), anyspec, anyspec],
+        out_specs=[row, row, row, col, whole((4, D)), whole((1, H)), anyspec, anyspec],
         out_shape=[
             sds((B, S, D), bf16),
             sds((B, S, D), f32),
             sds((B, S, D), bf16),
             sds((B, D, S), bf16),
             sds((4, D), f32),
-            sds((1, FF), f32),
-            sds(ou_mine.shape, bf16),
-            sds(ou_mine.shape, bf16),
-            sds(d_mine.shape, bf16),
-            sds(d_mine.shape, bf16),
+            sds((1, H), f32),
+            wide,
+            wide,
         ],
         scratch_shapes=[
             pltpu.VMEM((D, D), bf16),
-            pltpu.VMEM((D, FF), bf16),
-            pltpu.VMEM((FF, D), bf16),
+            pltpu.VMEM((D, H), bf16),
+            pltpu.VMEM((H, D), bf16),
             pltpu.VMEM((D, D), f32),
-            pltpu.VMEM((D, FF), f32),
-            pltpu.VMEM((FF, D), f32),
-            pltpu.VMEM((RT, D), f32),
-            pltpu.VMEM((RT, D), f32),
-            pltpu.VMEM((RT, D), bf16),
-            pltpu.SemaphoreType.DMA((6,)),
+            pltpu.VMEM((D, H), f32),
+            pltpu.VMEM((H, D), f32),
+            pltpu.VMEM((1, RT, D), f32),
+            pltpu.VMEM((1, RT, D), f32),
+            pltpu.SemaphoreType.DMA((3 + H // D,)),
         ],
         compiler_params=params(),
-        name="mlp_both",
-    )(core, tokens, trow, cot, mixed, vec, bup, ou_mine, ou_other, d_mine, d_other)
+        cost_estimate=pl.CostEstimate(flops=14 * B * S * D * H, bytes_accessed=60 * 10**6, transcendentals=0),
+        name="mlp_second",
+    )(core, acc, gh2, mid, hid, cot, mixed, vec, bup, wfirst, weights)
 
 
 def qkv_back_kernel(core_ref, tok_ref, row_ref, gmid_ref, dq_ref, dk_ref, dv_ref, vec_ref, mine_ref, other_ref,
@@ -470,6 +545,7 @@
             pltpu.SemaphoreType.DMA((2,)),
         ],
         compiler_params=params(),
+        cost_estimate=pl.CostEstimate(flops=12 * B * S * D * D, bytes_accessed=40 * 10**6, transcendentals=0),
         name="norm_qkv_back",
     )(core, tokens, trow, gmid, dq, dk, dv, vec, mine, other)
 
@@ -494,9 +570,54 @@
     size = lax.axis_size(axis)
     step = 1
     while step < size:
-        array = array + lax.ppermute(array, axis, [(i, i ^ step) for i in range(size)])
+        came = lax.ppermute(array, axis, [(i, i ^ step) for i in range(size)])
+        array = (array.astype(f32) + came.astype(f32)).astype(array.dtype)
         step *= 2
     return array
+
+
+def gather_small(array, axis):
+    size, me = lax.axis_size(axis), lax.axis_index(axis)
+    step = 1
+    while step < size:
+        came = lax.ppermute(array, axis, [(i, i ^ step) for i in range(size)])
+        low = (me & step) == 0
+        array = jnp.concatenate([jnp.where(low, array, came), jnp.where(low, came, array)], axis=0)
+        step *= 2
+    return array
+
+
+def scatter_small(array, axis):
+    size, me = lax.axis_size(axis), lax.axis_index(axis)
+    step = size // 2
+    while step >= 1:
+        half = array.shape[0] // 2
+        low = (me & step) == 0
+        keep = jnp.where(low, array[:half], array[half:])
+        send = jnp.where(low, array[half:], array[:half])
+        array = keep + lax.ppermute(send, axis, [(i, i ^ step) for i in range(size)])
+        step //= 2
+    return array
+
+
+EXTRA = 8
+
+
+def split_rows(values, width):
+    high = lax.reduce_precision(values, 8, 7)
+    parts = jnp.concatenate([high, values - high], axis=-2).astype(bf16)
+    pad = [(0, 0)] * (parts.ndim - 1) + [(0, width - parts.shape[-1])]
+    return jnp.pad(parts, pad)
+
+
+def exchange_reduce(array, extra, axis):
+    size = lax.axis_size(axis)
+    rows, width = array.shape[0] // size, array.shape[1]
+    extra = jnp.pad(extra, ((0, 0), (0, EXTRA - extra.shape[1]), (0, 0)))
+    sent = jnp.concatenate([array.reshape(size, rows, width), extra], axis=1)
+    came = lax.all_to_all(sent.reshape(size * (rows + EXTRA), width), axis, 0, 0, tiled=True)
+    came = came.reshape(size, rows + EXTRA, width)
+    return jnp.sum(came[:, :rows].astype(f32), axis=0).astype(bf16), came[:, rows:].astype(f32)
 
 
 def on_device(
@@ -523,39 +644,46 @@
     b_down,
 ):
     B, S, D = tokens.shape
-    every = ("xrep", "core", "shard")
     n = lax.axis_size("shard")
     me = lax.axis_index("shard")
     core = lax.axis_index("core")
     own = ln1_gain.shape[0]
     FF = b_up.shape[0] * n
-    hd, hf = D // 2, FF // 2
+    hd = D // 2
     core1 = core.reshape(1).astype(jnp.int32)
 
-    qkv_local = jnp.concatenate([w_query, w_key, w_value], axis=1)
-    qkv_mine = lax.all_gather(own_slice(qkv_local, core, 3 * hd, 1), "shard", axis=0, tiled=True)
-    qkv_other = swap(qkv_mine, "core")
-    ou_local = jnp.concatenate([own_slice(w_out, core, hd, 1), own_slice(w_up, core, hf, 1)], axis=1)
-    ou_mine = lax.all_gather(ou_local, "shard", axis=0, tiled=True)
-    ou_other = swap(ou_mine, "core")
-    d_mine = lax.all_gather(own_slice(w_down, core, hd, 1), "shard", axis=0, tiled=True)
-    d_other = swap(d_mine, "core")
-
-    small = (ln1_gain, ln1_bias, b_query, b_value, b_out, ln2_gain, ln2_bias, b_down)
-    packed = lax.all_gather(jnp.concatenate(small + (b_up,)), "shard", axis=0).astype(f32)
+    H = FF // 2
+    J = FF // D
+    thin = own // 2
+    qkv_local = own_slice(jnp.concatenate([w_query, w_key, w_value], axis=1), core, 3 * hd, 1)
+    qkv_mine = lax.all_gather(qkv_local, "shard", axis=0, tiled=True)
+    up_core = own_slice(w_up, core, thin, 0).reshape(thin, n, 2, J, thin)
+    up_core = up_core.transpose(0, 3, 1, 2, 4).reshape(thin, FF)
+    out_core = own_slice(w_out, core, thin, 0)
+    down_core = own_slice(w_down, core, J * thin, 0)
+    down_core = [down_core[j * thin : (j + 1) * thin] for j in range(J)]
+    local_a = jnp.concatenate([out_core, up_core[:, :H]] + down_core[: J // 2], axis=1)
+    local_b = jnp.concatenate([up_core[:, H:]] + down_core[J // 2 :], axis=1)
+
+    small = (ln1_gain, ln1_bias, b_query, b_value, b_out, ln2_gain, ln2_bias, b_down, b_up)
+    small = jnp.concatenate([v.astype(f32) for v in small] + [timesteps.astype(f32)])
+    packed = gather_small(small[None], "shard")
     g1, s1, bq, bv, bo, g2, s2, bd = [packed[:, i * own : (i + 1) * own].reshape(1, D) for i in range(8)]
-    bup = packed[:, 8 * own :].reshape(1, FF)
+    width = 8 * own + FF // n
+    bup = packed[:, 8 * own : width].reshape(n, 2, J, thin).transpose(2, 0, 1, 3).reshape(1, FF)
+    group = packed[:, width:].reshape(n * B, 1).astype(jnp.int32)
     vec1 = jnp.concatenate([g1, s1], axis=0)
     bias = jnp.concatenate([bq, jnp.zeros_like(bq), bv], axis=1)
     vec2 = jnp.concatenate([bo, g2, s2, bd], axis=0)
 
-    steps = lax.all_gather(timesteps, every, axis=0, tiled=True)
     own_rows = step_table.shape[0]
-    group = lax.all_gather(timesteps, "shard", axis=0, tiled=True)
     spots = me * own_rows + lax.broadcasted_iota(jnp.int32, (1, own_rows), 1)
-    picker = (group[:, None] == spots).astype(bf16)
-    found = jnp.dot(picker, step_table, preferred_element_type=f32)
-    trow = lax.psum_scatter(found, "shard", scatter_dimension=0, tiled=True).reshape(B, 1, D)
+    found = jnp.dot((group == spots).astype(bf16), step_table, preferred_element_type=f32)
+    trow = scatter_small(found, "shard").reshape(B, 1, D)
+    qkv_mine, trow, vec1 = lax.optimization_barrier((qkv_mine, trow, vec1))
+    qkv_other = swap(qkv_mine, "core")
+    local_a, qkv_mine = lax.optimization_barrier((local_a, qkv_mine))
+    w_a = lax.all_gather(local_a, ("shard", "core"), axis=0, tiled=True)
 
     lo, hi = key_ranges(segment_ids)
     segk = jnp.broadcast_to(segment_ids[:, :, None], (B, S, 128))
@@ -563,44 +691,68 @@
 
     q, k, v, qT, kT, vT = qkv_call(core1, tokens, trow, vec1, bias, qkv_mine, qkv_other)
     mixed, mixedT, lse = attn_fwd(lo, hi, q, k, vT, segk, segq)
-    out, gmid, gmix, gmixT, vecg2, bupg, ou_keep, ou_send, d_keep, d_send = mlp_call(
-        core1, tokens, trow, cot, mixed, vec2, bup, ou_mine, ou_other, d_mine, d_other
-    )
-
-    def reduce_half(keep, send):
-        half = (keep.astype(f32) + swap(send, "core").astype(f32)).astype(bf16)
-        return lax.psum_scatter(half, "shard", scatter_dimension=0, tiled=True)
+    local_b, w_a, mixed = lax.optimization_barrier((local_b, w_a, mixed))
+    w_b = lax.all_gather(local_b, ("shard", "core"), axis=0, tiled=True)
+    def core_sum(keep, send):
+        return (keep.astype(f32) + swap(send, "core").astype(f32)).astype(bf16)
 
     def finish(part):
-        half = all_sum(part.astype(f32), "xrep").astype(bf16)
+        half = all_sum(part, "xrep").astype(bf16)
         other = swap(half, "core").astype(f32)
         half = half.astype(f32)
         return jnp.where(core == 0, half, other), jnp.where(core == 0, other, half)
 
-    d_part = reduce_half(d_keep, d_send)
-    ou_part = reduce_half(ou_keep, ou_send)
-    dq, dk, dv = attn_bwd(lo, hi, q, qT, k, kT, v, gmix, gmixT, mixedT, lse, segk, segq)
+    acc, gh2, mid, hid, bupg_a, keep, send = mlp_first(core1, tokens, trow, cot, mixed, vec2, bup[:, :H], w_a)
+    half_a = core_sum(keep, send)
+    part_a = lax.all_to_all(half_a, "shard", 0, 0, tiled=True).reshape(n, own, H)
+    part_a = jnp.sum(part_a.astype(f32), axis=0).astype(bf16)
+    acc, half_a = lax.optimization_barrier((acc, half_a))
+    out, gmid, gmix, gmixT, vecg2, bupg_b, keep, send = mlp_second(
+        core1, acc, gh2, mid, hid, cot, mixed, vec2, bup[:, H:], w_a, w_b
+    )
+    half_b = core_sum(keep, send)
+    half_b, part_a = lax.optimization_barrier((half_b, part_a))
+    bupg = jnp.concatenate([bupg_a, bupg_b], axis=1)
+    bupg = bupg.reshape(J, n, 2, thin).transpose(1, 2, 0, 3).reshape(n, FF // n)
+    vectors = jnp.concatenate([vecg2[i].reshape(n, own) for i in range(4)] + [bupg], axis=1)
+    part_b, came_b = exchange_reduce(half_b, split_rows(vectors[:, None], half_b.shape[1]), "shard")
+    dq, dk, dv = attn_bwd(lo, hi, q, qT, k, kT, v, gmix, gmixT, mixedT, lse, segk, segq, half_b)
     gin, rsum, vecg1, qkv_keep, qkv_send = qkv_back_call(
         core1, tokens, trow, gmid, dq, dk, dv, vec1, qkv_mine, qkv_other
     )
-    qkv_part = reduce_half(qkv_keep, qkv_send)
-
-    flat = jnp.concatenate([vecg1, vecg2], axis=0)
-    flat = lax.psum(jnp.concatenate([flat.reshape(-1), bupg.reshape(-1)]), every)
-    vg = [own_slice(flat[i * D : (i + 1) * D], me, own, 0) for i in range(8)]
-    g_bup = own_slice(flat[8 * D :], me, FF // n, 0)
-    sums = lax.all_gather(rsum.reshape(B, D), every, axis=0, tiled=True)
-    owners = me * own_rows + lax.broadcasted_iota(jnp.int32, (own_rows, 1), 0)
-    g_table = jnp.dot(
-        (owners == steps[None, :]).astype(f32), sums, precision=lax.Precision.HIGHEST, preferred_element_type=f32
-    )
-
-    d_left, d_right = finish(d_part)
-    ou_left, ou_right = finish(ou_part)
+    qkv_half = core_sum(qkv_keep, qkv_send)
+    qkv_half, part_b, came_b = lax.optimization_barrier((qkv_half, part_b, came_b))
+    vectors = jnp.concatenate([vecg1[i].reshape(n, own) for i in range(4)], axis=1)
+    wide = qkv_half.shape[1]
+    digits = jnp.stack([timesteps // 32, timesteps % 32], axis=1).astype(f32)
+    table_rows = jnp.concatenate([rsum.reshape(B, D), digits], axis=1)
+    table_rows = jnp.broadcast_to(split_rows(table_rows, wide)[None], (n, 2 * B, wide))
+    extra = jnp.concatenate([split_rows(vectors[:, None], wide), table_rows], axis=1)
+    qkv_part, came_q = exchange_reduce(qkv_half, extra, "shard")
+
+    vg_b = jnp.sum(came_b[:, :2], axis=(0, 1))[: 4 * own + FF // n]
+    vg_q = jnp.sum(came_q[:, :2], axis=(0, 1))[: 4 * own]
+    vg = all_sum(all_sum(jnp.concatenate([vg_q, vg_b])[None], "core"), "xrep").reshape(-1)
+    g_bup = vg[8 * own :]
+    vg = [vg[i * own : (i + 1) * own] for i in range(8)]
+    sums = (came_q[:, 2 : 2 + B] + came_q[:, 2 + B : 2 + 2 * B])[:, :, : D + 2].reshape(n * B, D + 2)
+    for axis in ("core", "xrep"):
+        sums = gather_small(sums, axis)
+    own_rows = step_table.shape[0]
+    rows = me * own_rows + lax.broadcasted_iota(jnp.int32, (own_rows, 1), 0)
+    steps = 32 * sums[:, D] + sums[:, D + 1]
+    match = (rows == steps.astype(jnp.int32)[None, :]).astype(f32)
+    g_table = jnp.dot(match, sums[:, :D], precision=lax.Precision.HIGHEST, preferred_element_type=f32)
+
+    a_up, a_down = finish(part_a)
+    b_up_, b_down_ = finish(part_b)
+    g_up = jnp.concatenate([a_up, b_up_[:, :H]], axis=1)
+    g_up = g_up.reshape(own, J, n, 2, thin).transpose(0, 2, 3, 1, 4).reshape(own, FF)
+    blocks = jnp.concatenate([a_down, b_down_[:, :H]], axis=1).reshape(2, thin, J, D)
+    g_down = blocks.transpose(0, 2, 1, 3).reshape(FF // n, D)
+    g_out = jnp.concatenate([b_up_[:, H:], b_down_[:, H:]], axis=1)
+    qkv_part, g_up, g_down, g_out = lax.optimization_barrier((qkv_part, g_up, g_down, g_out))
     q_left, q_right = finish(qkv_part)
-    g_down = jnp.concatenate([d_left, d_right], axis=1)
-    g_out = jnp.concatenate([ou_left[:, :hd], ou_right[:, :hd]], axis=1)
-    g_up = jnp.concatenate([ou_left[:, hd:], ou_right[:, hd:]], axis=1)
     g_qkv = jnp.concatenate([q_left, q_right], axis=1)
     g_q, g_k, g_v = g_qkv[:, :D], g_qkv[:, D : 2 * D], g_qkv[:, 2 * D :]
     return (

time: 730 us -> 472 us (0.65)
  blocking collectives: 224 us -> 0 us
  waiting for transfers between devices: 182 us -> 79.2 us
  starting transfers between devices: 4.19 us -> 55 us
  local copies, waits for them, and re-layouts: 15 us -> 32.5 us
  other arithmetic: 23.1 us -> 33.2 us
  Pallas kernels: 266 us -> 256 us
    all_gather x2 -> x0, blocking collectives: 98.7 us -> none  [the longest x1 68.1 us: on_device(): sums = lax.all_gather(rsum.reshape(B, D), every, axis=0, tiled=True)]
    all_gather x3, waiting for transfers between devices: 118 us -> 20.2 us  [the longest x1 20.1 us: on_device(): qkv_mine = lax.all_gather(qkv_local, 'shard', axis=0, tiled=True)]
    unnamed x3 -> x0, blocking collectives: 82.4 us -> none
    psum x1 -> x0, blocking collectives: 43 us -> none  [on_device(): lax.psum(jnp.concatenate([flat.reshape(-1), bupg.reshape(-1)]), every)]
    all_to_all x0 -> x3, starting transfers between devices: none -> 37.9 us  [the longest x2 25.3 us: exchange_reduce(): lax.all_to_all(sent.reshape(size * (rows + EXTRA), width), axis, 0, 0, ti...]
    reduce_scatter x3 -> x0, waiting for transfers between devices: 34.7 us -> none  [reduce_half(): return lax.psum_scatter(half, 'shard', scatter_dimension=0, tiled=True)]
    ppermute x3 -> x13, waiting for transfers between devices: 15 us -> 35.8 us  [the longest x5 19.1 us: all_sum(): came = lax.ppermute(array, axis, [(i, i ^ step) for i in range(size)])]
    all_to_all x0 -> x3, waiting for transfers between devices: none -> 13.8 us  [the longest x2 13.8 us: exchange_reduce(): lax.all_to_all(sent.reshape(size * (rows + EXTRA), width), axis, 0, 0, ti...]
  transfers between devices with their start and end apart: 18 -> 26, of which waited for: 10 -> 17; matrix products, arithmetic and copies ran while one was open for 4% -> 10% of each run, Pallas kernels for 8% -> 54%
where the time goes in v2:
time: 472 us
  Pallas kernels  256 us (54%)
  waiting for transfers between devices  79.2 us (17%)
  starting transfers between devices  55 us (12%)
  other arithmetic  33.2 us (7%)
  local copies, waits for them, and re-layouts  32.5 us (7%)
  between operations  14.8 us (3%)
    pallas_call x1, Pallas kernels, attn_bwd(): pl.pallas_call(bwd_kernel, grid_spec=pltpu.PrefetchScalarGridSpec(num_sca...  62.2 us
    pallas_call x1, Pallas kernels, mlp_second(): pl.pallas_call(mlp_second_kernel, grid=(B * S // RT,), in_specs=[smem] +...  60.4 us
    pallas_call x1, Pallas kernels, mlp_first(): pl.pallas_call(mlp_first_kernel, grid=(B * S // RT,), in_specs=[smem, row...  52.1 us
    pallas_call x1, Pallas kernels, attn_fwd(): pl.pallas_call(fwd_kernel, grid_spec=pltpu.PrefetchScalarGridSpec(num_sca...  39.9 us
    pallas_call x1, Pallas kernels, qkv_back_call(): pl.pallas_call(qkv_back_kernel, grid=(B, S // RT), in_specs=[pl.BlockSpec...  26.5 us
    all_to_all x2, starting transfers between devices, exchange_reduce(): lax.all_to_all(sent.reshape(size * (rows + EXTRA), width), axis, 0, 0, ti...  25.3 us
    all_gather x1, waiting for transfers between devices, on_device(): qkv_mine = lax.all_gather(qkv_local, 'shard', axis=0, tiled=True)  20.1 us
    ppermute x5, waiting for transfers between devices, all_sum(): came = lax.ppermute(array, axis, [(i, i ^ step) for i in range(size)])  19.1 us
  transfers between devices with their start and end apart: 26, of which 17 were waited for; matrix products, arithmetic and copies ran while one was open for 10% of the time, Pallas kernels for 54%

profile of v2, /device:TPU:0, one launch (start us, length us, event | category | flops | bytes accessed | tf_op | source)
XLA Modules:
  0.0 471.9 jit_solution(13105086900525752224)
XLA Ops:
  8.5 6.1 %concatenate.137 = f32[1154]{0:T(1024)S(1)} concatenate(bf16[96]{0:T(256)(128)(2,1)} %param.26, bf16[96]{0:T(256)(128)(2,1)} %param.27, bf16[96]{0:T(256)(128)(2,1)} %param.29, bf16[96]{0:T(256)(128)(2,1)} %param.32, bf16[96]{0:T(256)(128)(2,1)} %param.34, bf16[96]{0:T(256)(128)(2,1)} %param.35, bf16[96]{0:T(256)(128)(2,1)} %param.36, bf16[96]{0:T(256)(128)(2,1)} %param.40, ...), dimensions={0} | concatenate | bytes 6928 | tf_op jit(solution)/shard_map/concatenate | solution.py:669
  14.7 3.0 collective-permute-start
  31.7 2.9 collective-permute-start.3
  42.5 3.0 collective-permute-done.5
  46.1 20.1 %all-gather.4.cloned.1.call-done.mine_ref = bf16[768,1152]{1,0:T(8,128)(2,1)} async-done(((bf16[96,1152]{1,0:T(8,128)(2,1)}), bf16[768,1152]{1,0:T(8,128)(2,1)}) %all-gather.4.cloned.1.call-update) | async-done | bytes 1769488 | tf_op jit(solution)/shard_map/all_gather | solution.py:659
  72.1 14.9 %norm_qkv.1 = (bf16[2,1024,768]{2,1,0:T(8,128)(2,1)}, bf16[2,1024,768]{2,1,0:T(8,128)(2,1)}, bf16[2,1024,768]{2,1,0:T(8,128)(2,1)}, bf16[2,768,1024]{2,1,0:T(8,1...) custom-call(s32[1]{0:T(128)} %bitcast.core_ref, bf16[2,1024,768]{2,1,0:T(8,128)(2,1)} %tok_ref.5, ...), custom_call_target="tpu_custom_call" | custom-call | flops 7247757312 | bytes 30000000 | tf_op jit(solution)/shard_map/norm_qkv/pallas_call | solution.py:97
  88.3 39.9 %attn_fwd.1 = (bf16[2,1024,768]{2,1,0:T(8,128)(2,1)}, f32[2,768,1024]{2,1,0:T(8,128)}, f32[2,12,1024]{2,1,0:T(8,128)}) custom-call(s32[8]{0:T(128)} %get-tuple-element.294.lo_ref, s32[8]{0:T(128)} %get-tuple-element.293.hi_ref, bf16[2,1024,768]{2,1,0:T(8,128)(2,1)} %get-tuple-element.73.q_ref, bf16[2,1024,768]{2,1,0:T(8,128)(2,1)} %get-tuple-element.74.k_ref, ...), custom_call_target="tpu_custom_call" | custom-call | flops 25769803776 | bytes 30000000 | tf_op jit(solution)/shard_map/attn_fwd/pallas_call | solution.py:163
  130.0 52.1 %mlp_first.1 = (f32[2,1024,768]{2,1,0:T(8,128)}, f32[2,1024,768]{2,1,0:T(8,128)}, f32[2,1024,768]{2,1,0:T(8,128)}, bf16[2,1024,768]{2,1,0:T(8,128)(2,1)}, f32[1,...) custom-call(s32[1]{0:T(128)} %bitcast.core_ref, bf16[2,1024,768]{2,1,0:T(8,128)(2,1)} %tok_ref.5, ...), custom_call_target="tpu_custom_call" | custom-call | flops 31406948352 | bytes 60000000 | tf_op jit(solution)/shard_map/mlp_first/pallas_call | solution.py:400
  182.4 4.8 %collective-permute-done.7 = bf16[768,1536]{1,0:T(8,128)(2,1)S(1)} collective-permute-done((bf16[768,1536]{1,0:T(8,128)(2,1)}, bf16[768,1536]{1,0:T(8,128)(2,1)S(1)}, u32[]{:S(2)}, u32[]{:S(2)}) %collective-permute-start.7) | collective-permute-done | bytes 2359328 | tf_op jit(solution)/shard_map/ppermute | solution.py:566
  187.2 3.8 add_convert_fusion.1
  191.0 12.6 %all-to-all-start = ((bf16[8,96,1536]{2,1,0:T(8,128)(2,1)}), bf16[8,96,1536]{2,1,0:T(8,128)(2,1)S(1)}, u32[]{:S(2)}, u32[]{:S(2)}) async-start(bf16[8,96,1536]{2,1,0:T(8,128)(2,1)} %bitcast.5), calls=%async_computation | async-start | bytes 4718592 | tf_op jit(solution)/shard_map/all_to_all | solution.py:707
  203.7 60.4 %mlp_second.1 = (bf16[2,1024,768]{2,1,0:T(8,128)(2,1)}, f32[2,1024,768]{2,1,0:T(8,128)}, bf16[2,1024,768]{2,1,0:T(8,128)(2,1)}, bf16[2,768,1024]{2,1,0:T(8,128)(...) custom-call(s32[1]{0:T(128)} %bitcast.core_ref, ...), custom_call_target="tpu_custom_call" | custom-call | flops 33822867456 | bytes 60000000 | tf_op jit(solution)/shard_map/mlp_second/pallas_call | solution.py:426
  267.0 2.8 collective-permute-done.8
  269.8 3.4 add_convert_fusion.after_ref
  276.8 6.2 %all-to-all-start.1 = ((bf16[8,104,1920]{2,1,0:T(8,128)(2,1)}), bf16[8,104,1920]{2,1,0:T(8,128)(2,1)S(1)}, u32[]{:S(2)}, u32[]{:S(2)}) async-start(bf16[8,104,1920]{2,1,0:T(8,128)(2,1)} %fusion.2), calls=%async_computation.1 | async-start | bytes 6389760 | tf_op jit(solution)/shard_map/all_to_all | solution.py:618
  283.0 62.2 %attn_bwd.1 = (bf16[2,1024,768]{2,1,0:T(8,128)(2,1)}, bf16[2,1024,768]{2,1,0:T(8,128)(2,1)}, bf16[2,1024,768]{2,1,0:T(8,128)(2,1)}) custom-call(s32[8]{0:T(128)} %get-tuple-element.294.lo_ref, s32[8]{0:T(128)} %get-tuple-element.293.hi_ref, bf16[2,1024,768]{2,1,0:T(8,128)(2,1)} %get-tuple-element.73.q_ref, bf16[2,768,1024]{2,1,0:T(8,128)(2,1)} %get-tuple-element.89.qT_ref, ...), custom_call_target="tpu_custom_call" | custom-call | flops 51539607552 | bytes 40000000 | tf_op jit(solution)/shard_map/attn_bwd/pallas_call | solution.py:229
  345.3 26.5 %norm_qkv_back.1 = (bf16[2,1024,768]{2,1,0:T(8,128)(2,1)}, f32[2,1,768]{2,1,0:T(1,128)}, f32[4,768]{1,0:T(4,128)}, bf16[768,1152]{1,0:T(8,128)(2,1)}, bf16[768,1152]{1,0:T(8,128)(2,1)}) custom-call(s32[1]{0:T(128)} %bitcast.core_ref, bf16[2,1024,768]{2,1,0:T(8,128)(2,1)} %tok_ref.5, f32[2,1,768]{2,1,0:T(1,128)} %reshape.501.row_ref, ...), custom_call_target="tpu_custom_call" | custom-call | flops 14495514624 | bytes 40000000 | tf_op jit(solution)/shard_map/norm_qkv_back/pallas_call | solution.py:519
  375.8 3.6 add_convert_fusion.2
  382.9 19.1 %all-to-all-start.2 = ((bf16[8,104,1152]{2,1,0:T(8,128)(2,1)}), bf16[8,104,1152]{2,1,0:T(8,128)(2,1)S(1)}, u32[]{:S(2)}, u32[]{:S(2)}) async-start(bf16[8,104,1152]{2,1,0:T(8,128)(2,1)} %fusion.3), calls=%async_computation.2 | async-start | bytes 3833856 | tf_op jit(solution)/shard_map/all_to_all | solution.py:618
  404.0 7.9 %collective-permute-done.14 = bf16[96,1536]{1,0:T(8,128)(2,1)S(1)} collective-permute-done((bf16[96,1536]{1,0:T(8,128)(2,1)S(1)}, bf16[96,1536]{1,0:T(8,128)(2,1)S(1)}, u32[]{:S(2)}, u32[]{:S(2)}) %collective-permute-start.14) | collective-permute-done | bytes 294944 | tf_op jit(solution)/shard_map/ppermute | solution.py:573
  412.1 6.6 %collective-permute-done.16 = bf16[96,1920]{1,0:T(8,128)(2,1)S(1)} collective-permute-done((bf16[96,1920]{1,0:T(8,128)(2,1)S(1)}, bf16[96,1920]{1,0:T(8,128)(2,1)S(1)}, u32[]{:S(2)}, u32[]{:S(2)}) %collective-permute-start.16) | collective-permute-done | bytes 368672 | tf_op jit(solution)/shard_map/ppermute | solution.py:573
  432.8 13.8 %all-to-all-done.2 = bf16[8,104,1152]{2,1,0:T(8,128)(2,1)S(1)} async-done(((bf16[8,104,1152]{2,1,0:T(8,128)(2,1)}), bf16[8,104,1152]{2,1,0:T(8,128)(2,1)S(1)}, u32[]{:S(2)}, u32[]{:S(2)}) %all-to-all-start.2) | async-done | bytes 1916960 | tf_op jit(solution)/shard_map/all_to_all | solution.py:618
  451.5 4.4 collective-permute-done.13
  457.5 3.9 collective-permute-done.11
  (210 shorter events, 73.0 us)
Async XLA Ops:
  7.2 59.1 %all-gather.4.cloned.1.call-start = ((), (), s32[]{:S(2)}) async-start(), calls=%async_computation.3 | async-start | bytes 1990656 | tf_op jit(solution)/shard_map/all_gather | solution.py:659
  14.7 8.0 %collective-permute-start = (f32[1,1154]{1,0:T(1,128)S(1)}, f32[1,1154]{1,0:T(1,128)S(1)}, u32[]{:S(2)}, u32[]{:S(2)}) collective-permute-start(f32[1,1154]{1,0:T(1,128)S(1)} %broadcast_in_dim.12), channel_id=1, source_target_pairs={{0,1},{1,0},{2,3},{3,2},{4,5},{5,4},{6,7},{7,6},{8,9},{9,8},{10,11... | collective-permute-start | bytes 13856 | tf_op jit(solution)/shard_map/ppermute | solution.py:583
  19.5 108.6 %all-gather.6.cloned.1.call-start = ((), (), s32[]{:S(2)}) async-start(), calls=%async_computation.4 | async-start | bytes 6266880 | tf_op jit(solution)/shard_map/all_gather | solution.py:686
  22.7 3.7 collective-permute-start.1
  26.5 4.9 %collective-permute-start.2 = (f32[4,1154]{1,0:T(4,128)S(1)}, f32[4,1154]{1,0:T(4,128)S(1)}, u32[]{:S(2)}, u32[]{:S(2)}) collective-permute-start(f32[4,1154]{1,0:T(4,128)S(1)} %pad_maximum_fusion.10), channel_id=1, source_target_pairs={{0,4},{1,5},{2,6},{3,7},{4,0},{5,1},{6,2},{7,3},{8,12},{9,13},{10,... | collective-permute-start | bytes 55400 | tf_op jit(solution)/shard_map/ppermute | solution.py:583
  31.7 6.3 %collective-permute-start.3 = (f32[8,768]{1,0:T(8,128)S(1)}, f32[8,768]{1,0:T(8,128)S(1)}, u32[]{:S(2)}, u32[]{:S(2)}) collective-permute-start(f32[8,768]{1,0:T(8,128)S(1)} %slice_select_fusion), channel_id=1, source_target_pairs={{0,4},{1,5},{2,6},{3,7},{4,0},{5,1},{6,2},{7,3},{8,12},{9,13},{10,... | collective-permute-start | bytes 73736 | tf_op jit(solution)/shard_map/ppermute | solution.py:598
  38.0 3.8 collective-permute-start.4
  41.8 3.7 collective-permute-start.5
  66.3 137.3 %all-gather.8.cloned.1.call-start = ((), (), s32[]{:S(2)}) async-start(), calls=%async_computation.5 | async-start | bytes 5013504 | tf_op jit(solution)/shard_map/all_gather | solution.py:695
  66.9 4.0 collective-permute-start.6
  182.1 5.1 %collective-permute-start.7 = (bf16[768,1536]{1,0:T(8,128)(2,1)}, bf16[768,1536]{1,0:T(8,128)(2,1)S(1)}, u32[]{:S(2)}, u32[]{:S(2)}) collective-permute-start(bf16[768,1536]{1,0:T(8,128)(2,1)} %get-tuple-element.81), channel_id=1, source_target_pairs={{0,8},{8,0},{1,9},{9,1},{2,10},{10,2},{3,11},{11,3},{4,12},{12,4},... | collective-permute-start | bytes 7077896 | tf_op jit(solution)/shard_map/ppermute | solution.py:566
  191.0 73.3 %all-to-all-start = ((bf16[8,96,1536]{2,1,0:T(8,128)(2,1)}), bf16[8,96,1536]{2,1,0:T(8,128)(2,1)S(1)}, u32[]{:S(2)}, u32[]{:S(2)}) async-start(bf16[8,96,1536]{2,1,0:T(8,128)(2,1)} %bitcast.5), calls=%async_computation | async-start | bytes 4718592 | tf_op jit(solution)/shard_map/all_to_all | solution.py:707
  264.0 5.8 %collective-permute-start.8 = (bf16[768,1920]{1,0:T(8,128)(2,1)}, bf16[768,1920]{1,0:T(8,128)(2,1)}, u32[]{:S(2)}, u32[]{:S(2)}) collective-permute-start(bf16[768,1920]{1,0:T(8,128)(2,1)} %get-tuple-element.97), channel_id=1, source_target_pairs={{0,8},{8,0},{1,9},{9,1},{2,10},{10,2},{3,11},{11,3},{4,12},{12,4},... | collective-permute-start | bytes 8847368 | tf_op jit(solution)/shard_map/ppermute | solution.py:566
  276.8 102.7 %all-to-all-start.1 = ((bf16[8,104,1920]{2,1,0:T(8,128)(2,1)}), bf16[8,104,1920]{2,1,0:T(8,128)(2,1)S(1)}, u32[]{:S(2)}, u32[]{:S(2)}) async-start(bf16[8,104,1920]{2,1,0:T(8,128)(2,1)} %fusion.2), calls=%async_computation.1 | async-start | bytes 6389760 | tf_op jit(solution)/shard_map/all_to_all | solution.py:618
  371.7 4.1 collective-permute-start.9
  382.9 63.7 %all-to-all-start.2 = ((bf16[8,104,1152]{2,1,0:T(8,128)(2,1)}), bf16[8,104,1152]{2,1,0:T(8,128)(2,1)S(1)}, u32[]{:S(2)}, u32[]{:S(2)}) async-start(bf16[8,104,1152]{2,1,0:T(8,128)(2,1)} %fusion.3), calls=%async_computation.2 | async-start | bytes 3833856 | tf_op jit(solution)/shard_map/all_to_all | solution.py:618
  401.9 10.0 %collective-permute-start.14 = (bf16[96,1536]{1,0:T(8,128)(2,1)S(1)}, bf16[96,1536]{1,0:T(8,128)(2,1)S(1)}, u32[]{:S(2)}, u32[]{:S(2)}) collective-permute-start(bf16[96,1536]{1,0:T(8,128)(2,1)S(1)} %reduce_sum.77), channel_id=1, source_target_pairs={{0,16},{16,0},{1,17},{17,1},{2,18},{18,2},{3,19},{19,3},{4,20},{20... | collective-permute-start | bytes 884744 | tf_op jit(solution)/shard_map/ppermute | solution.py:573
  402.0 16.6 %collective-permute-start.16 = (bf16[96,1920]{1,0:T(8,128)(2,1)S(1)}, bf16[96,1920]{1,0:T(8,128)(2,1)S(1)}, u32[]{:S(2)}, u32[]{:S(2)}) collective-permute-start(bf16[96,1920]{1,0:T(8,128)(2,1)S(1)} %copy-done.4), channel_id=1, source_target_pairs={{0,16},{16,0},{1,17},{17,1},{2,18},{18,2},{3,19},{19,3},{4,20},{20... | collective-permute-start | bytes 1105928 | tf_op jit(solution)/shard_map/ppermute | solution.py:573
  412.0 6.9 %collective-permute-start.15 = (bf16[96,1536]{1,0:T(8,128)(2,1)S(1)}, bf16[96,1536]{1,0:T(8,128)(2,1)S(1)}, u32[]{:S(2)}, u32[]{:S(2)}) collective-permute-start(bf16[96,1536]{1,0:T(8,128)(2,1)S(1)} %add_convert_fusion.4), channel_id=1, source_target_pairs={{0,8},{8,0},{1,9},{9,1},{2,10},{10,2},{3,11},{11,3},{4,12},{12,4},... | collective-permute-start | bytes 884744 | tf_op jit(solution)/shard_map/ppermute | solution.py:566
  418.8 2.1 collective-permute-start.17
  447.7 13.9 %collective-permute-start.18 = (bf16[96,1152]{1,0:T(8,128)(2,1)}, bf16[96,1152]{1,0:T(8,128)(2,1)S(1)}, u32[]{:S(2)}, u32[]{:S(2)}) collective-permute-start(bf16[96,1152]{1,0:T(8,128)(2,1)} %slice_reduce_fusion.1), channel_id=1, source_target_pairs={{0,16},{16,0},{1,17},{17,1},{2,18},{18,2},{3,19},{19,3},{4,20},{20... | collective-permute-start | bytes 663560 | tf_op jit(solution)/shard_map/ppermute | solution.py:573
  448.0 7.9 %collective-permute-start.13 = (f32[1,1152]{1,0:T(1,128)S(1)}, f32[1,1152]{1,0:T(1,128)S(1)}, u32[]{:S(2)}, u32[]{:S(2)}) collective-permute-start(f32[1,1152]{1,0:T(1,128)S(1)} %reshape_add_fusion), channel_id=1, source_target_pairs={{0,16},{16,0},{1,17},{17,1},{2,18},{18,2},{3,19},{19,3},{4,20},{20... | collective-permute-start | bytes 13832 | tf_op jit(solution)/shard_map/ppermute | solution.py:573
  451.4 5.1 %collective-permute-start.10 = (f32[16,770]{1,0:T(8,128)S(1)}, f32[16,770]{1,0:T(8,128)S(1)}, u32[]{:S(2)}, u32[]{:S(2)}) collective-permute-start(f32[16,770]{1,0:T(8,128)S(1)} %reshape.519), channel_id=1, source_target_pairs={{0,8},{8,0},{1,9},{9,1},{2,10},{10,2},{3,11},{11,3},{4,12},{12,4},... | collective-permute-start | bytes 147848 | tf_op jit(solution)/shard_map/ppermute | solution.py:583
  456.5 4.9 %collective-permute-start.11 = (f32[32,770]{1,0:T(8,128)S(1)}, f32[32,770]{1,0:T(8,128)S(1)}, u32[]{:S(2)}, u32[]{:S(2)}) collective-permute-start(f32[32,770]{1,0:T(8,128)S(1)} %pad_maximum_fusion.8), channel_id=1, source_target_pairs={{0,16},{16,0},{1,17},{17,1},{2,18},{18,2},{3,19},{19,3},{4,20},{20... | collective-permute-start | bytes 295688 | tf_op jit(solution)/shard_map/ppermute | solution.py:583
  (22 other events, 294.7 us)
Sparse Core Ops, SparseCore 0:
  19.6 46.6 all-gather.3
  69.1 58.7 all-gather.5
  130.8 58.1 all-gather.7

commit v3 on v2

--- a/solution.py
+++ b/solution.py
@@ -12,9 +12,12 @@
 QT = 256
 KT = 256
 RT = 512
-FC = 512
+MT = 512
+MT2 = 512
+FC = 768
 EPS = 1e-05
 NEG = -1e30
+LOG2E = 1.4426950408889634
 f32 = jnp.float32
 bf16 = jnp.bfloat16
 VMEM_BYTES = 60 * 1000 * 1024
@@ -67,7 +70,7 @@
 
 
 def qkv_kernel(core_ref, tok_ref, row_ref, vec_ref, bias_ref, mine_ref, other_ref,
-               q_ref, k_ref, v_ref, qT_ref, kT_ref, vT_ref, w_ref, sems):
+               q_ref, k_ref, v_ref, qT_ref, kT_ref, vT_ref, hid_ref, w_ref, sems):
     @pl.when((pl.program_id(0) == 0) & (pl.program_id(1) == 0))
     def _():
         copies = place_halves(mine_ref, other_ref, w_ref, core_ref[0], sems)
@@ -80,12 +83,14 @@
     base = tok_ref[0].astype(f32) + row_ref[0]
     normed, unused = normalize(base)
     hidden = (normed * vec_ref[0:1, :] + vec_ref[1:2, :]).astype(bf16)
+    hid_ref[0] = hidden
     scale = HD ** (-0.5)
     for n, (out, outT) in enumerate(((q_ref, qT_ref), (k_ref, kT_ref), (v_ref, vT_ref))):
         cols = slice(n * width, (n + 1) * width)
-        rows = (dg(hidden, w_ref[:, cols], 1, 0) + bias_ref[:, cols]).astype(bf16)
+        exact = dg(hidden, w_ref[:, cols], 1, 0) + bias_ref[:, cols]
+        rows = exact.astype(bf16)
         scaled = (rows.astype(f32) * scale).astype(bf16)
-        out[0] = scaled if n == 0 else rows
+        out[0] = (exact * (scale * LOG2E)).astype(bf16) if n == 0 else rows
         outT[0] = (rows if n == 2 else scaled).T
 
 
@@ -106,8 +111,10 @@
             anyspec,
             anyspec,
         ],
-        out_specs=[row, row, row, col, col, col],
-        out_shape=[jax.ShapeDtypeStruct((B, S, D), bf16)] * 3 + [jax.ShapeDtypeStruct((B, D, S), bf16)] * 3,
+        out_specs=[row, row, row, col, col, col, row],
+        out_shape=[jax.ShapeDtypeStruct((B, S, D), bf16)] * 3
+        + [jax.ShapeDtypeStruct((B, D, S), bf16)] * 3
+        + [jax.ShapeDtypeStruct((B, S, D), bf16)],
         scratch_shapes=[pltpu.VMEM((D, 3 * D), bf16), pltpu.SemaphoreType.DMA((2,))],
         compiler_params=params(),
         cost_estimate=pl.CostEstimate(flops=6 * B * S * D * D, bytes_accessed=30 * 10**6, transcendentals=0),
@@ -118,135 +125,207 @@
     lane=lax.broadcasted_iota(jnp.int32,(rows,256),1)
     return (lane//64)==h
 
-def fwd_kernel(lo_ref, hi_ref, q_ref, k_ref, vT_ref, segk_ref, segq_ref, mixed_ref, mixedT_ref, lse_ref, acc, mrow, lrow):
-    b=pl.program_id(0); i=pl.program_id(1)
-    nq=pl.num_programs(1)
-    lo=lo_ref[b*nq+i]; hi=hi_ref[b*nq+i]
-    segq=segq_ref[0]
-    acc[...]=jnp.zeros_like(acc)
-    mrow[...]=jnp.full_like(mrow,NEG); lrow[...]=jnp.zeros_like(lrow)
-    def body(c,carry):
-        c0=pl.multiple_of(c*KT,KT)
-        segk=segk_ref[0,pl.ds(c0,KT),:]
-        same=jnp.concatenate([segk,segk],axis=1)==segq
-        bias=jnp.where(same,0.0,NEG)
+SAVED = True
+HPAD = 16
+
+
+def masked_heads(block):
+    return jnp.concatenate([jnp.where(head_mask(j, block.shape[0]), block, jnp.zeros_like(block)) for j in range(4)], axis=0)
+
+
+def fwd_kernel(lo_ref, hi_ref, q_ref, k_ref, vT_ref, segk_ref, segq_ref,
+               mixed_ref, mixedT_ref, prob_ref, fac_ref, acc, mrow, lrow):
+    b = pl.program_id(0)
+    i = pl.program_id(1)
+    nq = pl.num_programs(1)
+    segq = segq_ref[0]
+    acc[...] = jnp.zeros_like(acc)
+    mrow[...] = jnp.full_like(mrow, NEG)
+    lrow[...] = jnp.zeros_like(lrow)
+
+    def body(c, carry):
+        c0 = pl.multiple_of(c * KT, KT)
+        segk = segk_ref[0, pl.ds(c0, KT), :]
+        bias = jnp.where(jnp.concatenate([segk, segk], axis=1) == segq, 0.0, NEG)
+
         def scores(quad):
-            k4=k_ref[0,pl.ds(c0,KT),quad*256:(quad+1)*256]
-            km=jnp.concatenate([jnp.where(head_mask(j,KT),k4,jnp.zeros_like(k4)) for j in range(4)],axis=0)
-            return dg(km,q_ref[0,:,quad*256:(quad+1)*256],1,1)
-        s_next=scores(0)
-        for quad in range(HEADS//4):
-            s4=s_next
-            if quad+1<HEADS//4: s_next=scores(quad+1)
+            cols = slice(quad * 256, (quad + 1) * 256)
+            return dg(masked_heads(k_ref[0, pl.ds(c0, KT), cols]), q_ref[0, :, cols], 1, 1)
+
+        ready = scores(0)
+        for quad in range(HEADS // 4):
+            s4 = ready
+            if quad + 1 < HEADS // 4:
+                ready = scores(quad + 1)
             for j in range(4):
-                h=quad*4+j
-                s=s4[j*KT:(j+1)*KT]+bias
-                m_old=mrow[h:h+1,:]
-                m_new=jnp.maximum(m_old,jnp.max(s,axis=0,keepdims=True))
-                p=jnp.exp(s-m_new)
-                alpha=jnp.exp(m_old-m_new)
-                mrow[h:h+1,:]=m_new
-                lrow[h:h+1,:]=lrow[h:h+1,:]*alpha+jnp.sum(p,axis=0,keepdims=True)
-                o=dg(vT_ref[0,h*HD:(h+1)*HD,pl.ds(c0,KT)],p.astype(bf16),1,0)
-                acc[h*HD:(h+1)*HD,:]=acc[h*HD:(h+1)*HD,:]*alpha+o
+                h = quad * 4 + j
+                rows = slice(h * HD, (h + 1) * HD)
+                s = s4[j * KT : (j + 1) * KT] + bias
+                m_old = mrow[h : h + 1, :]
+                m_new = jnp.maximum(m_old, jnp.max(s, axis=0, keepdims=True))
+                p = jnp.exp2(s - m_new)
+                alpha = jnp.exp2(m_old - m_new)
+                mrow[h : h + 1, :] = m_new
+                lrow[h : h + 1, :] = lrow[h : h + 1, :] * alpha + jnp.sum(p, axis=0, keepdims=True)
+                pb = p.astype(bf16)
+                prob_ref[0, 0, h, pl.ds(c0, KT), :] = pb
+                acc[rows, :] = acc[rows, :] * alpha + dg(vT_ref[0, rows, pl.ds(c0, KT)], pb, 1, 0)
+        fac_ref[0, 0, c] = mrow[...]
         return carry
-    lax.fori_loop(lo,hi,body,0)
-    inv=1.0/lrow[...]
-    lse_ref[0]=mrow[...]+jnp.log(lrow[...])
+
+    lax.fori_loop(lo_ref[b * nq + i], hi_ref[b * nq + i], body, 0)
+    total = lrow[0:HEADS, :]
+    inv = 1.0 / total
+    lse = mrow[0:HEADS, :] + jnp.log2(total)
+    for c in range(fac_ref.shape[2]):
+        fac_ref[0, 0, c, 0:HEADS, :] = jnp.exp2(fac_ref[0, 0, c, 0:HEADS, :] - lse)
     for h in range(HEADS):
-        o=acc[h*HD:(h+1)*HD,:]*inv[h:h+1,:]
-        mixedT_ref[0,h*HD:(h+1)*HD,:]=o
-    mixed_ref[0]=mixedT_ref[0].astype(bf16).T
-
-def attn_fwd(lo,hi,q,k,vT,segk,segq):
-    B,S,D=q.shape; nq=S//QT
-    return pl.pallas_call(fwd_kernel,
-      grid_spec=pltpu.PrefetchScalarGridSpec(num_scalar_prefetch=2, grid=(B,nq),
-        in_specs=[pl.BlockSpec((1,QT,D),lambda b,i,*_:(b,i,0)),
-                  pl.BlockSpec((1,S,D),lambda b,i,*_:(b,0,0)),
-                  pl.BlockSpec((1,D,S),lambda b,i,*_:(b,0,0)),
-                  pl.BlockSpec((1,S,128),lambda b,i,*_:(b,0,0)),
-                  pl.BlockSpec((1,1,QT),lambda b,i,*_:(b,0,i))],
-        out_specs=[pl.BlockSpec((1,QT,D),lambda b,i,*_:(b,i,0)),
-                   pl.BlockSpec((1,D,QT),lambda b,i,*_:(b,0,i)),
-                   pl.BlockSpec((1,HEADS,QT),lambda b,i,*_:(b,0,i))],
-        scratch_shapes=[pltpu.VMEM((D,QT),f32),pltpu.VMEM((HEADS,QT),f32),pltpu.VMEM((HEADS,QT),f32)]),
-      out_shape=[jax.ShapeDtypeStruct((B,S,D),bf16),jax.ShapeDtypeStruct((B,D,S),f32),jax.ShapeDtypeStruct((B,HEADS,S),f32)],
-      compiler_params=params(),
-      cost_estimate=pl.CostEstimate(flops=16 * B * S * S * D, bytes_accessed=30 * 10**6, transcendentals=0),
-      name="attn_fwd")(lo,hi,q,k,vT,segk,segq)
-
-def bwd_kernel(lo_ref, hi_ref, q_ref, qT_ref, k_ref, kT_ref, v_ref, do_ref, doT_ref, oT_ref, lse_ref, segk_ref, segq_ref, after_ref,
+        rows = slice(h * HD, (h + 1) * HD)
+        mixedT_ref[0, rows, :] = acc[rows, :] * inv[h : h + 1, :]
+    mixed_ref[0] = mixedT_ref[0].astype(bf16).T
+
+
+def attn_fwd(lo, hi, q, k, vT, segk, segq):
+    B, S, D = q.shape
+    nq = S // QT
+    nk = S // KT
+    row = pl.BlockSpec((1, QT, D), lambda b, i, *_: (b, i, 0))
+    col = pl.BlockSpec((1, D, QT), lambda b, i, *_: (b, 0, i))
+    sds = jax.ShapeDtypeStruct
+    return pl.pallas_call(
+        fwd_kernel,
+        grid_spec=pltpu.PrefetchScalarGridSpec(
+            num_scalar_prefetch=2,
+            grid=(B, nq),
+            in_specs=[
+                row,
+                pl.BlockSpec((1, S, D), lambda b, i, *_: (b, 0, 0)),
+                pl.BlockSpec((1, D, S), lambda b, i, *_: (b, 0, 0)),
+                pl.BlockSpec((1, S, 128), lambda b, i, *_: (b, 0, 0)),
+                pl.BlockSpec((1, 1, QT), lambda b, i, *_: (b, 0, i)),
+            ],
+            out_specs=[
+                row,
+                col,
+                pl.BlockSpec((1, 1, HEADS, S, QT), lambda b, i, *_: (b, i, 0, 0, 0)),
+                pl.BlockSpec((1, 1, nk, HPAD, QT), lambda b, i, *_: (b, i, 0, 0, 0)),
+            ],
+            scratch_shapes=[pltpu.VMEM((D, QT), f32), pltpu.VMEM((HPAD, QT), f32), pltpu.VMEM((HPAD, QT), f32)],
+        ),
+        out_shape=[
+            sds((B, S, D), bf16),
+            sds((B, D, S), f32),
+            sds((B, nq, HEADS, S, QT), bf16),
+            sds((B, nq, nk, HPAD, QT), f32),
+        ],
+        compiler_params=params(),
+        cost_estimate=pl.CostEstimate(flops=16 * B * S * S * D, bytes_accessed=80 * 10**6, transcendentals=0),
+        name="attn_fwd",
+    )(lo, hi, q, k, vT, segk, segq)
+
+
+def bwd_kernel(lo_ref, hi_ref, qT_ref, kT_ref, v_ref, do_ref, doT_ref, oT_ref, prob_ref, fac_ref, after_ref,
                dq_ref, dk_ref, dv_ref, dqT, dkT, dvT, dlt):
-    b=pl.program_id(0); i=pl.program_id(1)
-    nq=pl.num_programs(1)
-    lo=lo_ref[b*nq+i]; hi=hi_ref[b*nq+i]
-    segq=segq_ref[0]
-    @pl.when(i==0)
-    def _():
-        dkT[...]=jnp.zeros_like(dkT); dvT[...]=jnp.zeros_like(dvT)
-    dqT[...]=jnp.zeros_like(dqT)
+    b = pl.program_id(0)
+    i = pl.program_id(1)
+    nq = pl.num_programs(1)
+
+    @pl.when(i == 0)
+    def _():
+        dkT[...] = jnp.zeros_like(dkT)
+        dvT[...] = jnp.zeros_like(dvT)
+
+    dqT[...] = jnp.zeros_like(dqT)
     for h in range(HEADS):
-        sl=slice(h*HD,(h+1)*HD)
-        dlt[h:h+1,:]=jnp.sum(doT_ref[0,sl,:]*oT_ref[0,sl,:],axis=0,keepdims=True)
-    def body(c,carry):
-        c0=pl.multiple_of(c*KT,KT)
-        segk=segk_ref[0,pl.ds(c0,KT),:]
-        same=jnp.concatenate([segk,segk],axis=1)==segq
-        bias=jnp.where(same,0.0,NEG)
-        def two(quad):
-            ql=slice(quad*256,(quad+1)*256)
-            k4=k_ref[0,pl.ds(c0,KT),ql]; v4=v_ref[0,pl.ds(c0,KT),ql]
-            km=jnp.concatenate([jnp.where(head_mask(j,KT),k4,jnp.zeros_like(k4)) for j in range(4)],axis=0)
-            vm=jnp.concatenate([jnp.where(head_mask(j,KT),v4,jnp.zeros_like(v4)) for j in range(4)],axis=0)
-            return dg(km,q_ref[0,:,ql],1,1), dg(vm,do_ref[0,:,ql],1,1)
-        nxt=two(0)
-        for quad in range(HEADS//4):
-            s4,dp4=nxt
-            if quad+1<HEADS//4: nxt=two(quad+1)
+        rows = slice(h * HD, (h + 1) * HD)
+        dlt[h : h + 1, :] = jnp.sum(doT_ref[0, rows, :].astype(f32) * oT_ref[0, rows, :], axis=0, keepdims=True)
+
+    def body(c, carry):
+        c0 = pl.multiple_of(c * KT, KT)
+        keys = pl.ds(c0, KT)
+
+        def products(quad):
+            cols = slice(quad * 256, (quad + 1) * 256)
+            return dg(masked_heads(v_ref[0, keys, cols]), do_ref[0, :, cols], 1, 1)
+
+        ready = products(0)
+        for quad in range(HEADS // 4):
+            dp4 = ready
+            if quad + 1 < HEADS // 4:
+                ready = products(quad + 1)
             for j in range(4):
-                h=quad*4+j; sl=slice(h*HD,(h+1)*HD)
-                p=jnp.exp(s4[j*KT:(j+1)*KT]+bias-lse_ref[0,h:h+1,:])
-                ds=(p*(dp4[j*KT:(j+1)*KT]-dlt[h:h+1,:])).astype(bf16)
-                pb=p.astype(bf16)
-                dvT[sl,pl.ds(c0,KT)]+=dg(doT_ref[0,sl,:],pb,1,1)
-                dkT[sl,pl.ds(c0,KT)]+=dg(qT_ref[0,sl,:],ds,1,1)
-                dqT[sl,:]+=dg(kT_ref[0,sl,pl.ds(c0,KT)],ds,1,0)
+                h = quad * 4 + j
+                rows = slice(h * HD, (h + 1) * HD)
+                factor = fac_ref[0, 0, c, h : h + 1, :]
+                pb = prob_ref[0, 0, h, keys, :]
+                ds = (pb.astype(f32) * ((dp4[j * KT : (j + 1) * KT] - dlt[h : h + 1, :]) * factor)).astype(bf16)
+                scaled = (doT_ref[0, rows, :].astype(f32) * factor).astype(bf16)
+                dvT[rows, keys] += dg(scaled, pb, 1, 1)
+                dkT[rows, keys] += dg(qT_ref[0, rows, :], ds, 1, 1)
+                dqT[rows, :] += dg(kT_ref[0, rows, keys], ds, 1, 0)
         return carry
-    lax.fori_loop(lo,hi,body,0)
-    dq_ref[0]=dqT[...].astype(bf16).T
-    @pl.when(i==nq-1)
-    def _():
-        dk_ref[0]=dkT[...].astype(bf16).T
-        dv_ref[0]=dvT[...].astype(bf16).T
-
-def attn_bwd(lo,hi,q,qT,k,kT,v,do,doT,oT,lse,segk,segq,after):
-    B,S,D=q.shape; nq=S//QT
-    row=pl.BlockSpec((1,QT,D),lambda b,i,*_:(b,i,0))
-    col=pl.BlockSpec((1,D,QT),lambda b,i,*_:(b,0,i))
-    full=pl.BlockSpec((1,S,D),lambda b,i,*_:(b,0,0))
-    fullT=pl.BlockSpec((1,D,S),lambda b,i,*_:(b,0,0))
-    return pl.pallas_call(bwd_kernel,
-      grid_spec=pltpu.PrefetchScalarGridSpec(num_scalar_prefetch=2, grid=(B,nq),
-        in_specs=[row,col,full,fullT,full,row,col,col,
-                  pl.BlockSpec((1,HEADS,QT),lambda b,i,*_:(b,0,i)),
-                  pl.BlockSpec((1,S,128),lambda b,i,*_:(b,0,0)),
-                  pl.BlockSpec((1,1,QT),lambda b,i,*_:(b,0,i)),
-                  pl.BlockSpec(memory_space=pl.ANY)],
-        out_specs=[row,full,full],
-        scratch_shapes=[pltpu.VMEM((D,QT),f32),pltpu.VMEM((D,S),f32),pltpu.VMEM((D,S),f32),pltpu.VMEM((HEADS,QT),f32)]),
-      out_shape=[jax.ShapeDtypeStruct((B,S,D),bf16)]*3,
-      compiler_params=params(),
-      cost_estimate=pl.CostEstimate(flops=32 * B * S * S * D, bytes_accessed=40 * 10**6, transcendentals=0),
-      name="attn_bwd")(lo,hi,q,qT,k,kT,v,do,doT,oT,lse,segk,segq,after)
+
+    lax.fori_loop(lo_ref[b * nq + i], hi_ref[b * nq + i], body, 0)
+    dq_ref[0] = dqT[...].astype(bf16).T
+
+    @pl.when(i == nq - 1)
+    def _():
+        dk_ref[0] = dkT[...].astype(bf16).T
+        dv_ref[0] = dvT[...].astype(bf16).T
+
+
+def attn_bwd(lo, hi, qT, kT, v, do, doT, oT, prob, fac, after):
+    B, S, D = v.shape
+    nq = S // QT
+    nk = S // KT
+    row = pl.BlockSpec((1, QT, D), lambda b, i, *_: (b, i, 0))
+    col = pl.BlockSpec((1, D, QT), lambda b, i, *_: (b, 0, i))
+    full = pl.BlockSpec((1, S, D), lambda b, i, *_: (b, 0, 0))
+    fullT = pl.BlockSpec((1, D, S), lambda b, i, *_: (b, 0, 0))
+    return pl.pallas_call(
+        bwd_kernel,
+        grid_spec=pltpu.PrefetchScalarGridSpec(
+            num_scalar_prefetch=2,
+            grid=(B, nq),
+            in_specs=[
+                col,
+                fullT,
+                full,
+                row,
+                col,
+                col,
+                pl.BlockSpec((1, 1, HEADS, S, QT), lambda b, i, *_: (b, i, 0, 0, 0)),
+                pl.BlockSpec((1, 1, nk, HPAD, QT), lambda b, i, *_: (b, i, 0, 0, 0)),
+                pl.BlockSpec(memory_space=pl.ANY),
+            ],
+            out_specs=[row, full, full],
+            scratch_shapes=[
+                pltpu.VMEM((D, QT), f32),
+                pltpu.VMEM((D, S), f32),
+                pltpu.VMEM((D, S), f32),
+                pltpu.VMEM((HPAD, QT), f32),
+            ],
+        ),
+        out_shape=[jax.ShapeDtypeStruct((B, S, D), bf16)] * 3,
+        compiler_params=params(),
+        cost_estimate=pl.CostEstimate(flops=32 * B * S * S * D, bytes_accessed=90 * 10**6, transcendentals=0),
+        name="attn_bwd",
+    )(lo, hi, qT, kT, v, do, doT, oT, prob, fac, after)
 
 
 def mlp_chunks(hid, cot, wup, wdown, bup_ref, acc, gh2, aup, adown, bupg_ref):
-    def chunk(j, carry):
-        c0 = pl.multiple_of(j * FC, FC)
-        cols = pl.ds(c0, FC)
-        up = dg(hid, wup[:, cols], 1, 0) + bup_ref[:, cols]
-        ga = dg(cot, wdown[cols, :], 1, 1)
+    count = wup.shape[1] // FC
+
+    def products(j):
+        cols = slice(j * FC, (j + 1) * FC)
+        return dg(hid, wup[:, cols], 1, 0) + bup_ref[:, cols], dg(cot, wdown[cols, :], 1, 1)
+
+    ready = products(0)
+    for j in range(count):
+        cols = slice(j * FC, (j + 1) * FC)
+        up, ga = ready
+        if j + 1 < count:
+            ready = products(j + 1)
         active, slope = gelu_parts(up)
         active = active.astype(bf16)
         gu = (ga * slope).astype(bf16)
@@ -255,9 +334,6 @@
         gh2[0] += dg(gu, wup[:, cols], 1, 1)
         aup[:, cols] += dg(hid, gu, 0, 0)
         bupg_ref[:, cols] += col_sum(gu.astype(f32))
-        return carry
-
-    lax.fori_loop(0, wup.shape[1] // FC, chunk, 0)
 
 
 def mlp_load(first, w_ref, extra, wup, wdown, sems):
@@ -293,7 +369,7 @@
 
 def mlp_first_kernel(core_ref, tok_ref, row_ref, cot_ref, mix_ref, vec_ref, bup_ref, w_ref,
                      acc_ref, gh2_ref, mid_ref, hid_ref, bupg_ref, keep_ref, send_ref,
-                     wout, wup, wdown, aup, adown, sems):
+                     wout, wup, wdown, aup, adown, acc, gh2, sems):
     i = pl.program_id(0)
     D = tok_ref.shape[2]
 
@@ -313,9 +389,11 @@
     mid_ref[0] = middle
     normed, unused = normalize(middle)
     hid_ref[0] = (normed * vec_ref[1:2, :] + vec_ref[2:3, :]).astype(bf16)
-    acc_ref[0] = middle + vec_ref[3:4, :]
-    gh2_ref[...] = jnp.zeros_like(gh2_ref)
-    mlp_chunks(hid_ref[0], cot_ref[0], wup, wdown, bup_ref, acc_ref, gh2_ref, aup, adown, bupg_ref)
+    acc[...] = jnp.zeros_like(acc)
+    gh2[...] = jnp.zeros_like(gh2)
+    mlp_chunks(hid_ref[0], cot_ref[0], wup, wdown, bup_ref, acc, gh2, aup, adown, bupg_ref)
+    acc_ref[...] = acc[...].astype(bf16)
+    gh2_ref[...] = gh2[...].astype(bf16)
 
     @pl.when(i == pl.num_programs(0) - 1)
     def _():
@@ -345,8 +423,8 @@
         for c in copies:
             c.wait()
 
-    acc[...] = accin_ref[...]
-    gh2[...] = gh2in_ref[...]
+    acc[...] = accin_ref[...].astype(f32) + mid_ref[...] + vec_ref[3:4, :]
+    gh2[...] = gh2in_ref[...].astype(f32)
     cot = cot_ref[0]
     mlp_chunks(hid_ref[0], cot, wup, wdown, bup_ref, acc, gh2, aup, adown, bupg_ref)
     out_ref[0] = acc[0].astype(bf16)
@@ -379,11 +457,11 @@
         mlp_store(core, wup, wdown, keep_ref, send_ref, extra, sems)
 
 
-def mlp_specs(tokens):
+def mlp_specs(tokens, tile):
     B, S, D = tokens.shape
-    per = S // RT
-    row = pl.BlockSpec((1, RT, D), lambda i: (i // per, i % per, 0))
-    col = pl.BlockSpec((1, D, RT), lambda i: (i // per, 0, i % per))
+    per = S // tile
+    row = pl.BlockSpec((1, tile, D), lambda i: (i // per, i % per, 0))
+    col = pl.BlockSpec((1, D, tile), lambda i: (i // per, 0, i % per))
     one = pl.BlockSpec((1, 1, D), lambda i: (i // per, 0, 0))
     return row, col, one, pl.BlockSpec(memory_space=pl.ANY), pl.BlockSpec(memory_space=pltpu.SMEM)
 
@@ -395,20 +473,22 @@
 def mlp_first(core, tokens, trow, cot, mixed, vec, bup, weights):
     B, S, D = tokens.shape
     H = bup.shape[1]
-    row, col, one, anyspec, smem = mlp_specs(tokens)
+    row, col, one, anyspec, smem = mlp_specs(tokens, MT)
     sds = jax.ShapeDtypeStruct
     return pl.pallas_call(
         mlp_first_kernel,
-        grid=(B * S // RT,),
+        grid=(B * S // MT,),
         in_specs=[smem, row, one, row, row, whole(vec.shape), whole(bup.shape), anyspec],
         out_specs=[row, row, row, row, whole((1, H)), anyspec, anyspec],
-        out_shape=[sds((B, S, D), f32)] * 3 + [sds((B, S, D), bf16), sds((1, H), f32)] + [sds((D, H), bf16)] * 2,
+        out_shape=[sds((B, S, D), bf16)] * 2 + [sds((B, S, D), f32), sds((B, S, D), bf16), sds((1, H), f32)] + [sds((D, H), bf16)] * 2,
         scratch_shapes=[
             pltpu.VMEM((D, D), bf16),
             pltpu.VMEM((D, H), bf16),
             pltpu.VMEM((H, D), bf16),
             pltpu.VMEM((D, H), f32),
             pltpu.VMEM((H, D), f32),
+            pltpu.VMEM((1, MT, D), f32),
+            pltpu.VMEM((1, MT, D), f32),
             pltpu.SemaphoreType.DMA((2 + H // D,)),
         ],
         compiler_params=params(),
@@ -420,12 +500,12 @@
 def mlp_second(core, acc, gh2, mid, hid, cot, mixed, vec, bup, wfirst, weights):
     B, S, D = cot.shape
     H = bup.shape[1]
-    row, col, one, anyspec, smem = mlp_specs(cot)
+    row, col, one, anyspec, smem = mlp_specs(cot, MT2)
     sds = jax.ShapeDtypeStruct
     wide = sds((D, H + D // 2), bf16)
     return pl.pallas_call(
         mlp_second_kernel,
-        grid=(B * S // RT,),
+        grid=(B * S // MT2,),
         in_specs=[smem] + [row] * 6 + [whole(vec.shape), whole(bup.shape), anyspec, anyspec],
         out_specs=[row, row, row, col, whole((4, D)), whole((1, H)), anyspec, anyspec],
         out_shape=[
@@ -445,8 +525,8 @@
             pltpu.VMEM((D, D), f32),
             pltpu.VMEM((D, H), f32),
             pltpu.VMEM((H, D), f32),
-            pltpu.VMEM((1, RT, D), f32),
-            pltpu.VMEM((1, RT, D), f32),
+            pltpu.VMEM((1, MT2, D), f32),
+            pltpu.VMEM((1, MT2, D), f32),
             pltpu.SemaphoreType.DMA((3 + H // D,)),
         ],
         compiler_params=params(),
@@ -455,19 +535,63 @@
     )(core, acc, gh2, mid, hid, cot, mixed, vec, bup, wfirst, weights)
 
 
-def qkv_back_kernel(core_ref, tok_ref, row_ref, gmid_ref, dq_ref, dk_ref, dv_ref, vec_ref, mine_ref, other_ref,
-                    gin_ref, rsum_ref, vecg_ref, keep_ref, send_ref, w_ref, aw_ref, sems):
+def qkv_weights_kernel(core_ref, hid_ref, dq_ref, dk_ref, dv_ref, keep_ref, send_ref, aw_ref, low_ref, sems):
     b = pl.program_id(0)
     i = pl.program_id(1)
     core = core_ref[0]
-    D = tok_ref.shape[2]
+    D = hid_ref.shape[2]
 
     @pl.when((b == 0) & (i == 0))
     def _():
-        copies = place_halves(mine_ref, other_ref, w_ref, core, sems)
+        aw_ref[...] = jnp.zeros_like(aw_ref)
+
+    for n, g in enumerate((dq_ref[0], dk_ref[0], dv_ref[0])):
+        aw_ref[:, n * D : (n + 1) * D] += dg(hid_ref[0], g, 0, 0)
+
+    @pl.when((b == pl.num_programs(0) - 1) & (i == pl.num_programs(1) - 1))
+    def _():
+        low_ref[...] = aw_ref[...].astype(bf16)
+        half = keep_ref.shape[1]
+        at = pl.multiple_of(core * half, 128)
+        rest = pl.multiple_of((1 - core) * half, 128)
+        copies = (
+            pltpu.make_async_copy(low_ref.at[:, pl.ds(at, half)], keep_ref, sems.at[0]),
+            pltpu.make_async_copy(low_ref.at[:, pl.ds(rest, half)], send_ref, sems.at[1]),
+        )
         for c in copies:
             c.start()
-        aw_ref[...] = jnp.zeros_like(aw_ref)
+        for c in copies:
+            c.wait()
+
+
+def qkv_weights_call(core, hid, dq, dk, dv):
+    B, S, D = hid.shape
+    row = pl.BlockSpec((1, S, D), lambda b, i: (b, i, 0))
+    anyspec = pl.BlockSpec(memory_space=pl.ANY)
+    half = jax.ShapeDtypeStruct((D, 3 * D // 2), bf16)
+    return pl.pallas_call(
+        qkv_weights_kernel,
+        grid=(B, 1),
+        in_specs=[pl.BlockSpec(memory_space=pltpu.SMEM), row, row, row, row],
+        out_specs=[anyspec, anyspec],
+        out_shape=[half, half],
+        scratch_shapes=[pltpu.VMEM((D, 3 * D), f32), pltpu.VMEM((D, 3 * D), bf16), pltpu.SemaphoreType.DMA((2,))],
+        compiler_params=params(),
+        cost_estimate=pl.CostEstimate(flops=6 * B * S * D * D, bytes_accessed=20 * 10**6, transcendentals=0),
+        name="qkv_weights",
+    )(core, hid, dq, dk, dv)
+
+
+def qkv_back_kernel(core_ref, tok_ref, row_ref, gmid_ref, dq_ref, dk_ref, dv_ref, vec_ref, mine_ref, other_ref, after_ref,
+                    gin_ref, rsum_ref, vecg_ref, w_ref, sems):
+    b = pl.program_id(0)
+    i = pl.program_id(1)
+
+    @pl.when((b == 0) & (i == 0))
+    def _():
+        copies = place_halves(mine_ref, other_ref, w_ref, core_ref[0], sems)
+        for c in copies:
+            c.start()
         vecg_ref[...] = jnp.zeros_like(vecg_ref)
         for c in copies:
             c.wait()
@@ -476,16 +600,10 @@
     def _():
         rsum_ref[...] = jnp.zeros_like(rsum_ref)
 
+    grads = (dq_ref[0], dk_ref[0], dv_ref[0])
+    grad_hidden = dg(jnp.concatenate(grads, axis=1), w_ref[...], 1, 1)
     base = tok_ref[0].astype(f32) + row_ref[0]
     normed, inv = normalize(base)
-    hidden = (normed * vec_ref[0:1, :] + vec_ref[1:2, :]).astype(bf16)
-    grads = (dq_ref[0], dk_ref[0], dv_ref[0])
-    grad_hidden = None
-    for n, g in enumerate(grads):
-        cols = slice(n * D, (n + 1) * D)
-        part = dg(g, w_ref[:, cols], 1, 1)
-        grad_hidden = part if grad_hidden is None else grad_hidden + part
-        aw_ref[:, cols] += dg(hidden, g, 0, 0)
     gbase = gmid_ref[0] + norm_back(grad_hidden, normed, inv, vec_ref[0:1, :])
     gin_ref[0] = gbase.astype(bf16)
     rsum_ref[0] += col_sum(gbase)
@@ -494,23 +612,8 @@
     vecg_ref[2:3, :] += col_sum(grads[0].astype(f32))
     vecg_ref[3:4, :] += col_sum(grads[2].astype(f32))
 
-    @pl.when((b == pl.num_programs(0) - 1) & (i == pl.num_programs(1) - 1))
-    def _():
-        w_ref[...] = aw_ref[...].astype(bf16)
-        half = keep_ref.shape[1]
-        at = pl.multiple_of(core * half, 128)
-        rest = pl.multiple_of((1 - core) * half, 128)
-        copies = (
-            pltpu.make_async_copy(w_ref.at[:, pl.ds(at, half)], keep_ref, sems.at[0]),
-            pltpu.make_async_copy(w_ref.at[:, pl.ds(rest, half)], send_ref, sems.at[1]),
-        )
-        for c in copies:
-            c.start()
-        for c in copies:
-            c.wait()
-
-
-def qkv_back_call(core, tokens, trow, gmid, dq, dk, dv, vec, mine, other):
+
+def qkv_back_call(core, tokens, trow, gmid, dq, dk, dv, vec, mine, other, after):
     B, S, D = tokens.shape
     row = pl.BlockSpec((1, RT, D), lambda b, i: (b, i, 0))
     seq = pl.BlockSpec((1, 1, D), lambda b, i: (b, 0, 0))
@@ -530,24 +633,15 @@
             pl.BlockSpec(vec.shape, lambda b, i: (0, 0)),
             anyspec,
             anyspec,
+            anyspec,
         ],
-        out_specs=[row, seq, pl.BlockSpec((4, D), lambda b, i: (0, 0)), anyspec, anyspec],
-        out_shape=[
-            sds((B, S, D), bf16),
-            sds((B, 1, D), f32),
-            sds((4, D), f32),
-            sds(mine.shape, bf16),
-            sds(mine.shape, bf16),
-        ],
-        scratch_shapes=[
-            pltpu.VMEM((D, 3 * D), bf16),
-            pltpu.VMEM((D, 3 * D), f32),
-            pltpu.SemaphoreType.DMA((2,)),
-        ],
+        out_specs=[row, seq, pl.BlockSpec((4, D), lambda b, i: (0, 0))],
+        out_shape=[sds((B, S, D), bf16), sds((B, 1, D), f32), sds((4, D), f32)],
+        scratch_shapes=[pltpu.VMEM((D, 3 * D), bf16), pltpu.SemaphoreType.DMA((2,))],
         compiler_params=params(),
-        cost_estimate=pl.CostEstimate(flops=12 * B * S * D * D, bytes_accessed=40 * 10**6, transcendentals=0),
+        cost_estimate=pl.CostEstimate(flops=6 * B * S * D * D, bytes_accessed=40 * 10**6, transcendentals=0),
         name="norm_qkv_back",
-    )(core, tokens, trow, gmid, dq, dk, dv, vec, mine, other)
+    )(core, tokens, trow, gmid, dq, dk, dv, vec, mine, other, after)
 
 
 def key_ranges(segment_ids):
@@ -618,6 +712,14 @@
     came = lax.all_to_all(sent.reshape(size * (rows + EXTRA), width), axis, 0, 0, tiled=True)
     came = came.reshape(size, rows + EXTRA, width)
     return jnp.sum(came[:, :rows].astype(f32), axis=0).astype(bf16), came[:, rows:].astype(f32)
+
+
+def direct_exchange(array, axis):
+    size, me = lax.axis_size(axis), lax.axis_index(axis)
+    came = [own_slice(array, me, 1, 0)]
+    for r in range(1, size):
+        came.append(lax.ppermute(own_slice(array, me ^ r, 1, 0), axis, [(i, i ^ r) for i in range(size)]))
+    return jnp.concatenate(came, axis=0)
 
 
 def on_device(
@@ -689,8 +791,8 @@
     segk = jnp.broadcast_to(segment_ids[:, :, None], (B, S, 128))
     segq = segment_ids[:, None, :]
 
-    q, k, v, qT, kT, vT = qkv_call(core1, tokens, trow, vec1, bias, qkv_mine, qkv_other)
-    mixed, mixedT, lse = attn_fwd(lo, hi, q, k, vT, segk, segq)
+    q, k, v, qT, kT, vT, hid1 = qkv_call(core1, tokens, trow, vec1, bias, qkv_mine, qkv_other)
+    mixed, mixedT, prob, fac = attn_fwd(lo, hi, q, k, vT, segk, segq)
     local_b, w_a, mixed = lax.optimization_barrier((local_b, w_a, mixed))
     w_b = lax.all_gather(local_b, ("shard", "core"), axis=0, tiled=True)
     def core_sum(keep, send):
@@ -716,26 +818,30 @@
     bupg = bupg.reshape(J, n, 2, thin).transpose(1, 2, 0, 3).reshape(n, FF // n)
     vectors = jnp.concatenate([vecg2[i].reshape(n, own) for i in range(4)] + [bupg], axis=1)
     part_b, came_b = exchange_reduce(half_b, split_rows(vectors[:, None], half_b.shape[1]), "shard")
-    dq, dk, dv = attn_bwd(lo, hi, q, qT, k, kT, v, gmix, gmixT, mixedT, lse, segk, segq, half_b)
-    gin, rsum, vecg1, qkv_keep, qkv_send = qkv_back_call(
-        core1, tokens, trow, gmid, dq, dk, dv, vec1, qkv_mine, qkv_other
+    dq, dk, dv = attn_bwd(lo, hi, qT, kT, v, gmix, gmixT, mixedT, prob, fac, half_b)
+    keep, send = qkv_weights_call(core1, hid1, dq, dk, dv)
+    qkv_half = core_sum(keep, send)
+    qkv_half, part_b, came_b = lax.optimization_barrier((qkv_half, part_b, came_b))
+    came = lax.all_to_all(qkv_half, "shard", 0, 0, tiled=True).reshape(n, own, 3 * hd)
+    qkv_part = jnp.sum(came.astype(f32), axis=0).astype(bf16)
+    gin, rsum, vecg1 = qkv_back_call(
+        core1, tokens, trow, gmid, dq, dk, dv, vec1, qkv_mine, qkv_other, qkv_half
     )
-    qkv_half = core_sum(qkv_keep, qkv_send)
-    qkv_half, part_b, came_b = lax.optimization_barrier((qkv_half, part_b, came_b))
     vectors = jnp.concatenate([vecg1[i].reshape(n, own) for i in range(4)], axis=1)
-    wide = qkv_half.shape[1]
+    wide = -(-(D + 2) // 128) * 128
     digits = jnp.stack([timesteps // 32, timesteps % 32], axis=1).astype(f32)
     table_rows = jnp.concatenate([rsum.reshape(B, D), digits], axis=1)
-    table_rows = jnp.broadcast_to(split_rows(table_rows, wide)[None], (n, 2 * B, wide))
-    extra = jnp.concatenate([split_rows(vectors[:, None], wide), table_rows], axis=1)
-    qkv_part, came_q = exchange_reduce(qkv_half, extra, "shard")
+    table_rows = jnp.broadcast_to(jnp.pad(table_rows, ((0, 0), (0, wide - D - 2)))[None], (n, B, wide))
+    extra = jnp.concatenate([jnp.pad(vectors, ((0, 0), (0, wide - 4 * own)))[:, None], table_rows], axis=1)
+    extra, qkv_part = lax.optimization_barrier((extra, qkv_part))
+    came_q = direct_exchange(extra, "shard")
 
     vg_b = jnp.sum(came_b[:, :2], axis=(0, 1))[: 4 * own + FF // n]
-    vg_q = jnp.sum(came_q[:, :2], axis=(0, 1))[: 4 * own]
+    vg_q = jnp.sum(came_q[:, 0], axis=0)[: 4 * own]
     vg = all_sum(all_sum(jnp.concatenate([vg_q, vg_b])[None], "core"), "xrep").reshape(-1)
     g_bup = vg[8 * own :]
     vg = [vg[i * own : (i + 1) * own] for i in range(8)]
-    sums = (came_q[:, 2 : 2 + B] + came_q[:, 2 + B : 2 + 2 * B])[:, :, : D + 2].reshape(n * B, D + 2)
+    sums = came_q[:, 1:].reshape(n * B, wide)
     for axis in ("core", "xrep"):
         sums = gather_small(sums, axis)
     own_rows = step_table.shape[0]
@@ -751,7 +857,6 @@
     blocks = jnp.concatenate([a_down, b_down_[:, :H]], axis=1).reshape(2, thin, J, D)
     g_down = blocks.transpose(0, 2, 1, 3).reshape(FF // n, D)
     g_out = jnp.concatenate([b_up_[:, H:], b_down_[:, H:]], axis=1)
-    qkv_part, g_up, g_down, g_out = lax.optimization_barrier((qkv_part, g_up, g_down, g_out))
     q_left, q_right = finish(qkv_part)
     g_qkv = jnp.concatenate([q_left, q_right], axis=1)
     g_q, g_k, g_v = g_qkv[:, :D], g_qkv[:, D : 2 * D], g_qkv[:, 2 * D :]

time: 472 us -> 458 us (0.970); the launches traced: 472 us -> 450 us
  starting transfers between devices: 55 us -> 40.8 us
  waiting for transfers between devices: 79.2 us -> 72.3 us
    all_to_all x2 -> x1, starting transfers between devices: 25.3 us -> 5.87 us  [exchange_reduce(): lax.all_to_all(sent.reshape(size * (rows + EXTRA), width), axis, 0, 0, ti...]
    ppermute x5, waiting for transfers between devices: 19.1 us -> 0.01 us  [all_sum(): came = lax.ppermute(array, axis, [(i, i ^ step) for i in range(size)])]
    all_to_all x0 -> x1, waiting for transfers between devices: none -> 16.4 us  [on_device(): lax.all_to_all(qkv_half, 'shard', 0, 0, tiled=True).reshape(n, own, 3 * hd)]
    all_to_all x2 -> x1, waiting for transfers between devices: 13.8 us -> 0.01 us  [exchange_reduce(): lax.all_to_all(sent.reshape(size * (rows + EXTRA), width), axis, 0, 0, ti...]
    ppermute x0 -> x7, starting transfers between devices: none -> 11.3 us  [direct_exchange(): lax.ppermute(own_slice(array, me ^ r, 1, 0), axis, [(i, i ^ r) for i in r...]
    pallas_call x1, Pallas kernels: 26.5 us -> 17 us  [qkv_back_call(): pl.pallas_call(qkv_back_kernel, grid=(B, S // RT), in_specs=[pl.BlockSpec...]
    all_to_all x1, starting transfers between devices: 12.6 us -> 3.79 us  [on_device(): lax.all_to_all(half_a, 'shard', 0, 0, tiled=True).reshape(n, own, H)]
    pallas_call x2 -> x3, Pallas kernels: 113 us -> 120 us  [the longest x1 55.5 us: mlp_second(): pl.pallas_call(mlp_second_kernel, grid=(B * S // MT2,), in_specs=[smem] +...]
  transfers between devices with their start and end apart: 26 -> 33, of which waited for: 17 -> 16; matrix products, arithmetic and copies ran while one was open for 10% -> 10% of each run, Pallas kernels for 54% -> 58%
where the time goes in v3:
time: 458 us; the launch traced here: 450 us
  Pallas kernels  260 us (57%)
  waiting for transfers between devices  72.3 us (16%)
  starting transfers between devices  40.8 us (9%)
  other arithmetic  32 us (7%)
  local copies, waits for them, and re-layouts  28.9 us (6%)
  between operations  15 us (3%)
    pallas_call x1, Pallas kernels, attn_bwd(): pl.pallas_call(bwd_kernel, grid_spec=pltpu.PrefetchScalarGridSpec(num_sca...  60.1 us
    pallas_call x1, Pallas kernels, mlp_second(): pl.pallas_call(mlp_second_kernel, grid=(B * S // MT2,), in_specs=[smem] +...  55.5 us
    pallas_call x1, Pallas kernels, mlp_first(): pl.pallas_call(mlp_first_kernel, grid=(B * S // MT,), in_specs=[smem, row...  51.8 us
    pallas_call x1, Pallas kernels, attn_fwd(): pl.pallas_call(fwd_kernel, grid_spec=pltpu.PrefetchScalarGridSpec(num_sca...  47 us
    all_gather x1, waiting for transfers between devices, on_device(): qkv_mine = lax.all_gather(qkv_local, 'shard', axis=0, tiled=True)  20.1 us
    pallas_call x1, Pallas kernels, qkv_back_call(): pl.pallas_call(qkv_back_kernel, grid=(B, S // RT), in_specs=[pl.BlockSpec...  17 us
    all_to_all x1, waiting for transfers between devices, on_device(): lax.all_to_all(qkv_half, 'shard', 0, 0, tiled=True).reshape(n, own, 3 * hd)  16.4 us
    pallas_call x1, Pallas kernels, qkv_call(): pl.pallas_call(qkv_kernel, grid=(B, S // RT), in_specs=[pl.BlockSpec(memo...  15.3 us
  transfers between devices with their start and end apart: 33, of which 16 were waited for; matrix products, arithmetic and copies ran while one was open for 10% of the time, Pallas kernels for 58%

profile of v3, /device:TPU:0, one launch (start us, length us, event | category | flops | bytes accessed | tf_op | source)
XLA Modules:
  0.0 450.1 jit_solution(11223411958129818003)
XLA Ops:
  8.5 6.1 %concatenate.104 = f32[1154]{0:T(1024)S(1)} concatenate(bf16[96]{0:T(256)(128)(2,1)} %param.26, bf16[96]{0:T(256)(128)(2,1)} %param.27, bf16[96]{0:T(256)(128)(2,1)} %param.29, bf16[96]{0:T(256)(128)(2,1)} %param.32, bf16[96]{0:T(256)(128)(2,1)} %param.34, bf16[96]{0:T(256)(128)(2,1)} %param.35, bf16[96]{0:T(256)(128)(2,1)} %param.36, bf16[96]{0:T(256)(128)(2,1)} %param.40, ...), dimensions={0} | concatenate | bytes 6928 | tf_op jit(solution)/shard_map/concatenate | solution.py:771
  14.7 3.0 collective-permute-start
  31.7 2.9 collective-permute-start.3
  39.0 2.8 collective-permute-done.4
  42.5 3.0 collective-permute-done.5
  46.1 20.1 %all-gather.4.cloned.1.call-done.mine_ref = bf16[768,1152]{1,0:T(8,128)(2,1)} async-done(((bf16[96,1152]{1,0:T(8,128)(2,1)}), bf16[768,1152]{1,0:T(8,128)(2,1)}) %all-gather.4.cloned.1.call-update) | async-done | bytes 1769488 | tf_op jit(solution)/shard_map/all_gather | solution.py:761
  71.6 15.3 %norm_qkv.1 = (bf16[2,1024,768]{2,1,0:T(8,128)(2,1)}, bf16[2,1024,768]{2,1,0:T(8,128)(2,1)}, bf16[2,1024,768]{2,1,0:T(8,128)(2,1)}, bf16[2,768,1024]{2,1,0:T(8,1...) custom-call(s32[1]{0:T(128)} %bitcast.core_ref, ...), custom_call_target="tpu_custom_call" | custom-call | flops 7247757312 | bytes 30000000 | tf_op jit(solution)/shard_map/norm_qkv/pallas_call | solution.py:102
  88.2 47.0 %attn_fwd.1 = (bf16[2,1024,768]{2,1,0:T(8,128)(2,1)}, f32[2,768,1024]{2,1,0:T(8,128)}, bf16[2,4,12,1024,256]{4,3,2,1,0:T(8,128)(2,1)}, f32[2,4,4,16,256]{4,3,2,1,0:T(8,128)}) custom-call(s32[8]{0:T(128)} %get-tuple-element.295.lo_ref, s32[8]{0:T(128)} %get-tuple-element.294.hi_ref, bf16[2,1024,768]{2,1,0:T(8,128)(2,1)} %get-tuple-element.73.q_ref, ...), custom_call_target="tpu_custom_call" | custom-call | flops 25769803776 | bytes 80000000 | tf_op jit(solution)/shard_map/attn_fwd/pallas_call | solution.py:195
  137.1 51.8 %mlp_first.1 = (bf16[2,1024,768]{2,1,0:T(8,128)(2,1)}, bf16[2,1024,768]{2,1,0:T(8,128)(2,1)}, f32[2,1024,768]{2,1,0:T(8,128)}, bf16[2,1024,768]{2,1,0:T(8,128)(2...) custom-call(s32[1]{0:T(128)} %bitcast.core_ref, bf16[2,1024,768]{2,1,0:T(8,128)(2,1)} %tok_ref.5, ...), custom_call_target="tpu_custom_call" | custom-call | flops 31406948352 | bytes 60000000 | tf_op jit(solution)/shard_map/mlp_first/pallas_call | solution.py:478
  189.0 4.7 %collective-permute-done.7 = bf16[768,1536]{1,0:T(8,128)(2,1)S(1)} collective-permute-done((bf16[768,1536]{1,0:T(8,128)(2,1)}, bf16[768,1536]{1,0:T(8,128)(2,1)S(1)}, u32[]{:S(2)}, u32[]{:S(2)}) %collective-permute-start.7) | collective-permute-done | bytes 2359328 | tf_op jit(solution)/shard_map/ppermute | solution.py:660
  193.7 3.6 add_convert_fusion.1
  197.3 3.8 all-to-all-start
  201.1 55.5 %mlp_second.1 = (bf16[2,1024,768]{2,1,0:T(8,128)(2,1)}, f32[2,1024,768]{2,1,0:T(8,128)}, bf16[2,1024,768]{2,1,0:T(8,128)(2,1)}, bf16[2,768,1024]{2,1,0:T(8,128)(...) custom-call(s32[1]{0:T(128)} %bitcast.core_ref, ...), custom_call_target="tpu_custom_call" | custom-call | flops 33822867456 | bytes 60000000 | tf_op jit(solution)/shard_map/mlp_second/pallas_call | solution.py:506
  262.5 3.4 add_convert_fusion.after_ref
  269.4 5.9 %all-to-all-start.1 = ((bf16[8,104,1920]{2,1,0:T(8,128)(2,1)}), bf16[8,104,1920]{2,1,0:T(8,128)(2,1)S(1)}, u32[]{:S(2)}, u32[]{:S(2)}) async-start(bf16[8,104,1920]{2,1,0:T(8,128)(2,1)} %fusion.1), calls=%async_computation.1 | async-start | bytes 6389760 | tf_op jit(solution)/shard_map/all_to_all | solution.py:712
  275.3 60.1 %attn_bwd.1 = (bf16[2,1024,768]{2,1,0:T(8,128)(2,1)}, bf16[2,1024,768]{2,1,0:T(8,128)(2,1)}, bf16[2,1024,768]{2,1,0:T(8,128)(2,1)}) custom-call(s32[8]{0:T(128)} %get-tuple-element.295.lo_ref, s32[8]{0:T(128)} %get-tuple-element.294.hi_ref, bf16[2,768,1024]{2,1,0:T(8,128)(2,1)} %get-tuple-element.89.qT_ref, bf16[2,768,1024]{2,1,0:T(8,128)(2,1)} %get-tuple-element.90.kT_ref, ...), custom_call_target="tpu_custom_call" | custom-call | flops 51539607552 | bytes 90000000 | tf_op jit(solution)/shard_map/attn_bwd/pallas_call | solution.py:285
  335.4 13.2 %qkv_weights.1 = (bf16[768,1152]{1,0:T(8,128)(2,1)}, bf16[768,1152]{1,0:T(8,128)(2,1)}) custom-call(s32[1]{0:T(128)} %bitcast.core_ref, bf16[2,1024,768]{2,1,0:T(8,128)(2,1)} %get-tuple-element.103.hid_ref, bf16[2,1024,768]{2,1,0:T(8,128)(2,1)} %get-tuple-element.100.dq_ref, bf16[2,1024,768]{2,1,0:T(8,128)(2,1)} %get-tuple-element.101.dk_ref, ...), custom_call_target="tpu_custom_call" | custom-call | flops 7247757312 | bytes 20000000 | tf_op jit(solution)/shard_map/qkv_weights/pallas_call | solution.py:572
  348.7 3.8 collective-permute-done.9
  352.5 3.2 add_convert_fusion.2.after_ref
  357.7 4.8 %all-to-all-start.2 = ((bf16[8,96,1152]{2,1,0:T(8,128)(2,1)}), bf16[8,96,1152]{2,1,0:T(8,128)(2,1)S(1)}, u32[]{:S(2)}, u32[]{:S(2)}) async-start(bf16[8,96,1152]{2,1,0:T(8,128)(2,1)} %bitcast.42), calls=%async_computation.2 | async-start | bytes 3538944 | tf_op jit(solution)/shard_map/all_to_all | solution.py:825
  366.3 17.0 %norm_qkv_back.1 = (bf16[2,1024,768]{2,1,0:T(8,128)(2,1)}, f32[2,1,768]{2,1,0:T(1,128)}, f32[4,768]{1,0:T(4,128)}) custom-call(s32[1]{0:T(128)} %bitcast.core_ref, bf16[2,1024,768]{2,1,0:T(8,128)(2,1)} %tok_ref.5, f32[2,1,768]{2,1,0:T(1,128)} %reshape.352.row_ref, f32[2,1024,768]{2,1,0:T(8,128)} %get-tuple-element.88.gmid_ref, ...), custom_call_target="tpu_custom_call" | custom-call | flops 7247757312 | bytes 40000000 | tf_op jit(solution)/shard_map/norm_qkv_back/pallas_call | solution.py:622
  387.8 16.4 %all-to-all-done.2 = bf16[8,96,1152]{2,1,0:T(8,128)(2,1)S(1)} async-done(((bf16[8,96,1152]{2,1,0:T(8,128)(2,1)}), bf16[8,96,1152]{2,1,0:T(8,128)(2,1)S(1)}, u32[]{:S(2)}, u32[]{:S(2)}) %all-to-all-start.2) | async-done | bytes 1769504 | tf_op jit(solution)/shard_map/all_to_all | solution.py:825
  410.9 2.9 collective-permute-start.14
  434.7 5.6 %collective-permute-done.18 = f32[32,896]{1,0:T(8,128)S(1)} collective-permute-done((f32[32,896]{1,0:T(8,128)S(1)}, f32[32,896]{1,0:T(8,128)S(1)}, u32[]{:S(2)}, u32[]{:S(2)}) %collective-permute-start.18) | collective-permute-done | bytes 114720 | tf_op jit(solution)/shard_map/ppermute | solution.py:677
  (226 shorter events, 79.1 us)
Async XLA Ops:
  7.2 59.1 %all-gather.4.cloned.1.call-start = ((), (), s32[]{:S(2)}) async-start(), calls=%async_computation.3 | async-start | bytes 1990656 | tf_op jit(solution)/shard_map/all_gather | solution.py:761
  14.7 8.0 %collective-permute-start = (f32[1,1154]{1,0:T(1,128)S(1)}, f32[1,1154]{1,0:T(1,128)S(1)}, u32[]{:S(2)}, u32[]{:S(2)}) collective-permute-start(f32[1,1154]{1,0:T(1,128)S(1)} %broadcast_in_dim.14), channel_id=1, source_target_pairs={{0,1},{1,0},{2,3},{3,2},{4,5},{5,4},{6,7},{7,6},{8,9},{9,8},{10,11... | collective-permute-start | bytes 13856 | tf_op jit(solution)/shard_map/ppermute | solution.py:677
  19.5 115.7 %all-gather.6.cloned.1.call-start = ((), (), s32[]{:S(2)}) async-start(), calls=%async_computation.4 | async-start | bytes 6266880 | tf_op jit(solution)/shard_map/all_gather | solution.py:788
  26.5 4.9 %collective-permute-start.2 = (f32[4,1154]{1,0:T(4,128)S(1)}, f32[4,1154]{1,0:T(4,128)S(1)}, u32[]{:S(2)}, u32[]{:S(2)}) collective-permute-start(f32[4,1154]{1,0:T(4,128)S(1)} %pad_maximum_fusion.11), channel_id=1, source_target_pairs={{0,4},{1,5},{2,6},{3,7},{4,0},{5,1},{6,2},{7,3},{8,12},{9,13},{10,... | collective-permute-start | bytes 55400 | tf_op jit(solution)/shard_map/ppermute | solution.py:677
  31.7 6.3 %collective-permute-start.3 = (f32[8,768]{1,0:T(8,128)S(1)}, f32[8,768]{1,0:T(8,128)S(1)}, u32[]{:S(2)}, u32[]{:S(2)}) collective-permute-start(f32[8,768]{1,0:T(8,128)S(1)} %slice_select_fusion), channel_id=1, source_target_pairs={{0,4},{1,5},{2,6},{3,7},{4,0},{5,1},{6,2},{7,3},{8,12},{9,13},{10,... | collective-permute-start | bytes 73736 | tf_op jit(solution)/shard_map/ppermute | solution.py:692
  66.3 134.8 %all-gather.8.cloned.1.call-start = ((), (), s32[]{:S(2)}) async-start(), calls=%async_computation.5 | async-start | bytes 5013504 | tf_op jit(solution)/shard_map/all_gather | solution.py:797
  188.9 4.8 %collective-permute-start.7 = (bf16[768,1536]{1,0:T(8,128)(2,1)}, bf16[768,1536]{1,0:T(8,128)(2,1)S(1)}, u32[]{:S(2)}, u32[]{:S(2)}) collective-permute-start(bf16[768,1536]{1,0:T(8,128)(2,1)} %get-tuple-element.81), channel_id=1, source_target_pairs={{0,8},{8,0},{1,9},{9,1},{2,10},{10,2},{3,11},{11,3},{4,12},{12,4},... | collective-permute-start | bytes 7077896 | tf_op jit(solution)/shard_map/ppermute | solution.py:660
  197.3 59.8 %all-to-all-start = ((bf16[8,96,1536]{2,1,0:T(8,128)(2,1)}), bf16[8,96,1536]{2,1,0:T(8,128)(2,1)S(1)}, u32[]{:S(2)}, u32[]{:S(2)}) async-start(bf16[8,96,1536]{2,1,0:T(8,128)(2,1)} %bitcast.5), calls=%async_computation | async-start | bytes 4718592 | tf_op jit(solution)/shard_map/all_to_all | solution.py:809
  256.6 5.9 %collective-permute-start.8 = (bf16[768,1920]{1,0:T(8,128)(2,1)}, bf16[768,1920]{1,0:T(8,128)(2,1)}, u32[]{:S(2)}, u32[]{:S(2)}) collective-permute-start(bf16[768,1920]{1,0:T(8,128)(2,1)} %get-tuple-element.98), channel_id=1, source_target_pairs={{0,8},{8,0},{1,9},{9,1},{2,10},{10,2},{3,11},{11,3},{4,12},{12,4},... | collective-permute-start | bytes 8847368 | tf_op jit(solution)/shard_map/ppermute | solution.py:660
  269.4 86.3 %all-to-all-start.1 = ((bf16[8,104,1920]{2,1,0:T(8,128)(2,1)}), bf16[8,104,1920]{2,1,0:T(8,128)(2,1)S(1)}, u32[]{:S(2)}, u32[]{:S(2)}) async-start(bf16[8,104,1920]{2,1,0:T(8,128)(2,1)} %fusion.1), calls=%async_computation.1 | async-start | bytes 6389760 | tf_op jit(solution)/shard_map/all_to_all | solution.py:712
  348.6 13.9 %collective-permute-start.25 = (bf16[96,1536]{1,0:T(8,128)(2,1)S(1)}, bf16[96,1536]{1,0:T(8,128)(2,1)}, u32[]{:S(2)}, u32[]{:S(2)}) collective-permute-start(bf16[96,1536]{1,0:T(8,128)(2,1)S(1)} %reduce_sum.77), channel_id=1, source_target_pairs={{0,16},{16,0},{1,17},{17,1},{2,18},{18,2},{3,19},{19,3},{4,20},{20... | collective-permute-start | bytes 884744 | tf_op jit(solution)/shard_map/ppermute | solution.py:667
  357.7 46.5 %all-to-all-start.2 = ((bf16[8,96,1152]{2,1,0:T(8,128)(2,1)}), bf16[8,96,1152]{2,1,0:T(8,128)(2,1)S(1)}, u32[]{:S(2)}, u32[]{:S(2)}) async-start(bf16[8,96,1152]{2,1,0:T(8,128)(2,1)} %bitcast.42), calls=%async_computation.2 | async-start | bytes 3538944 | tf_op jit(solution)/shard_map/all_to_all | solution.py:825
  366.3 18.2 %collective-permute-start.23 = (bf16[96,1920]{1,0:T(8,128)(2,1)S(1)}, bf16[96,1920]{1,0:T(8,128)(2,1)S(1)}, u32[]{:S(2)}, u32[]{:S(2)}) collective-permute-start(bf16[96,1920]{1,0:T(8,128)(2,1)S(1)} %copy-done.6), channel_id=1, source_target_pairs={{0,16},{16,0},{1,17},{17,1},{2,18},{18,2},{3,19},{19,3},{4,20},{20... | collective-permute-start | bytes 1105928 | tf_op jit(solution)/shard_map/ppermute | solution.py:667
  405.2 8.7 %collective-permute-start.10 = (f32[1,3,896]{2,1,0:T(4,128)S(1)}, f32[1,3,896]{2,1,0:T(4,128)S(1)}, u32[]{:S(2)}, u32[]{:S(2)}) collective-permute-start(f32[1,3,896]{2,1,0:T(4,128)S(1)} %get-tuple-element.261), channel_id=1, source_target_pairs={{0,1},{1,0},{2,3},{3,2},{4,5},{5,4},{6,7},{7,6},{8,9},{9,8},{10,11... | collective-permute-start | bytes 32264 | tf_op jit(solution)/shard_map/ppermute | solution.py:721
  407.9 7.4 %collective-permute-start.11 = (f32[1,3,896]{2,1,0:T(4,128)S(1)}, f32[1,3,896]{2,1,0:T(4,128)S(1)}, u32[]{:S(2)}, u32[]{:S(2)}) collective-permute-start(f32[1,3,896]{2,1,0:T(4,128)S(1)} %get-tuple-element.260), channel_id=1, source_target_pairs={{0,2},{1,3},{2,0},{3,1},{4,6},{5,7},{6,4},{7,5},{8,10},{9,11},{10,... | collective-permute-start | bytes 32264 | tf_op jit(solution)/shard_map/ppermute | solution.py:721
  408.0 9.7 %collective-permute-start.12 = (f32[1,3,896]{2,1,0:T(4,128)S(1)}, f32[1,3,896]{2,1,0:T(4,128)S(1)}, u32[]{:S(2)}, u32[]{:S(2)}) collective-permute-start(f32[1,3,896]{2,1,0:T(4,128)S(1)} %get-tuple-element.259), channel_id=1, source_target_pairs={{0,3},{1,2},{2,1},{3,0},{4,7},{5,6},{6,5},{7,4},{8,11},{9,10},{10,... | collective-permute-start | bytes 32264 | tf_op jit(solution)/shard_map/ppermute | solution.py:721
  410.0 7.8 %collective-permute-start.13 = (f32[1,3,896]{2,1,0:T(4,128)S(1)}, f32[1,3,896]{2,1,0:T(4,128)S(1)}, u32[]{:S(2)}, u32[]{:S(2)}) collective-permute-start(f32[1,3,896]{2,1,0:T(4,128)S(1)} %get-tuple-element.258), channel_id=1, source_target_pairs={{0,4},{1,5},{2,6},{3,7},{4,0},{5,1},{6,2},{7,3},{8,12},{9,13},{10,... | collective-permute-start | bytes 32264 | tf_op jit(solution)/shard_map/ppermute | solution.py:721
  410.9 6.9 %collective-permute-start.14 = (f32[1,3,896]{2,1,0:T(4,128)S(1)}, f32[1,3,896]{2,1,0:T(4,128)S(1)}, u32[]{:S(2)}, u32[]{:S(2)}) collective-permute-start(f32[1,3,896]{2,1,0:T(4,128)S(1)} %get-tuple-element.257), channel_id=1, source_target_pairs={{0,5},{1,4},{2,7},{3,6},{4,1},{5,0},{6,3},{7,2},{8,13},{9,12},{10,... | collective-permute-start | bytes 32264 | tf_op jit(solution)/shard_map/ppermute | solution.py:721
  413.8 5.5 %collective-permute-start.15 = (f32[1,3,896]{2,1,0:T(4,128)S(1)}, f32[1,3,896]{2,1,0:T(4,128)S(1)}, u32[]{:S(2)}, u32[]{:S(2)}) collective-permute-start(f32[1,3,896]{2,1,0:T(4,128)S(1)} %get-tuple-element.256), channel_id=1, source_target_pairs={{0,6},{1,7},{2,4},{3,5},{4,2},{5,3},{6,0},{7,1},{8,14},{9,15},{10,... | collective-permute-start | bytes 32264 | tf_op jit(solution)/shard_map/ppermute | solution.py:721
  415.3 6.5 %collective-permute-start.16 = (f32[1,3,896]{2,1,0:T(4,128)S(1)}, f32[1,3,896]{2,1,0:T(4,128)S(1)}, u32[]{:S(2)}, u32[]{:S(2)}) collective-permute-start(f32[1,3,896]{2,1,0:T(4,128)S(1)} %get-tuple-element.255), channel_id=1, source_target_pairs={{0,7},{1,6},{2,5},{3,4},{4,3},{5,2},{6,1},{7,0},{8,15},{9,14},{10,... | collective-permute-start | bytes 32264 | tf_op jit(solution)/shard_map/ppermute | solution.py:721
  424.6 7.9 %collective-permute-start.17 = (f32[16,896]{1,0:T(8,128)}, f32[16,896]{1,0:T(8,128)}, u32[]{:S(2)}, u32[]{:S(2)}) collective-permute-start(f32[16,896]{1,0:T(8,128)} %reshape.369), channel_id=1, source_target_pairs={{0,8},{8,0},{1,9},{9,1},{2,10},{10,2},{3,11},{11,3},{4,12},{12,4},... | collective-permute-start | bytes 172040 | tf_op jit(solution)/shard_map/ppermute | solution.py:677
  425.8 6.7 %collective-permute-start.20 = (f32[1,1152]{1,0:T(1,128)S(1)}, f32[1,1152]{1,0:T(1,128)S(1)}, u32[]{:S(2)}, u32[]{:S(2)}) collective-permute-start(f32[1,1152]{1,0:T(1,128)S(1)} %reshape_add_fusion), channel_id=1, source_target_pairs={{0,16},{16,0},{1,17},{17,1},{2,18},{18,2},{3,19},{19,3},{4,20},{20... | collective-permute-start | bytes 13832 | tf_op jit(solution)/shard_map/ppermute | solution.py:667
  430.5 10.0 %collective-permute-start.21 = (bf16[96,1152]{1,0:T(8,128)(2,1)S(1)}, bf16[96,1152]{1,0:T(8,128)(2,1)S(1)}, u32[]{:S(2)}, u32[]{:S(2)}) collective-permute-start(bf16[96,1152]{1,0:T(8,128)(2,1)S(1)} %copy-done.7), channel_id=1, source_target_pairs={{0,16},{16,0},{1,17},{17,1},{2,18},{18,2},{3,19},{19,3},{4,20},{20... | collective-permute-start | bytes 663560 | tf_op jit(solution)/shard_map/ppermute | solution.py:667
  433.4 6.9 %collective-permute-start.18 = (f32[32,896]{1,0:T(8,128)S(1)}, f32[32,896]{1,0:T(8,128)S(1)}, u32[]{:S(2)}, u32[]{:S(2)}) collective-permute-start(f32[32,896]{1,0:T(8,128)S(1)} %pad_maximum_fusion.9), channel_id=1, source_target_pairs={{0,16},{16,0},{1,17},{17,1},{2,18},{18,2},{3,19},{19,3},{4,20},{20... | collective-permute-start | bytes 344072 | tf_op jit(solution)/shard_map/ppermute | solution.py:677
  (27 other events, 285.2 us)
Sparse Core Ops, SparseCore 0:
  19.6 46.6 all-gather.3
  69.1 58.7 all-gather.5
  135.4 51.2 all-gather.7

commit v4 on v3

--- a/solution.py
+++ b/solution.py
@@ -798,11 +798,13 @@
     def core_sum(keep, send):
         return (keep.astype(f32) + swap(send, "core").astype(f32)).astype(bf16)
 
+    def two(half, other):
+        half, other = half.astype(f32), other.astype(f32)
+        return jnp.where(core == 0, half, other), jnp.where(core == 0, other, half)
+
     def finish(part):
-        half = all_sum(part, "xrep").astype(bf16)
-        other = swap(half, "core").astype(f32)
-        half = half.astype(f32)
-        return jnp.where(core == 0, half, other), jnp.where(core == 0, other, half)
+        half = all_sum(part, "xrep")
+        return two(half, swap(half, "core"))
 
     acc, gh2, mid, hid, bupg_a, keep, send = mlp_first(core1, tokens, trow, cot, mixed, vec2, bup[:, :H], w_a)
     half_a = core_sum(keep, send)
@@ -819,7 +821,11 @@
     vectors = jnp.concatenate([vecg2[i].reshape(n, own) for i in range(4)] + [bupg], axis=1)
     part_b, came_b = exchange_reduce(half_b, split_rows(vectors[:, None], half_b.shape[1]), "shard")
     dq, dk, dv = attn_bwd(lo, hi, qT, kT, v, gmix, gmixT, mixedT, prob, fac, half_b)
+    part_a = all_sum(part_a, "xrep")
+    dq, part_a = lax.optimization_barrier((dq, part_a))
+    other_a = swap(part_a, "core")
     keep, send = qkv_weights_call(core1, hid1, dq, dk, dv)
+    keep, other_a = lax.optimization_barrier((keep, other_a))
     qkv_half = core_sum(keep, send)
     qkv_half, part_b, came_b = lax.optimization_barrier((qkv_half, part_b, came_b))
     came = lax.all_to_all(qkv_half, "shard", 0, 0, tiled=True).reshape(n, own, 3 * hd)
@@ -827,30 +833,35 @@
     gin, rsum, vecg1 = qkv_back_call(
         core1, tokens, trow, gmid, dq, dk, dv, vec1, qkv_mine, qkv_other, qkv_half
     )
+    part_b, part_a, other_a, vecg1 = lax.optimization_barrier((part_b, part_a, other_a, vecg1))
     vectors = jnp.concatenate([vecg1[i].reshape(n, own) for i in range(4)], axis=1)
-    wide = -(-(D + 2) // 128) * 128
+    thick = -(-(D + 2) // 128) * 128
     digits = jnp.stack([timesteps // 32, timesteps % 32], axis=1).astype(f32)
     table_rows = jnp.concatenate([rsum.reshape(B, D), digits], axis=1)
-    table_rows = jnp.broadcast_to(jnp.pad(table_rows, ((0, 0), (0, wide - D - 2)))[None], (n, B, wide))
-    extra = jnp.concatenate([jnp.pad(vectors, ((0, 0), (0, wide - 4 * own)))[:, None], table_rows], axis=1)
-    extra, qkv_part = lax.optimization_barrier((extra, qkv_part))
-    came_q = direct_exchange(extra, "shard")
+    table_rows = jnp.broadcast_to(jnp.pad(table_rows, ((0, 0), (0, thick - D - 2)))[None], (n, B, thick))
+    vectors = jnp.pad(vectors, ((0, 0), (0, thick - 4 * own)))[:, None]
+    came_q = direct_exchange(jnp.concatenate([table_rows, vectors], axis=1), "shard")
+    came_q, qkv_part = lax.optimization_barrier((came_q, qkv_part))
 
     vg_b = jnp.sum(came_b[:, :2], axis=(0, 1))[: 4 * own + FF // n]
-    vg_q = jnp.sum(came_q[:, 0], axis=0)[: 4 * own]
-    vg = all_sum(all_sum(jnp.concatenate([vg_q, vg_b])[None], "core"), "xrep").reshape(-1)
-    g_bup = vg[8 * own :]
-    vg = [vg[i * own : (i + 1) * own] for i in range(8)]
-    sums = came_q[:, 1:].reshape(n * B, wide)
+    vg_q = jnp.sum(came_q[:, B], axis=0)[: 4 * own]
+    vg = jnp.concatenate([vg_q, vg_b])
+    lines = -(-vg.shape[0] // thick)
+    vg = jnp.pad(vg, (0, lines * thick - vg.shape[0])).reshape(lines, thick)
+    sums = jnp.concatenate([came_q[:, :B].reshape(n * B, thick), vg], axis=0)[None]
     for axis in ("core", "xrep"):
         sums = gather_small(sums, axis)
+    vg = jnp.sum(sums[:, n * B :], axis=0).reshape(-1)
+    sums = sums[:, : n * B].reshape(-1, thick)
+    g_bup = vg[8 * own : 8 * own + FF // n]
+    vg = [vg[i * own : (i + 1) * own] for i in range(8)]
     own_rows = step_table.shape[0]
     rows = me * own_rows + lax.broadcasted_iota(jnp.int32, (own_rows, 1), 0)
     steps = 32 * sums[:, D] + sums[:, D + 1]
     match = (rows == steps.astype(jnp.int32)[None, :]).astype(f32)
     g_table = jnp.dot(match, sums[:, :D], precision=lax.Precision.HIGHEST, preferred_element_type=f32)
 
-    a_up, a_down = finish(part_a)
+    a_up, a_down = two(part_a, other_a)
     b_up_, b_down_ = finish(part_b)
     g_up = jnp.concatenate([a_up, b_up_[:, :H]], axis=1)
     g_up = g_up.reshape(own, J, n, 2, thin).transpose(0, 2, 3, 1, 4).reshape(own, FF)

time: 458 us -> 444 us (0.969)
  Pallas kernels: 260 us -> 241 us
  starting transfers between devices: 40.8 us -> 58.9 us
  waiting for transfers between devices: 72.3 us -> 58.7 us
    all_to_all x1, waiting for transfers between devices: 16.4 us -> 0.01 us  [on_device(): lax.all_to_all(qkv_half, 'shard', 0, 0, tiled=True).reshape(n, own, 3 * hd)]
    pallas_call x1, Pallas kernels: 60.1 us -> 49.4 us  [attn_bwd(): pl.pallas_call(bwd_kernel, grid_spec=pltpu.PrefetchScalarGridSpec(num_sca...]
    all_to_all x1, starting transfers between devices: 4.79 us -> 15.2 us  [on_device(): lax.all_to_all(qkv_half, 'shard', 0, 0, tiled=True).reshape(n, own, 3 * hd)]
    pallas_call x1, Pallas kernels: 47 us -> 38.6 us  [attn_fwd(): pl.pallas_call(fwd_kernel, grid_spec=pltpu.PrefetchScalarGridSpec(num_sca...]
    ppermute x5, waiting for transfers between devices: 9.89 us -> 4.29 us  [gather_small(): came = lax.ppermute(array, axis, [(i, i ^ step) for i in range(size)])]
    ppermute x7, waiting for transfers between devices: 3.98 us -> 9.39 us  [direct_exchange(): lax.ppermute(own_slice(array, me ^ r, 1, 0), axis, [(i, i ^ r) for i in r...]
    all_to_all x1, starting transfers between devices: 3.79 us -> 8.68 us  [on_device(): lax.all_to_all(half_a, 'shard', 0, 0, tiled=True).reshape(n, own, H)]
  transfers between devices with their start and end apart: 33 -> 31, of which waited for: 16 -> 17; matrix products, arithmetic and copies ran while one was open for 10% -> 10% of each run, Pallas kernels for 58% -> 55%
where the time goes in v4:
time: 444 us; the launch traced here: 438 us
  Pallas kernels  241 us (54%)
  starting transfers between devices  58.9 us (13%)
  waiting for transfers between devices  58.7 us (13%)
  other arithmetic  33.8 us (8%)
  local copies, waits for them, and re-layouts  30.1 us (7%)
  between operations  15.1 us (3%)
    pallas_call x1, Pallas kernels, mlp_second(): pl.pallas_call(mlp_second_kernel, grid=(B * S // MT2,), in_specs=[smem] +...  55.5 us
    pallas_call x1, Pallas kernels, mlp_first(): pl.pallas_call(mlp_first_kernel, grid=(B * S // MT,), in_specs=[smem, row...  51.6 us
    pallas_call x1, Pallas kernels, attn_bwd(): pl.pallas_call(bwd_kernel, grid_spec=pltpu.PrefetchScalarGridSpec(num_sca...  49.4 us
    pallas_call x1, Pallas kernels, attn_fwd(): pl.pallas_call(fwd_kernel, grid_spec=pltpu.PrefetchScalarGridSpec(num_sca...  38.6 us
    all_gather x1, waiting for transfers between devices, on_device(): qkv_mine = lax.all_gather(qkv_local, 'shard', axis=0, tiled=True)  20.1 us
    pallas_call x1, Pallas kernels, qkv_back_call(): pl.pallas_call(qkv_back_kernel, grid=(B, S // RT), in_specs=[pl.BlockSpec...  17 us
    pallas_call x1, Pallas kernels, qkv_call(): pl.pallas_call(qkv_kernel, grid=(B, S // RT), in_specs=[pl.BlockSpec(memo...  15.3 us
    all_to_all x1, starting transfers between devices, on_device(): lax.all_to_all(qkv_half, 'shard', 0, 0, tiled=True).reshape(n, own, 3 * hd)  15.2 us
  transfers between devices with their start and end apart: 31, of which 17 were waited for; matrix products, arithmetic and copies ran while one was open for 10% of the time, Pallas kernels for 55%

profile of v4, /device:TPU:0, one launch (start us, length us, event | category | flops | bytes accessed | tf_op | source)
XLA Modules:
  0.0 438.3 jit_solution(4786003637752188553)
XLA Ops:
  8.5 6.1 %concatenate.107 = f32[1154]{0:T(1024)S(1)} concatenate(bf16[96]{0:T(256)(128)(2,1)} %param.26, bf16[96]{0:T(256)(128)(2,1)} %param.27, bf16[96]{0:T(256)(128)(2,1)} %param.29, bf16[96]{0:T(256)(128)(2,1)} %param.32, bf16[96]{0:T(256)(128)(2,1)} %param.34, bf16[96]{0:T(256)(128)(2,1)} %param.35, bf16[96]{0:T(256)(128)(2,1)} %param.36, bf16[96]{0:T(256)(128)(2,1)} %param.40, ...), dimensions={0} | concatenate | bytes 6928 | tf_op jit(solution)/shard_map/concatenate | solution.py:771
  14.7 3.0 collective-permute-start
  31.7 2.9 collective-permute-start.3
  39.0 2.8 collective-permute-done.4
  42.5 3.0 collective-permute-done.5
  46.1 20.1 %all-gather.4.cloned.1.call-done.mine_ref = bf16[768,1152]{1,0:T(8,128)(2,1)} async-done(((bf16[96,1152]{1,0:T(8,128)(2,1)}), bf16[768,1152]{1,0:T(8,128)(2,1)}) %all-gather.4.cloned.1.call-update) | async-done | bytes 1769488 | tf_op jit(solution)/shard_map/all_gather | solution.py:761
  71.5 15.3 %norm_qkv.1 = (bf16[2,1024,768]{2,1,0:T(8,128)(2,1)}, bf16[2,1024,768]{2,1,0:T(8,128)(2,1)}, bf16[2,1024,768]{2,1,0:T(8,128)(2,1)}, bf16[2,768,1024]{2,1,0:T(8,1...) custom-call(s32[1]{0:T(128)} %bitcast.core_ref, ...), custom_call_target="tpu_custom_call" | custom-call | flops 7247757312 | bytes 30000000 | tf_op jit(solution)/shard_map/norm_qkv/pallas_call | solution.py:102
  88.2 38.6 %attn_fwd.1 = (bf16[2,1024,768]{2,1,0:T(8,128)(2,1)}, f32[2,768,1024]{2,1,0:T(8,128)}, bf16[2,4,12,1024,256]{4,3,2,1,0:T(8,128)(2,1)}, f32[2,4,4,16,256]{4,3,2,1,0:T(8,128)}) custom-call(s32[8]{0:T(128)} %get-tuple-element.311.lo_ref, s32[8]{0:T(128)} %get-tuple-element.310.hi_ref, bf16[2,1024,768]{2,1,0:T(8,128)(2,1)} %get-tuple-element.81.q_ref, ...), custom_call_target="tpu_custom_call" | custom-call | flops 25769803776 | bytes 80000000 | tf_op jit(solution)/shard_map/attn_fwd/pallas_call | solution.py:195
  129.7 51.6 %mlp_first.1 = (bf16[2,1024,768]{2,1,0:T(8,128)(2,1)}, bf16[2,1024,768]{2,1,0:T(8,128)(2,1)}, f32[2,1024,768]{2,1,0:T(8,128)}, bf16[2,1024,768]{2,1,0:T(8,128)(2...) custom-call(s32[1]{0:T(128)} %bitcast.core_ref, bf16[2,1024,768]{2,1,0:T(8,128)(2,1)} %tok_ref.5, ...), custom_call_target="tpu_custom_call" | custom-call | flops 31406948352 | bytes 60000000 | tf_op jit(solution)/shard_map/mlp_first/pallas_call | solution.py:478
  181.8 4.6 %collective-permute-done.7 = bf16[768,1536]{1,0:T(8,128)(2,1)S(1)} collective-permute-done((bf16[768,1536]{1,0:T(8,128)(2,1)}, bf16[768,1536]{1,0:T(8,128)(2,1)S(1)}, u32[]{:S(2)}, u32[]{:S(2)}) %collective-permute-start.7) | collective-permute-done | bytes 2359328 | tf_op jit(solution)/shard_map/ppermute | solution.py:660
  186.4 3.6 add_convert_fusion.1
  190.1 8.7 %all-to-all-start = ((bf16[8,96,1536]{2,1,0:T(8,128)(2,1)}), bf16[8,96,1536]{2,1,0:T(8,128)(2,1)S(1)}, u32[]{:S(2)}, u32[]{:S(2)}) async-start(bf16[8,96,1536]{2,1,0:T(8,128)(2,1)} %bitcast.5), calls=%async_computation | async-start | bytes 4718592 | tf_op jit(solution)/shard_map/all_to_all | solution.py:811
  198.8 55.5 %mlp_second.1 = (bf16[2,1024,768]{2,1,0:T(8,128)(2,1)}, f32[2,1024,768]{2,1,0:T(8,128)}, bf16[2,1024,768]{2,1,0:T(8,128)(2,1)}, bf16[2,768,1024]{2,1,0:T(8,128)(...) custom-call(s32[1]{0:T(128)} %bitcast.core_ref, ...), custom_call_target="tpu_custom_call" | custom-call | flops 33822867456 | bytes 60000000 | tf_op jit(solution)/shard_map/mlp_second/pallas_call | solution.py:506
  260.1 3.4 add_convert_fusion.after_ref
  267.0 6.0 %all-to-all-start.1 = ((bf16[8,104,1920]{2,1,0:T(8,128)(2,1)}), bf16[8,104,1920]{2,1,0:T(8,128)(2,1)S(1)}, u32[]{:S(2)}, u32[]{:S(2)}) async-start(bf16[8,104,1920]{2,1,0:T(8,128)(2,1)} %fusion.1), calls=%async_computation.1 | async-start | bytes 6389760 | tf_op jit(solution)/shard_map/all_to_all | solution.py:712
  274.5 49.4 %attn_bwd.1 = (bf16[2,1024,768]{2,1,0:T(8,128)(2,1)}, bf16[2,1024,768]{2,1,0:T(8,128)(2,1)}, bf16[2,1024,768]{2,1,0:T(8,128)(2,1)}) custom-call(s32[8]{0:T(128)} %get-tuple-element.311.lo_ref, s32[8]{0:T(128)} %get-tuple-element.310.hi_ref, bf16[2,768,1024]{2,1,0:T(8,128)(2,1)} %get-tuple-element.97.qT_ref, bf16[2,768,1024]{2,1,0:T(8,128)(2,1)} %get-tuple-element.98.kT_ref, ...), custom_call_target="tpu_custom_call" | custom-call | flops 51539607552 | bytes 90000000 | tf_op jit(solution)/shard_map/attn_bwd/pallas_call | solution.py:285
  324.0 13.2 %qkv_weights.1 = (bf16[768,1152]{1,0:T(8,128)(2,1)}, bf16[768,1152]{1,0:T(8,128)(2,1)}) custom-call(s32[1]{0:T(128)} %bitcast.core_ref, bf16[2,1024,768]{2,1,0:T(8,128)(2,1)} %get-tuple-element.113.hid_ref, bf16[2,1024,768]{2,1,0:T(8,128)(2,1)} %get-tuple-element.110.dq_ref, bf16[2,1024,768]{2,1,0:T(8,128)(2,1)} %get-tuple-element.111.dk_ref, ...), custom_call_target="tpu_custom_call" | custom-call | flops 7247757312 | bytes 20000000 | tf_op jit(solution)/shard_map/qkv_weights/pallas_call | solution.py:572
  338.0 3.1 collective-permute-done.10
  341.7 3.6 add_convert_fusion.2.after_ref
  347.3 15.2 %all-to-all-start.2 = ((bf16[8,96,1152]{2,1,0:T(8,128)(2,1)}), bf16[8,96,1152]{2,1,0:T(8,128)(2,1)S(1)}, u32[]{:S(2)}, u32[]{:S(2)}) async-start(bf16[8,96,1152]{2,1,0:T(8,128)(2,1)} %bitcast.33), calls=%async_computation.2 | async-start | bytes 3538944 | tf_op jit(solution)/shard_map/all_to_all | solution.py:831
  362.5 17.0 %norm_qkv_back.1 = (bf16[2,1024,768]{2,1,0:T(8,128)(2,1)}, f32[2,1,768]{2,1,0:T(1,128)}, f32[4,768]{1,0:T(4,128)}) custom-call(s32[1]{0:T(128)} %bitcast.core_ref, bf16[2,1024,768]{2,1,0:T(8,128)(2,1)} %tok_ref.5, f32[2,1,768]{2,1,0:T(1,128)} %reshape.351.row_ref, f32[2,1024,768]{2,1,0:T(8,128)} %get-tuple-element.96.gmid_ref, ...), custom_call_target="tpu_custom_call" | custom-call | flops 7247757312 | bytes 40000000 | tf_op jit(solution)/shard_map/norm_qkv_back/pallas_call | solution.py:622
  381.7 3.9 collective-permute-start.16
  398.5 7.9 %collective-permute-done.15 = f32[1,3,896]{2,1,0:T(4,128)S(1)} collective-permute-done((f32[1,3,896]{2,1,0:T(4,128)S(1)}, f32[1,3,896]{2,1,0:T(4,128)S(1)}, u32[]{:S(2)}, u32[]{:S(2)}) %collective-permute-start.15) | collective-permute-done | bytes 10784 | tf_op jit(solution)/shard_map/ppermute | solution.py:721
  426.0 2.8 collective-permute-done.21
  (240 shorter events, 81.9 us)
Async XLA Ops:
  7.2 59.1 %all-gather.4.cloned.1.call-start = ((), (), s32[]{:S(2)}) async-start(), calls=%async_computation.3 | async-start | bytes 1990656 | tf_op jit(solution)/shard_map/all_gather | solution.py:761
  14.7 8.0 %collective-permute-start = (f32[1,1154]{1,0:T(1,128)S(1)}, f32[1,1154]{1,0:T(1,128)S(1)}, u32[]{:S(2)}, u32[]{:S(2)}) collective-permute-start(f32[1,1154]{1,0:T(1,128)S(1)} %broadcast_in_dim.14), channel_id=1, source_target_pairs={{0,1},{1,0},{2,3},{3,2},{4,5},{5,4},{6,7},{7,6},{8,9},{9,8},{10,11... | collective-permute-start | bytes 13856 | tf_op jit(solution)/shard_map/ppermute | solution.py:677
  19.5 108.4 %all-gather.6.cloned.1.call-start = ((), (), s32[]{:S(2)}) async-start(), calls=%async_computation.4 | async-start | bytes 6266880 | tf_op jit(solution)/shard_map/all_gather | solution.py:788
  26.5 4.9 %collective-permute-start.2 = (f32[4,1154]{1,0:T(4,128)S(1)}, f32[4,1154]{1,0:T(4,128)S(1)}, u32[]{:S(2)}, u32[]{:S(2)}) collective-permute-start(f32[4,1154]{1,0:T(4,128)S(1)} %pad_maximum_fusion.9), channel_id=1, source_target_pairs={{0,4},{1,5},{2,6},{3,7},{4,0},{5,1},{6,2},{7,3},{8,12},{9,13},{10,... | collective-permute-start | bytes 55400 | tf_op jit(solution)/shard_map/ppermute | solution.py:677
  31.7 6.3 %collective-permute-start.3 = (f32[8,768]{1,0:T(8,128)S(1)}, f32[8,768]{1,0:T(8,128)S(1)}, u32[]{:S(2)}, u32[]{:S(2)}) collective-permute-start(f32[8,768]{1,0:T(8,128)S(1)} %slice_select_fusion), channel_id=1, source_target_pairs={{0,4},{1,5},{2,6},{3,7},{4,0},{5,1},{6,2},{7,3},{8,12},{9,13},{10,... | collective-permute-start | bytes 73736 | tf_op jit(solution)/shard_map/ppermute | solution.py:692
  66.3 132.5 %all-gather.8.cloned.1.call-start = ((), (), s32[]{:S(2)}) async-start(), calls=%async_computation.5 | async-start | bytes 5013504 | tf_op jit(solution)/shard_map/all_gather | solution.py:797
  181.3 5.1 %collective-permute-start.7 = (bf16[768,1536]{1,0:T(8,128)(2,1)}, bf16[768,1536]{1,0:T(8,128)(2,1)S(1)}, u32[]{:S(2)}, u32[]{:S(2)}) collective-permute-start(bf16[768,1536]{1,0:T(8,128)(2,1)} %get-tuple-element.89), channel_id=1, source_target_pairs={{0,8},{8,0},{1,9},{9,1},{2,10},{10,2},{3,11},{11,3},{4,12},{12,4},... | collective-permute-start | bytes 7077896 | tf_op jit(solution)/shard_map/ppermute | solution.py:660
  190.1 64.7 %all-to-all-start = ((bf16[8,96,1536]{2,1,0:T(8,128)(2,1)}), bf16[8,96,1536]{2,1,0:T(8,128)(2,1)S(1)}, u32[]{:S(2)}, u32[]{:S(2)}) async-start(bf16[8,96,1536]{2,1,0:T(8,128)(2,1)} %bitcast.5), calls=%async_computation | async-start | bytes 4718592 | tf_op jit(solution)/shard_map/all_to_all | solution.py:811
  254.3 5.8 %collective-permute-start.8 = (bf16[768,1920]{1,0:T(8,128)(2,1)}, bf16[768,1920]{1,0:T(8,128)(2,1)}, u32[]{:S(2)}, u32[]{:S(2)}) collective-permute-start(bf16[768,1920]{1,0:T(8,128)(2,1)} %get-tuple-element.106), channel_id=1, source_target_pairs={{0,8},{8,0},{1,9},{9,1},{2,10},{10,2},{3,11},{11,3},{4,12},{12,4},... | collective-permute-start | bytes 8847368 | tf_op jit(solution)/shard_map/ppermute | solution.py:660
  267.0 78.3 %all-to-all-start.1 = ((bf16[8,104,1920]{2,1,0:T(8,128)(2,1)}), bf16[8,104,1920]{2,1,0:T(8,128)(2,1)S(1)}, u32[]{:S(2)}, u32[]{:S(2)}) async-start(bf16[8,104,1920]{2,1,0:T(8,128)(2,1)} %fusion.1), calls=%async_computation.1 | async-start | bytes 6389760 | tf_op jit(solution)/shard_map/all_to_all | solution.py:712
  273.0 50.8 %collective-permute-start.9 = (bf16[96,1536]{1,0:T(8,128)(2,1)S(1)}, bf16[96,1536]{1,0:T(8,128)(2,1)S(1)}, u32[]{:S(2)}, u32[]{:S(2)}) collective-permute-start(bf16[96,1536]{1,0:T(8,128)(2,1)S(1)} %reduce_sum.86), channel_id=1, source_target_pairs={{0,16},{16,0},{1,17},{17,1},{2,18},{18,2},{3,19},{19,3},{4,20},{20... | collective-permute-start | bytes 884744 | tf_op jit(solution)/shard_map/ppermute | solution.py:667
  337.2 4.5 %collective-permute-start.11 = (bf16[768,1152]{1,0:T(8,128)(2,1)}, bf16[768,1152]{1,0:T(8,128)(2,1)}, u32[]{:S(2)}, u32[]{:S(2)}) collective-permute-start(bf16[768,1152]{1,0:T(8,128)(2,1)} %get-tuple-element.117), channel_id=1, source_target_pairs={{0,8},{8,0},{1,9},{9,1},{2,10},{10,2},{3,11},{11,3},{4,12},{12,4},... | collective-permute-start | bytes 5308424 | tf_op jit(solution)/shard_map/ppermute | solution.py:660
  347.3 61.4 %all-to-all-start.2 = ((bf16[8,96,1152]{2,1,0:T(8,128)(2,1)}), bf16[8,96,1152]{2,1,0:T(8,128)(2,1)S(1)}, u32[]{:S(2)}, u32[]{:S(2)}) async-start(bf16[8,96,1152]{2,1,0:T(8,128)(2,1)} %bitcast.33), calls=%async_computation.2 | async-start | bytes 3538944 | tf_op jit(solution)/shard_map/all_to_all | solution.py:831
  379.6 18.8 %collective-permute-start.23 = (bf16[96,1920]{1,0:T(8,128)(2,1)S(1)}, bf16[96,1920]{1,0:T(8,128)(2,1)S(1)}, u32[]{:S(2)}, u32[]{:S(2)}) collective-permute-start(bf16[96,1920]{1,0:T(8,128)(2,1)S(1)} %copy-done.6), channel_id=1, source_target_pairs={{0,16},{16,0},{1,17},{17,1},{2,18},{18,2},{3,19},{19,3},{4,20},{20... | collective-permute-start | bytes 1105928 | tf_op jit(solution)/shard_map/ppermute | solution.py:667
  381.7 25.4 %collective-permute-start.16 = (f32[1,3,896]{2,1,0:T(4,128)S(1)}, f32[1,3,896]{2,1,0:T(4,128)S(1)}, u32[]{:S(2)}, u32[]{:S(2)}) collective-permute-start(f32[1,3,896]{2,1,0:T(4,128)S(1)} %get-tuple-element.278), channel_id=1, source_target_pairs={{0,5},{1,4},{2,7},{3,6},{4,1},{5,0},{6,3},{7,2},{8,13},{9,12},{10,... | collective-permute-start | bytes 32264 | tf_op jit(solution)/shard_map/ppermute | solution.py:721
  385.6 6.8 %collective-permute-start.12 = (f32[1,3,896]{2,1,0:T(4,128)S(1)}, f32[1,3,896]{2,1,0:T(4,128)S(1)}, u32[]{:S(2)}, u32[]{:S(2)}) collective-permute-start(f32[1,3,896]{2,1,0:T(4,128)S(1)} %get-tuple-element.273), channel_id=1, source_target_pairs={{0,1},{1,0},{2,3},{3,2},{4,5},{5,4},{6,7},{7,6},{8,9},{9,8},{10,11... | collective-permute-start | bytes 32264 | tf_op jit(solution)/shard_map/ppermute | solution.py:721
  386.3 7.6 %collective-permute-start.13 = (f32[1,3,896]{2,1,0:T(4,128)S(1)}, f32[1,3,896]{2,1,0:T(4,128)S(1)}, u32[]{:S(2)}, u32[]{:S(2)}) collective-permute-start(f32[1,3,896]{2,1,0:T(4,128)S(1)} %get-tuple-element.274), channel_id=1, source_target_pairs={{0,2},{1,3},{2,0},{3,1},{4,6},{5,7},{6,4},{7,5},{8,10},{9,11},{10,... | collective-permute-start | bytes 32264 | tf_op jit(solution)/shard_map/ppermute | solution.py:721
  387.7 8.7 %collective-permute-start.14 = (f32[1,3,896]{2,1,0:T(4,128)S(1)}, f32[1,3,896]{2,1,0:T(4,128)S(1)}, u32[]{:S(2)}, u32[]{:S(2)}) collective-permute-start(f32[1,3,896]{2,1,0:T(4,128)S(1)} %get-tuple-element.275), channel_id=1, source_target_pairs={{0,3},{1,2},{2,1},{3,0},{4,7},{5,6},{6,5},{7,4},{8,11},{9,10},{10,... | collective-permute-start | bytes 32264 | tf_op jit(solution)/shard_map/ppermute | solution.py:721
  392.4 13.9 %collective-permute-start.15 = (f32[1,3,896]{2,1,0:T(4,128)S(1)}, f32[1,3,896]{2,1,0:T(4,128)S(1)}, u32[]{:S(2)}, u32[]{:S(2)}) collective-permute-start(f32[1,3,896]{2,1,0:T(4,128)S(1)} %get-tuple-element.276), channel_id=1, source_target_pairs={{0,4},{1,5},{2,6},{3,7},{4,0},{5,1},{6,2},{7,3},{8,12},{9,13},{10,... | collective-permute-start | bytes 32264 | tf_op jit(solution)/shard_map/ppermute | solution.py:721
  393.8 13.3 %collective-permute-start.17 = (f32[1,3,896]{2,1,0:T(4,128)S(1)}, f32[1,3,896]{2,1,0:T(4,128)S(1)}, u32[]{:S(2)}, u32[]{:S(2)}) collective-permute-start(f32[1,3,896]{2,1,0:T(4,128)S(1)} %get-tuple-element.277), channel_id=1, source_target_pairs={{0,6},{1,7},{2,4},{3,5},{4,2},{5,3},{6,0},{7,1},{8,14},{9,15},{10,... | collective-permute-start | bytes 32264 | tf_op jit(solution)/shard_map/ppermute | solution.py:721
  396.4 10.8 %collective-permute-start.18 = (f32[1,3,896]{2,1,0:T(4,128)S(1)}, f32[1,3,896]{2,1,0:T(4,128)S(1)}, u32[]{:S(2)}, u32[]{:S(2)}) collective-permute-start(f32[1,3,896]{2,1,0:T(4,128)S(1)} %get-tuple-element.271), channel_id=1, source_target_pairs={{0,7},{1,6},{2,5},{3,4},{4,3},{5,2},{6,1},{7,0},{8,15},{9,14},{10,... | collective-permute-start | bytes 32264 | tf_op jit(solution)/shard_map/ppermute | solution.py:721
  398.4 8.8 %collective-permute-start.24 = (bf16[96,1920]{1,0:T(8,128)(2,1)S(1)}, bf16[96,1920]{1,0:T(8,128)(2,1)S(1)}, u32[]{:S(2)}, u32[]{:S(2)}) collective-permute-start(bf16[96,1920]{1,0:T(8,128)(2,1)S(1)} %add_convert_fusion.3), channel_id=1, source_target_pairs={{0,8},{8,0},{1,9},{9,1},{2,10},{10,2},{3,11},{11,3},{4,12},{12,4},... | collective-permute-start | bytes 1105928 | tf_op jit(solution)/shard_map/ppermute | solution.py:660
  412.0 11.0 %collective-permute-start.20 = (f32[2,18,896]{2,1,0:T(8,128)}, f32[2,18,896]{2,1,0:T(8,128)}, u32[]{:S(2)}, u32[]{:S(2)}) collective-permute-start(f32[2,18,896]{2,1,0:T(8,128)} %pad_maximum_fusion.6), channel_id=1, source_target_pairs={{0,16},{16,0},{1,17},{17,1},{2,18},{18,2},{3,19},{19,3},{4,20},{20... | collective-permute-start | bytes 387080 | tf_op jit(solution)/shard_map/ppermute | solution.py:677
  421.0 7.8 %collective-permute-start.21 = (bf16[96,1152]{1,0:T(8,128)(2,1)S(1)}, bf16[96,1152]{1,0:T(8,128)(2,1)S(1)}, u32[]{:S(2)}, u32[]{:S(2)}) collective-permute-start(bf16[96,1152]{1,0:T(8,128)(2,1)S(1)} %copy-done.9), channel_id=1, source_target_pairs={{0,16},{16,0},{1,17},{17,1},{2,18},{18,2},{3,19},{19,3},{4,20},{20... | collective-permute-start | bytes 663560 | tf_op jit(solution)/shard_map/ppermute | solution.py:667
  (33 other events, 328.0 us)
Sparse Core Ops, SparseCore 0:
  19.6 46.6 all-gather.3
  69.1 58.7 all-gather.5
  130.8 56.3 all-gather.7

commit v5 on v4

--- a/solution.py
+++ b/solution.py
@@ -127,6 +127,7 @@
 
 SAVED = True
 HPAD = 16
+HROWS = HD + 16
 
 
 def masked_heads(block):
@@ -134,14 +135,14 @@
 
 
 def fwd_kernel(lo_ref, hi_ref, q_ref, k_ref, vT_ref, segk_ref, segq_ref,
-               mixed_ref, mixedT_ref, prob_ref, fac_ref, acc, mrow, lrow):
+               mixed_ref, mixedT_ref, prob_ref, fac_ref, acc, mrow):
     b = pl.program_id(0)
     i = pl.program_id(1)
     nq = pl.num_programs(1)
     segq = segq_ref[0]
     acc[...] = jnp.zeros_like(acc)
     mrow[...] = jnp.full_like(mrow, NEG)
-    lrow[...] = jnp.zeros_like(lrow)
+    ones = jnp.ones((HROWS - HD, KT), bf16)
 
     def body(c, carry):
         c0 = pl.multiple_of(c * KT, KT)
@@ -166,22 +167,23 @@
                 p = jnp.exp2(s - m_new)
                 alpha = jnp.exp2(m_old - m_new)
                 mrow[h : h + 1, :] = m_new
-                lrow[h : h + 1, :] = lrow[h : h + 1, :] * alpha + jnp.sum(p, axis=0, keepdims=True)
                 pb = p.astype(bf16)
                 prob_ref[0, 0, h, pl.ds(c0, KT), :] = pb
-                acc[rows, :] = acc[rows, :] * alpha + dg(vT_ref[0, rows, pl.ds(c0, KT)], pb, 1, 0)
+                values = jnp.concatenate([vT_ref[0, rows, pl.ds(c0, KT)], ones], axis=0)
+                held = slice(h * HROWS, h * HROWS + HD + 8)
+                acc[held, :] = acc[held, :] * alpha + dg(values, pb, 1, 0)[: HD + 8]
         fac_ref[0, 0, c] = mrow[...]
         return carry
 
     lax.fori_loop(lo_ref[b * nq + i], hi_ref[b * nq + i], body, 0)
-    total = lrow[0:HEADS, :]
+    total = jnp.concatenate([acc[h * HROWS + HD : h * HROWS + HD + 1, :] for h in range(HEADS)], axis=0)
     inv = 1.0 / total
     lse = mrow[0:HEADS, :] + jnp.log2(total)
     for c in range(fac_ref.shape[2]):
         fac_ref[0, 0, c, 0:HEADS, :] = jnp.exp2(fac_ref[0, 0, c, 0:HEADS, :] - lse)
     for h in range(HEADS):
         rows = slice(h * HD, (h + 1) * HD)
-        mixedT_ref[0, rows, :] = acc[rows, :] * inv[h : h + 1, :]
+        mixedT_ref[0, rows, :] = acc[h * HROWS : h * HROWS + HD, :] * inv[h : h + 1, :]
     mixed_ref[0] = mixedT_ref[0].astype(bf16).T
 
 
@@ -210,7 +212,7 @@
                 pl.BlockSpec((1, 1, HEADS, S, QT), lambda b, i, *_: (b, i, 0, 0, 0)),
                 pl.BlockSpec((1, 1, nk, HPAD, QT), lambda b, i, *_: (b, i, 0, 0, 0)),
             ],
-            scratch_shapes=[pltpu.VMEM((D, QT), f32), pltpu.VMEM((HPAD, QT), f32), pltpu.VMEM((HPAD, QT), f32)],
+            scratch_shapes=[pltpu.VMEM((HEADS * HROWS, QT), f32), pltpu.VMEM((HPAD, QT), f32)],
         ),
         out_shape=[
             sds((B, S, D), bf16),
@@ -566,12 +568,12 @@
 
 def qkv_weights_call(core, hid, dq, dk, dv):
     B, S, D = hid.shape
-    row = pl.BlockSpec((1, S, D), lambda b, i: (b, i, 0))
+    row = pl.BlockSpec((1, RT, D), lambda b, i: (b, i, 0))
     anyspec = pl.BlockSpec(memory_space=pl.ANY)
     half = jax.ShapeDtypeStruct((D, 3 * D // 2), bf16)
     return pl.pallas_call(
         qkv_weights_kernel,
-        grid=(B, 1),
+        grid=(B, S // RT),
         in_specs=[pl.BlockSpec(memory_space=pltpu.SMEM), row, row, row, row],
         out_specs=[anyspec, anyspec],
         out_shape=[half, half],

time: 444 us -> 450 us (1.014)
  Pallas kernels: 241 us -> 246 us
  transfers between devices with their start and end apart: 31 -> 31, of which waited for: 17 -> 16; matrix products, arithmetic and copies ran while one was open for 10% -> 10% of each run, Pallas kernels for 55% -> 55%
where the time goes in v5:
time: 450 us; the launch traced here: 445 us
  Pallas kernels  246 us (55%)
  starting transfers between devices  61.1 us (14%)
  waiting for transfers between devices  57.6 us (13%)
  other arithmetic  33.8 us (8%)
  local copies, waits for them, and re-layouts  30.1 us (7%)
  between operations  15 us (3%)
    pallas_call x1, Pallas kernels, mlp_second(): pl.pallas_call(mlp_second_kernel, grid=(B * S // MT2,), in_specs=[smem] +...  55.5 us
    pallas_call x1, Pallas kernels, attn_bwd(): pl.pallas_call(bwd_kernel, grid_spec=pltpu.PrefetchScalarGridSpec(num_sca...  53 us
    pallas_call x1, Pallas kernels, mlp_first(): pl.pallas_call(mlp_first_kernel, grid=(B * S // MT,), in_specs=[smem, row...  51.6 us
    pallas_call x1, Pallas kernels, attn_fwd(): pl.pallas_call(fwd_kernel, grid_spec=pltpu.PrefetchScalarGridSpec(num_sca...  40.5 us
    all_gather x1, waiting for transfers between devices, on_device(): qkv_mine = lax.all_gather(qkv_local, 'shard', axis=0, tiled=True)  20.1 us
    pallas_call x1, Pallas kernels, qkv_back_call(): pl.pallas_call(qkv_back_kernel, grid=(B, S // RT), in_specs=[pl.BlockSpec...  17 us
    all_to_all x1, starting transfers between devices, on_device(): lax.all_to_all(qkv_half, 'shard', 0, 0, tiled=True).reshape(n, own, 3 * hd)  16.4 us
    pallas_call x1, Pallas kernels, qkv_call(): pl.pallas_call(qkv_kernel, grid=(B, S // RT), in_specs=[pl.BlockSpec(memo...  15.3 us
  transfers between devices with their start and end apart: 31, of which 16 were waited for; matrix products, arithmetic and copies ran while one was open for 10% of the time, Pallas kernels for 55%

profile of v5, /device:TPU:0, one launch (start us, length us, event | category | flops | bytes accessed | tf_op | source)
XLA Modules:
  0.0 444.6 jit_solution(7731008617570681552)
XLA Ops:
  8.5 6.1 %concatenate.107 = f32[1154]{0:T(1024)S(1)} concatenate(bf16[96]{0:T(256)(128)(2,1)} %param.26, bf16[96]{0:T(256)(128)(2,1)} %param.27, bf16[96]{0:T(256)(128)(2,1)} %param.29, bf16[96]{0:T(256)(128)(2,1)} %param.32, bf16[96]{0:T(256)(128)(2,1)} %param.34, bf16[96]{0:T(256)(128)(2,1)} %param.35, bf16[96]{0:T(256)(128)(2,1)} %param.36, bf16[96]{0:T(256)(128)(2,1)} %param.40, ...), dimensions={0} | concatenate | bytes 6928 | tf_op jit(solution)/shard_map/concatenate | solution.py:773
  14.7 3.0 collective-permute-start
  31.7 2.9 collective-permute-start.3
  42.5 3.0 collective-permute-done.5
  46.1 20.1 %all-gather.4.cloned.1.call-done.mine_ref = bf16[768,1152]{1,0:T(8,128)(2,1)} async-done(((bf16[96,1152]{1,0:T(8,128)(2,1)}), bf16[768,1152]{1,0:T(8,128)(2,1)}) %all-gather.4.cloned.1.call-update) | async-done | bytes 1769488 | tf_op jit(solution)/shard_map/all_gather | solution.py:763
  71.5 15.3 %norm_qkv.1 = (bf16[2,1024,768]{2,1,0:T(8,128)(2,1)}, bf16[2,1024,768]{2,1,0:T(8,128)(2,1)}, bf16[2,1024,768]{2,1,0:T(8,128)(2,1)}, bf16[2,768,1024]{2,1,0:T(8,1...) custom-call(s32[1]{0:T(128)} %bitcast.core_ref, ...), custom_call_target="tpu_custom_call" | custom-call | flops 7247757312 | bytes 30000000 | tf_op jit(solution)/shard_map/norm_qkv/pallas_call | solution.py:102
  88.2 40.5 %attn_fwd.1 = (bf16[2,1024,768]{2,1,0:T(8,128)(2,1)}, f32[2,768,1024]{2,1,0:T(8,128)}, bf16[2,4,12,1024,256]{4,3,2,1,0:T(8,128)(2,1)}, f32[2,4,4,16,256]{4,3,2,1,0:T(8,128)}) custom-call(s32[8]{0:T(128)} %get-tuple-element.311.lo_ref, s32[8]{0:T(128)} %get-tuple-element.310.hi_ref, bf16[2,1024,768]{2,1,0:T(8,128)(2,1)} %get-tuple-element.81.q_ref, ...), custom_call_target="tpu_custom_call" | custom-call | flops 25769803776 | bytes 80000000 | tf_op jit(solution)/shard_map/attn_fwd/pallas_call | solution.py:197
  130.6 51.6 %mlp_first.1 = (bf16[2,1024,768]{2,1,0:T(8,128)(2,1)}, bf16[2,1024,768]{2,1,0:T(8,128)(2,1)}, f32[2,1024,768]{2,1,0:T(8,128)}, bf16[2,1024,768]{2,1,0:T(8,128)(2...) custom-call(s32[1]{0:T(128)} %bitcast.core_ref, bf16[2,1024,768]{2,1,0:T(8,128)(2,1)} %tok_ref.5, ...), custom_call_target="tpu_custom_call" | custom-call | flops 31406948352 | bytes 60000000 | tf_op jit(solution)/shard_map/mlp_first/pallas_call | solution.py:480
  182.2 4.7 %collective-permute-done.7 = bf16[768,1536]{1,0:T(8,128)(2,1)S(1)} collective-permute-done((bf16[768,1536]{1,0:T(8,128)(2,1)}, bf16[768,1536]{1,0:T(8,128)(2,1)S(1)}, u32[]{:S(2)}, u32[]{:S(2)}) %collective-permute-start.7) | collective-permute-done | bytes 2359328 | tf_op jit(solution)/shard_map/ppermute | solution.py:662
  187.0 3.6 add_convert_fusion.1
  190.6 10.2 %all-to-all-start = ((bf16[8,96,1536]{2,1,0:T(8,128)(2,1)}), bf16[8,96,1536]{2,1,0:T(8,128)(2,1)S(1)}, u32[]{:S(2)}, u32[]{:S(2)}) async-start(bf16[8,96,1536]{2,1,0:T(8,128)(2,1)} %bitcast.5), calls=%async_computation | async-start | bytes 4718592 | tf_op jit(solution)/shard_map/all_to_all | solution.py:813
  200.9 55.5 %mlp_second.1 = (bf16[2,1024,768]{2,1,0:T(8,128)(2,1)}, f32[2,1024,768]{2,1,0:T(8,128)}, bf16[2,1024,768]{2,1,0:T(8,128)(2,1)}, bf16[2,768,1024]{2,1,0:T(8,128)(...) custom-call(s32[1]{0:T(128)} %bitcast.core_ref, ...), custom_call_target="tpu_custom_call" | custom-call | flops 33822867456 | bytes 60000000 | tf_op jit(solution)/shard_map/mlp_second/pallas_call | solution.py:508
  262.2 3.4 add_convert_fusion.after_ref
  269.1 6.0 %all-to-all-start.1 = ((bf16[8,104,1920]{2,1,0:T(8,128)(2,1)}), bf16[8,104,1920]{2,1,0:T(8,128)(2,1)S(1)}, u32[]{:S(2)}, u32[]{:S(2)}) async-start(bf16[8,104,1920]{2,1,0:T(8,128)(2,1)} %fusion.1), calls=%async_computation.1 | async-start | bytes 6389760 | tf_op jit(solution)/shard_map/all_to_all | solution.py:714
  276.6 53.0 %attn_bwd.1 = (bf16[2,1024,768]{2,1,0:T(8,128)(2,1)}, bf16[2,1024,768]{2,1,0:T(8,128)(2,1)}, bf16[2,1024,768]{2,1,0:T(8,128)(2,1)}) custom-call(s32[8]{0:T(128)} %get-tuple-element.311.lo_ref, s32[8]{0:T(128)} %get-tuple-element.310.hi_ref, bf16[2,768,1024]{2,1,0:T(8,128)(2,1)} %get-tuple-element.97.qT_ref, bf16[2,768,1024]{2,1,0:T(8,128)(2,1)} %get-tuple-element.98.kT_ref, ...), custom_call_target="tpu_custom_call" | custom-call | flops 51539607552 | bytes 90000000 | tf_op jit(solution)/shard_map/attn_bwd/pallas_call | solution.py:287
  329.7 12.7 %qkv_weights.1 = (bf16[768,1152]{1,0:T(8,128)(2,1)}, bf16[768,1152]{1,0:T(8,128)(2,1)}) custom-call(s32[1]{0:T(128)} %bitcast.core_ref, bf16[2,1024,768]{2,1,0:T(8,128)(2,1)} %get-tuple-element.113.hid_ref, bf16[2,1024,768]{2,1,0:T(8,128)(2,1)} %get-tuple-element.110.dq_ref, bf16[2,1024,768]{2,1,0:T(8,128)(2,1)} %get-tuple-element.111.dk_ref, ...), custom_call_target="tpu_custom_call" | custom-call | flops 7247757312 | bytes 20000000 | tf_op jit(solution)/shard_map/qkv_weights/pallas_call | solution.py:574
  343.3 3.1 collective-permute-done.10
  347.0 3.6 add_convert_fusion.2.after_ref
  352.6 16.4 %all-to-all-start.2 = ((bf16[8,96,1152]{2,1,0:T(8,128)(2,1)}), bf16[8,96,1152]{2,1,0:T(8,128)(2,1)S(1)}, u32[]{:S(2)}, u32[]{:S(2)}) async-start(bf16[8,96,1152]{2,1,0:T(8,128)(2,1)} %bitcast.33), calls=%async_computation.2 | async-start | bytes 3538944 | tf_op jit(solution)/shard_map/all_to_all | solution.py:833
  368.9 17.0 %norm_qkv_back.1 = (bf16[2,1024,768]{2,1,0:T(8,128)(2,1)}, f32[2,1,768]{2,1,0:T(1,128)}, f32[4,768]{1,0:T(4,128)}) custom-call(s32[1]{0:T(128)} %bitcast.core_ref, bf16[2,1024,768]{2,1,0:T(8,128)(2,1)} %tok_ref.5, f32[2,1,768]{2,1,0:T(1,128)} %reshape.351.row_ref, f32[2,1024,768]{2,1,0:T(8,128)} %get-tuple-element.96.gmid_ref, ...), custom_call_target="tpu_custom_call" | custom-call | flops 7247757312 | bytes 40000000 | tf_op jit(solution)/shard_map/norm_qkv_back/pallas_call | solution.py:624
  388.3 3.9 collective-permute-start.16
  400.0 3.0 collective-permute-start.17
  404.5 8.0 %collective-permute-done.15 = f32[1,3,896]{2,1,0:T(4,128)S(1)} collective-permute-done((f32[1,3,896]{2,1,0:T(4,128)S(1)}, f32[1,3,896]{2,1,0:T(4,128)S(1)}, u32[]{:S(2)}, u32[]{:S(2)}) %collective-permute-start.15) | collective-permute-done | bytes 10784 | tf_op jit(solution)/shard_map/ppermute | solution.py:723
  432.2 2.9 collective-permute-done.21
  (240 shorter events, 79.7 us)
Async XLA Ops:
  7.2 59.1 %all-gather.4.cloned.1.call-start = ((), (), s32[]{:S(2)}) async-start(), calls=%async_computation.3 | async-start | bytes 1990656 | tf_op jit(solution)/shard_map/all_gather | solution.py:763
  14.7 8.0 %collective-permute-start = (f32[1,1154]{1,0:T(1,128)S(1)}, f32[1,1154]{1,0:T(1,128)S(1)}, u32[]{:S(2)}, u32[]{:S(2)}) collective-permute-start(f32[1,1154]{1,0:T(1,128)S(1)} %broadcast_in_dim.14), channel_id=1, source_target_pairs={{0,1},{1,0},{2,3},{3,2},{4,5},{5,4},{6,7},{7,6},{8,9},{9,8},{10,11... | collective-permute-start | bytes 13856 | tf_op jit(solution)/shard_map/ppermute | solution.py:679
  19.5 109.2 %all-gather.6.cloned.1.call-start = ((), (), s32[]{:S(2)}) async-start(), calls=%async_computation.4 | async-start | bytes 6266880 | tf_op jit(solution)/shard_map/all_gather | solution.py:790
  26.5 4.9 %collective-permute-start.2 = (f32[4,1154]{1,0:T(4,128)S(1)}, f32[4,1154]{1,0:T(4,128)S(1)}, u32[]{:S(2)}, u32[]{:S(2)}) collective-permute-start(f32[4,1154]{1,0:T(4,128)S(1)} %pad_maximum_fusion.9), channel_id=1, source_target_pairs={{0,4},{1,5},{2,6},{3,7},{4,0},{5,1},{6,2},{7,3},{8,12},{9,13},{10,... | collective-permute-start | bytes 55400 | tf_op jit(solution)/shard_map/ppermute | solution.py:679
  31.7 6.3 %collective-permute-start.3 = (f32[8,768]{1,0:T(8,128)S(1)}, f32[8,768]{1,0:T(8,128)S(1)}, u32[]{:S(2)}, u32[]{:S(2)}) collective-permute-start(f32[8,768]{1,0:T(8,128)S(1)} %slice_select_fusion), channel_id=1, source_target_pairs={{0,4},{1,5},{2,6},{3,7},{4,0},{5,1},{6,2},{7,3},{8,12},{9,13},{10,... | collective-permute-start | bytes 73736 | tf_op jit(solution)/shard_map/ppermute | solution.py:694
  66.3 134.5 %all-gather.8.cloned.1.call-start = ((), (), s32[]{:S(2)}) async-start(), calls=%async_computation.5 | async-start | bytes 5013504 | tf_op jit(solution)/shard_map/all_gather | solution.py:799
  182.1 4.8 %collective-permute-start.7 = (bf16[768,1536]{1,0:T(8,128)(2,1)}, bf16[768,1536]{1,0:T(8,128)(2,1)S(1)}, u32[]{:S(2)}, u32[]{:S(2)}) collective-permute-start(bf16[768,1536]{1,0:T(8,128)(2,1)} %get-tuple-element.89), channel_id=1, source_target_pairs={{0,8},{8,0},{1,9},{9,1},{2,10},{10,2},{3,11},{11,3},{4,12},{12,4},... | collective-permute-start | bytes 7077896 | tf_op jit(solution)/shard_map/ppermute | solution.py:662
  190.6 66.0 %all-to-all-start = ((bf16[8,96,1536]{2,1,0:T(8,128)(2,1)}), bf16[8,96,1536]{2,1,0:T(8,128)(2,1)S(1)}, u32[]{:S(2)}, u32[]{:S(2)}) async-start(bf16[8,96,1536]{2,1,0:T(8,128)(2,1)} %bitcast.5), calls=%async_computation | async-start | bytes 4718592 | tf_op jit(solution)/shard_map/all_to_all | solution.py:813
  256.4 5.8 %collective-permute-start.8 = (bf16[768,1920]{1,0:T(8,128)(2,1)}, bf16[768,1920]{1,0:T(8,128)(2,1)}, u32[]{:S(2)}, u32[]{:S(2)}) collective-permute-start(bf16[768,1920]{1,0:T(8,128)(2,1)} %get-tuple-element.106), channel_id=1, source_target_pairs={{0,8},{8,0},{1,9},{9,1},{2,10},{10,2},{3,11},{11,3},{4,12},{12,4},... | collective-permute-start | bytes 8847368 | tf_op jit(solution)/shard_map/ppermute | solution.py:662
  269.1 81.5 %all-to-all-start.1 = ((bf16[8,104,1920]{2,1,0:T(8,128)(2,1)}), bf16[8,104,1920]{2,1,0:T(8,128)(2,1)S(1)}, u32[]{:S(2)}, u32[]{:S(2)}) async-start(bf16[8,104,1920]{2,1,0:T(8,128)(2,1)} %fusion.1), calls=%async_computation.1 | async-start | bytes 6389760 | tf_op jit(solution)/shard_map/all_to_all | solution.py:714
  275.1 54.5 %collective-permute-start.9 = (bf16[96,1536]{1,0:T(8,128)(2,1)S(1)}, bf16[96,1536]{1,0:T(8,128)(2,1)S(1)}, u32[]{:S(2)}, u32[]{:S(2)}) collective-permute-start(bf16[96,1536]{1,0:T(8,128)(2,1)S(1)} %reduce_sum.86), channel_id=1, source_target_pairs={{0,16},{16,0},{1,17},{17,1},{2,18},{18,2},{3,19},{19,3},{4,20},{20... | collective-permute-start | bytes 884744 | tf_op jit(solution)/shard_map/ppermute | solution.py:669
  342.4 4.5 %collective-permute-start.11 = (bf16[768,1152]{1,0:T(8,128)(2,1)}, bf16[768,1152]{1,0:T(8,128)(2,1)}, u32[]{:S(2)}, u32[]{:S(2)}) collective-permute-start(bf16[768,1152]{1,0:T(8,128)(2,1)} %get-tuple-element.117), channel_id=1, source_target_pairs={{0,8},{8,0},{1,9},{9,1},{2,10},{10,2},{3,11},{11,3},{4,12},{12,4},... | collective-permute-start | bytes 5308424 | tf_op jit(solution)/shard_map/ppermute | solution.py:662
  352.6 62.4 %all-to-all-start.2 = ((bf16[8,96,1152]{2,1,0:T(8,128)(2,1)}), bf16[8,96,1152]{2,1,0:T(8,128)(2,1)S(1)}, u32[]{:S(2)}, u32[]{:S(2)}) async-start(bf16[8,96,1152]{2,1,0:T(8,128)(2,1)} %bitcast.33), calls=%async_computation.2 | async-start | bytes 3538944 | tf_op jit(solution)/shard_map/all_to_all | solution.py:833
  386.0 18.4 %collective-permute-start.23 = (bf16[96,1920]{1,0:T(8,128)(2,1)S(1)}, bf16[96,1920]{1,0:T(8,128)(2,1)S(1)}, u32[]{:S(2)}, u32[]{:S(2)}) collective-permute-start(bf16[96,1920]{1,0:T(8,128)(2,1)S(1)} %copy-done.6), channel_id=1, source_target_pairs={{0,16},{16,0},{1,17},{17,1},{2,18},{18,2},{3,19},{19,3},{4,20},{20... | collective-permute-start | bytes 1105928 | tf_op jit(solution)/shard_map/ppermute | solution.py:669
  388.3 25.0 %collective-permute-start.16 = (f32[1,3,896]{2,1,0:T(4,128)S(1)}, f32[1,3,896]{2,1,0:T(4,128)S(1)}, u32[]{:S(2)}, u32[]{:S(2)}) collective-permute-start(f32[1,3,896]{2,1,0:T(4,128)S(1)} %get-tuple-element.278), channel_id=1, source_target_pairs={{0,5},{1,4},{2,7},{3,6},{4,1},{5,0},{6,3},{7,2},{8,13},{9,12},{10,... | collective-permute-start | bytes 32264 | tf_op jit(solution)/shard_map/ppermute | solution.py:723
  392.3 6.8 %collective-permute-start.12 = (f32[1,3,896]{2,1,0:T(4,128)S(1)}, f32[1,3,896]{2,1,0:T(4,128)S(1)}, u32[]{:S(2)}, u32[]{:S(2)}) collective-permute-start(f32[1,3,896]{2,1,0:T(4,128)S(1)} %get-tuple-element.273), channel_id=1, source_target_pairs={{0,1},{1,0},{2,3},{3,2},{4,5},{5,4},{6,7},{7,6},{8,9},{9,8},{10,11... | collective-permute-start | bytes 32264 | tf_op jit(solution)/shard_map/ppermute | solution.py:723
  392.9 7.1 %collective-permute-start.13 = (f32[1,3,896]{2,1,0:T(4,128)S(1)}, f32[1,3,896]{2,1,0:T(4,128)S(1)}, u32[]{:S(2)}, u32[]{:S(2)}) collective-permute-start(f32[1,3,896]{2,1,0:T(4,128)S(1)} %get-tuple-element.274), channel_id=1, source_target_pairs={{0,2},{1,3},{2,0},{3,1},{4,6},{5,7},{6,4},{7,5},{8,10},{9,11},{10,... | collective-permute-start | bytes 32264 | tf_op jit(solution)/shard_map/ppermute | solution.py:723
  394.3 8.7 %collective-permute-start.14 = (f32[1,3,896]{2,1,0:T(4,128)S(1)}, f32[1,3,896]{2,1,0:T(4,128)S(1)}, u32[]{:S(2)}, u32[]{:S(2)}) collective-permute-start(f32[1,3,896]{2,1,0:T(4,128)S(1)} %get-tuple-element.275), channel_id=1, source_target_pairs={{0,3},{1,2},{2,1},{3,0},{4,7},{5,6},{6,5},{7,4},{8,11},{9,10},{10,... | collective-permute-start | bytes 32264 | tf_op jit(solution)/shard_map/ppermute | solution.py:723
  399.1 13.5 %collective-permute-start.15 = (f32[1,3,896]{2,1,0:T(4,128)S(1)}, f32[1,3,896]{2,1,0:T(4,128)S(1)}, u32[]{:S(2)}, u32[]{:S(2)}) collective-permute-start(f32[1,3,896]{2,1,0:T(4,128)S(1)} %get-tuple-element.276), channel_id=1, source_target_pairs={{0,4},{1,5},{2,6},{3,7},{4,0},{5,1},{6,2},{7,3},{8,12},{9,13},{10,... | collective-permute-start | bytes 32264 | tf_op jit(solution)/shard_map/ppermute | solution.py:723
  400.0 13.3 %collective-permute-start.17 = (f32[1,3,896]{2,1,0:T(4,128)S(1)}, f32[1,3,896]{2,1,0:T(4,128)S(1)}, u32[]{:S(2)}, u32[]{:S(2)}) collective-permute-start(f32[1,3,896]{2,1,0:T(4,128)S(1)} %get-tuple-element.277), channel_id=1, source_target_pairs={{0,6},{1,7},{2,4},{3,5},{4,2},{5,3},{6,0},{7,1},{8,14},{9,15},{10,... | collective-permute-start | bytes 32264 | tf_op jit(solution)/shard_map/ppermute | solution.py:723
  403.0 10.3 %collective-permute-start.18 = (f32[1,3,896]{2,1,0:T(4,128)S(1)}, f32[1,3,896]{2,1,0:T(4,128)S(1)}, u32[]{:S(2)}, u32[]{:S(2)}) collective-permute-start(f32[1,3,896]{2,1,0:T(4,128)S(1)} %get-tuple-element.271), channel_id=1, source_target_pairs={{0,7},{1,6},{2,5},{3,4},{4,3},{5,2},{6,1},{7,0},{8,15},{9,14},{10,... | collective-permute-start | bytes 32264 | tf_op jit(solution)/shard_map/ppermute | solution.py:723
  404.4 9.0 %collective-permute-start.24 = (bf16[96,1920]{1,0:T(8,128)(2,1)S(1)}, bf16[96,1920]{1,0:T(8,128)(2,1)S(1)}, u32[]{:S(2)}, u32[]{:S(2)}) collective-permute-start(bf16[96,1920]{1,0:T(8,128)(2,1)S(1)} %add_convert_fusion.3), channel_id=1, source_target_pairs={{0,8},{8,0},{1,9},{9,1},{2,10},{10,2},{3,11},{11,3},{4,12},{12,4},... | collective-permute-start | bytes 1105928 | tf_op jit(solution)/shard_map/ppermute | solution.py:662
  418.2 11.0 %collective-permute-start.20 = (f32[2,18,896]{2,1,0:T(8,128)}, f32[2,18,896]{2,1,0:T(8,128)}, u32[]{:S(2)}, u32[]{:S(2)}) collective-permute-start(f32[2,18,896]{2,1,0:T(8,128)} %pad_maximum_fusion.6), channel_id=1, source_target_pairs={{0,16},{16,0},{1,17},{17,1},{2,18},{18,2},{3,19},{19,3},{4,20},{20... | collective-permute-start | bytes 387080 | tf_op jit(solution)/shard_map/ppermute | solution.py:679
  427.6 7.5 %collective-permute-start.21 = (bf16[96,1152]{1,0:T(8,128)(2,1)S(1)}, bf16[96,1152]{1,0:T(8,128)(2,1)S(1)}, u32[]{:S(2)}, u32[]{:S(2)}) collective-permute-start(bf16[96,1152]{1,0:T(8,128)(2,1)S(1)} %copy-done.9), channel_id=1, source_target_pairs={{0,16},{16,0},{1,17},{17,1},{2,18},{18,2},{3,19},{19,3},{4,20},{20... | collective-permute-start | bytes 663560 | tf_op jit(solution)/shard_map/ppermute | solution.py:669
  (33 other events, 331.3 us)
Sparse Core Ops, SparseCore 0:
  19.6 46.6 all-gather.3
  69.1 58.7 all-gather.5
  130.8 57.0 all-gather.7
